TPU v7x, 32 devices: a whole 2x2x4 slice. The times are simulated.
32 devices in a mesh: groups: 2 (over x), seq: 16 (over z, y, core).
Axes of the slice: x: 2, y: 2, z: 4, core: 2. Of those that a mesh axis runs over, the one named last changes fastest.
Arguments:
- inputs: bfloat16 [16384, 2560], P(('groups', 'seq')), parts along dimension 0, may hold values from -6 to 6
- raw_steps: float32 [16384, 40], P(('groups', 'seq')), parts along dimension 0, may hold values from -4 to 4
- input_map: bfloat16 [16384, 128], P(('groups', 'seq')), parts along dimension 0, may hold values from -0.875 to 0.875
- output_map: bfloat16 [16384, 128], P(('groups', 'seq')), parts along dimension 0, may hold values from -0.875 to 0.875
- decay_rates: float32 [40], replicated, may hold values from 6.1035156e-05 to 0.03
- skip_gain: float32 [40], replicated, may hold values from 0.5 to 1.5
- starts: int32 [16384], P(('groups', 'seq')), parts along dimension 0, may hold values from 0 to 1, as said below
- cotangent: bfloat16 [16384, 2560], P(('groups', 'seq')), parts along dimension 0, may hold values from -6 to 6
Outputs:
- outputs: bfloat16 [16384, 2560], P(('groups', 'seq')), parts along dimension 0
- grad_inputs: bfloat16 [16384, 2560], P(('groups', 'seq')), parts along dimension 0
- grad_steps: float32 [16384, 40], P(('groups', 'seq')), parts along dimension 0
- grad_input_map: bfloat16 [16384, 128], P(('groups', 'seq')), parts along dimension 0
- grad_output_map: bfloat16 [16384, 128], P(('groups', 'seq')), parts along dimension 0
There are 2 independent parts, one for each index of `groups`. A program takes and returns all parts, laid end to end along the dimension named above; an argument that names none is the same for every part. Nothing has to cross between parts.
Inputs may be any that keep to these rules, and one draw needn't show every extreme that they name: `starts`: exactly 2 entries are 1, at positions drawn from the seed; all others are 0.
All inputs are finite; a program needn't handle non-finite values.
Results may differ from a plain program's by a relative error of at most 0.014.
Values sent between devices are 32-bit elements; how exact they have to be, the bound alone decides.
No kernel may reach another device: no remote copies, remote signals or barrier semaphores. Data moves between devices by JAX's collectives and lax.ppermute only.
A program may use at most 128 MiB of HBM per device.

v0:
```python
import jax
import jax.numpy as jnp
from jax import lax
from jax.sharding import PartitionSpec as P

SPAN = 256


def block_parts(in_block, raw_block, key_block, query_block, start_block, decay_rates, skip_gain):
    block_len = in_block.shape[0]
    head_count = decay_rates.shape[0]
    by_head = in_block.reshape(block_len, head_count, -1)
    step_size = jax.nn.softplus(raw_block)
    cumulative = jnp.cumsum(-step_size * decay_rates[None, :], axis=0)
    start_count = jnp.cumsum(start_block, axis=0, dtype=jnp.int32)
    position = jnp.arange(block_len, dtype=jnp.int32)
    allowed = (start_count[:, None] == start_count[None, :]) & (
        position[:, None] >= position[None, :]
    )
    query_key = jnp.dot(query_block, key_block.T, preferred_element_type=jnp.float32)
    cum_heads = cumulative.T
    log_gap = jnp.where(allowed[None], cum_heads[:, :, None] - cum_heads[:, None, :], 0.0)
    weight = jnp.where(
        allowed[None], jnp.exp(log_gap) * query_key[None] * step_size.T[:, None, :], 0.0
    ).astype(jnp.bfloat16)
    local_out = jnp.einsum("hts,shp->thp", weight, by_head, preferred_element_type=jnp.float32)
    local_out = local_out + skip_gain[None, :, None] * by_head.astype(jnp.float32)
    final_count = start_count[-1]
    tail_scale = jnp.where(
        (start_count == final_count)[:, None],
        jnp.exp(cumulative[-1][None, :] - cumulative) * step_size,
        0.0,
    )
    scaled = (by_head * tail_scale[:, :, None]).astype(jnp.bfloat16)
    block_state = jnp.einsum("shp,sn->hpn", scaled, key_block, preferred_element_type=jnp.float32)
    block_decay = jnp.where(final_count == 0, jnp.exp(cumulative[-1]), 0.0)
    return (local_out.reshape(block_len, -1), block_state, block_decay)


def carried_part(carried, raw_block, query_block, start_block, decay_rates):
    step_size = jax.nn.softplus(raw_block)
    cumulative = jnp.cumsum(-step_size * decay_rates[None, :], axis=0)
    start_count = jnp.cumsum(start_block, axis=0, dtype=jnp.int32)
    lead_scale = jnp.where((start_count == 0)[:, None], jnp.exp(cumulative), 0.0)
    rounded_state = carried.astype(jnp.bfloat16)
    reached = jnp.einsum(
        "tn,hpn->thp", query_block, rounded_state, preferred_element_type=jnp.float32
    )
    return (reached * lead_scale[:, :, None]).reshape(query_block.shape[0], -1)


def carried_grad(carried, raw_block, query_block, start_block, decay_rates, cot_block):
    reached, pullback = jax.vjp(
        lambda state_in: carried_part(state_in, raw_block, query_block, start_block, decay_rates),
        carried,
    )
    return (reached, pullback(cot_block.astype(jnp.float32))[0])


def block_grads(
    in_block,
    raw_block,
    key_block,
    query_block,
    start_block,
    decay_rates,
    skip_gain,
    carried,
    cot_block,
    state_cot,
    decay_cot,
):

    def forward(in_value, raw_in, key_in, query_in):
        local_out, block_state, block_decay = block_parts(
            in_value, raw_in, key_in, query_in, start_block, decay_rates, skip_gain
        )
        return (
            local_out + carried_part(carried, raw_in, query_in, start_block, decay_rates),
            block_state,
            block_decay,
        )

    _, pullback = jax.vjp(forward, in_block, raw_block, key_block, query_block)
    return pullback((cot_block.astype(jnp.float32), state_cot, decay_cot))


def combine_rows(earlier, following):
    return (earlier[0] * following[0], following[0] * earlier[1] + following[1])


def row_decays(device_decay, head_size):
    gathered = lax.all_gather(device_decay[None, :], "seq", axis=0, tiled=True)
    head_count = gathered.shape[1]
    row_count = head_count * head_size // lax.axis_size("seq")
    first_row = lax.axis_index("seq") * row_count
    row_head = (first_row + jnp.arange(row_count, dtype=jnp.int32)) // head_size
    selector = (jnp.arange(head_count, dtype=jnp.int32)[:, None] == row_head[None, :]).astype(
        jnp.float32
    )
    return jnp.dot(gathered, selector, precision=lax.Precision.HIGHEST)


def relay_chain(values, row_decay, reverse):
    head_count, head_size, state_size = values.shape
    flattened = values.reshape(1, head_count * head_size, state_size)
    received = lax.all_to_all(flattened, "seq", split_axis=1, concat_axis=0, tiled=True)
    decay_rows = row_decay[:, :, None]
    prefix_decay, prefix_state = lax.associative_scan(
        combine_rows,
        (jnp.broadcast_to(decay_rows, received.shape), received),
        reverse=reverse,
        axis=0,
    )
    zero_row = jnp.zeros_like(received[:1])
    if reverse:
        shifted = jnp.concatenate([prefix_state[1:], zero_row], axis=0)
    else:
        shifted = jnp.concatenate([zero_row, prefix_state[:-1]], axis=0)
    returned = lax.all_to_all(shifted, "seq", split_axis=0, concat_axis=1, tiled=True)
    return returned.reshape(head_count, head_size, state_size)


def local(inputs, raw_steps, input_map, output_map, decay_rates, skip_gain, starts, cotangent):
    block_total = inputs.shape[0] // SPAN
    head_count = decay_rates.shape[0]
    head_size = inputs.shape[1] // head_count
    state_size = input_map.shape[1]

    def blocks(values):
        return values.reshape((block_total, SPAN) + values.shape[1:])

    in_blocks, raw_blocks, key_blocks, query_blocks, start_blocks, cot_blocks = [
        blocks(v) for v in (inputs, raw_steps, input_map, output_map, starts, cotangent)
    ]
    local_outs, states, decays = lax.map(
        lambda packed: block_parts(
            packed[0], packed[1], packed[2], packed[3], packed[4], decay_rates, skip_gain
        ),
        (in_blocks, raw_blocks, key_blocks, query_blocks, start_blocks),
    )
    unit_decay = jnp.ones((head_count,), jnp.float32)
    zero_state = jnp.zeros((head_count, head_size, state_size), jnp.float32)

    def fold_forward(running, element):
        before_decay, before_state = running
        decay_now, block_state = element
        return (
            (before_decay * decay_now, decay_now[:, None, None] * before_state + block_state),
            (before_decay, before_state),
        )

    (device_decay, device_state), (before_decay, before_state) = lax.scan(
        fold_forward, (unit_decay, zero_state), (decays, states)
    )
    row_decay = row_decays(device_decay, head_size)
    entering = relay_chain(device_state, row_decay, False)
    carried_all = before_decay[:, :, None, None] * entering[None] + before_state

    def output_block(packed):
        local_out, carried, raw_block, query_block, start_block, cot_block = packed
        reached, direct = carried_grad(
            carried, raw_block, query_block, start_block, decay_rates, cot_block
        )
        return ((local_out + reached).astype(jnp.bfloat16), direct)

    produced, directs = lax.map(
        output_block, (local_outs, carried_all, raw_blocks, query_blocks, start_blocks, cot_blocks)
    )

    def fold_backward(running, element):
        after_decay, after_state = running
        decay_now, direct = element
        return (
            (decay_now * after_decay, direct + decay_now[:, None, None] * after_state),
            (after_decay, after_state),
        )

    (_, device_grad), (after_decay, after_state) = lax.scan(
        fold_backward, (unit_decay, zero_state), (decays, directs), reverse=True
    )
    leaving = relay_chain(device_grad, row_decay, True)
    state_grads = after_decay[:, :, None, None] * leaving[None] + after_state
    decay_grads = jnp.sum(state_grads * carried_all, axis=(2, 3))

    def grad_block(packed):
        return block_grads(
            packed[0],
            packed[1],
            packed[2],
            packed[3],
            packed[4],
            decay_rates,
            skip_gain,
            packed[5],
            packed[6],
            packed[7],
            packed[8],
        )

    grad_in, grad_raw, grad_key, grad_query = lax.map(
        grad_block,
        (
            in_blocks,
            raw_blocks,
            key_blocks,
            query_blocks,
            start_blocks,
            carried_all,
            cot_blocks,
            state_grads,
            decay_grads,
        ),
    )
    return (
        produced.reshape(inputs.shape),
        grad_in.reshape(inputs.shape),
        grad_raw.reshape(raw_steps.shape),
        grad_key.reshape(input_map.shape),
        grad_query.reshape(output_map.shape),
    )


def solution(mesh):
    return jax.shard_map(
        local,
        mesh=mesh,
        in_specs=(
            P(("groups", "seq"), None),
            P(("groups", "seq"), None),
            P(("groups", "seq"), None),
            P(("groups", "seq"), None),
            P(),
            P(),
            P(("groups", "seq")),
            P(("groups", "seq"), None),
        ),
        out_specs=(
            P(("groups", "seq"), None),
            P(("groups", "seq"), None),
            P(("groups", "seq"), None),
            P(("groups", "seq"), None),
            P(("groups", "seq"), None),
        ),
        check_vma=False,
    )
```

profile of v0, /device:TPU:0, one launch (start us, length us, event | category | flops | bytes accessed | tf_op | source)
XLA Modules:
  0.0 357.3 jit_solution(17368974691465040955)
XLA Ops:
  2.2 4.4 %copy.87 = bf16[2,256,2560]{1,2,0:T(8,128)(2,1)} copy(bf16[2,256,2560]{2,1,0:T(8,128)(2,1)} %bitcast.616) | data formatting | bytes 5242880 | tf_op jit(solution)/shard_map/while | solution.py:136
  7.6 23.0 %while.80 = (s32[]{:T(128)}, f32[2,256,2560]{1,2,0:T(8,128)}, f32[2,40,64,128]{3,2,1,0:T(8,128)S(1)}, f32[2,40]{1,0:T(2,128)S(1)}, bf16[2,256,2560]{1,2,0:T(8,12...) while((s32[]{:T(128)}, f32[2,256,2560]{1,2,0:T(8,128)}, ...), condition=%wide.region_5.6_spmd, body=%wide.region_0.5_spmd.sunk | while | flops 541479296 | bytes 53869964 | solution.py:136
  13.3 3.0 bitcast_add_fusion.9
  24.9 3.0 bitcast_add_fusion.9
  32.5 7.7 %while.83 = (s32[]{:T(128)}, f32[40]{0:T(128)S(1)}, f32[40,64,128]{2,1,0:T(8,128)}, f32[2,40]{1,0:T(2,128)S(1)}, f32[2,40,64,128]{3,2,1,0:T(8,128)}, /*index=5*/...) while((s32[]{:T(128)}, f32[40]{0:T(128)S(1)}, ...), condition=%wide.region_7.8_spmd.clone, body=%wide.region_6.7_spmd.clone.sunk | while | flops 1310803 | bytes 6555509 | solution.py:153
  35.0 2.5 bitcast_dynamic-update-slice_fusion.4
  37.5 2.6 bitcast_add_fusion.10
  40.2 7.4 %all-to-all-start = ((f32[1,2560,128]{2,0,1:T(1,128)}), f32[1,2560,128]{2,0,1:T(1,128)S(1)}, u32[]{:S(2)}, u32[]{:S(2)}) async-start(f32[1,2560,128]{2,0,1:T(1,128)} %bitcast.66), calls=%async_computation | async-start | bytes 2621440 | tf_op jit(solution)/shard_map/all_to_all | solution.py:107
  49.1 48.0 %all-reduce.20 = f32[640]{0:T(1024)S(1)} all-reduce(f32[640]{0:T(1024)S(1)} %dynamic-update-slice), channel_id=2, replica_groups=mesh['groups'=2,'seq'=16] {'seq'}, use_global_device_ids=true, to_apply=%add.20 | all-reduce | flops 640 | bytes 5120
  101.2 3.7 %pad.130 = f32[16,160,128]{2,1,0:T(8,128)S(1)} pad(f32[8,160,128]{2,1,0:T(8,128)} %add.194, f32[]{:T(128)} %constant.172.clone.1), padding=1_0_1x0_0_0x0_0_0 | pad | bytes 1966084
  107.5 4.6 %all-to-all-start.1 = ((f32[16,160,128]{2,1,0:T(8,128)}), f32[16,160,128]{2,1,0:T(8,128)}, u32[]{:S(2)}, u32[]{:S(2)}) async-start(f32[16,160,128]{2,1,0:T(8,128)} %concatenate.27), calls=%async_computation.1 | async-start | bytes 2621440 | tf_op jit(solution)/shard_map/all_to_all | solution.py:120
  112.2 4.6 %copy.91 = bf16[2,256,2560]{1,2,0:T(8,128)(2,1)} copy(bf16[2,256,2560]{2,1,0:T(8,128)(2,1)} %bitcast.617) | data formatting | bytes 5242880 | tf_op jit(solution)/shard_map/while | solution.py:167
  116.7 22.6 %all-to-all-done.1 = f32[16,160,128]{2,1,0:T(8,128)} async-done(((f32[16,160,128]{2,1,0:T(8,128)}), f32[16,160,128]{2,1,0:T(8,128)}, u32[]{:S(2)}, u32[]{:S(2)}) %all-to-all-start.1) | async-done | bytes 1310752 | tf_op jit(solution)/shard_map/all_to_all | solution.py:120
  139.3 2.8 fusion.148
  146.3 19.3 %while.81 = (s32[]{:T(128)}, bf16[2,256,2560]{2,1,0:T(8,128)(2,1)}, f32[2,40,64,128]{3,2,1,0:T(8,128)}, f32[2,256,2560]{1,2,0:T(8,128)}, bf16[2,256,128]{2,1,0:T...) while((s32[]{:T(128)}, bf16[2,256,2560]{2,1,0:T(8,128)(2,1)}, ...), condition=%wide.region_13.14_spmd, body=%wide.region_8.13_spmd.sunk | while | flops 341240192 | bytes 31272048 | solution.py:167
  166.5 9.5 %while.84 = (s32[]{:T(128)}, f32[40]{0:T(128)S(1)}, f32[40,64,128]{2,1,0:T(8,128)}, f32[2,40]{1,0:T(2,128)}, f32[2,40,64,128]{3,2,1,0:T(8,128)S(1)}, /*index=5*/...) while((s32[]{:T(128)}, f32[40]{0:T(128)S(1)}, ...), condition=%wide.region_15.16_spmd.clone, body=%wide.region_14.15_spmd.clone.sunk | while | flops 1310804 | bytes 6555013 | solution.py:179
  166.6 2.6 bitcast_add_fusion.11
  171.8 3.0 bitcast_add_fusion.11
  175.9 8.2 %all-to-all-start.2 = ((f32[1,2560,128]{2,0,1:T(1,128)}), f32[1,2560,128]{2,0,1:T(1,128)}, u32[]{:S(2)}, u32[]{:S(2)}) async-start(f32[1,2560,128]{2,0,1:T(1,128)} %bitcast.76), calls=%async_computation.2 | async-start | bytes 2621440 | tf_op jit(solution)/shard_map/all_to_all | solution.py:107
  184.7 26.9 %all-to-all-done.2 = f32[1,2560,128]{2,0,1:T(1,128)} async-done(((f32[1,2560,128]{2,0,1:T(1,128)}), f32[1,2560,128]{2,0,1:T(1,128)}, u32[]{:S(2)}, u32[]{:S(2)}) %all-to-all-start.2) | async-done | bytes 1310752 | tf_op jit(solution)/shard_map/all_to_all | solution.py:107
  216.3 3.7 %pad.131 = f32[16,160,128]{2,1,0:T(8,128)S(1)} pad(f32[8,160,128]{2,1,0:T(8,128)} %add.206, f32[]{:T(128)} %constant.172.clone.1), padding=1_0_1x0_0_0x0_0_0 | pad | bytes 1966084
  222.1 3.7 %pad.90 = f32[15,160,128]{2,1,0:T(8,128)S(1)} pad(f32[8,160,128]{2,1,0:T(8,128)} %pad_maximum_fusion.1, f32[]{:T(128)} %constant.172.clone.1), padding=0_0_1x0_0_0x0_0_0 | pad | bytes 1884164 | tf_op jit(solution)/shard_map/slice | solution.py:117
  229.4 2.6 concatenate.31
  232.1 8.1 %all-to-all-start.3 = ((f32[16,160,128]{2,1,0:T(8,128)}), f32[16,160,128]{2,1,0:T(8,128)}, u32[]{:S(2)}, u32[]{:S(2)}) async-start(f32[16,160,128]{2,1,0:T(8,128)} %concatenate.31), calls=%async_computation.3 | async-start | bytes 2621440 | tf_op jit(solution)/shard_map/all_to_all | solution.py:120
  240.2 27.4 %all-to-all-done.3 = f32[16,160,128]{2,1,0:T(8,128)} async-done(((f32[16,160,128]{2,1,0:T(8,128)}), f32[16,160,128]{2,1,0:T(8,128)}, u32[]{:S(2)}, u32[]{:S(2)}) %all-to-all-start.3) | async-done | bytes 1310752 | tf_op jit(solution)/shard_map/all_to_all | solution.py:120
  267.6 4.2 %multiply_reduce_fusion.2 = (f32[2,40]{1,0:T(2,128)S(1)}, bf16[2,40,64,128]{3,2,1,0:T(8,128)(2,1)}) fusion(f32[2,40,64,128]{3,2,1,0:T(8,128)S(1)} %copy-done.2, f32[2,40,64,128]{3,2,1,0:T(8,128)} %copy-done.9, f32[40,64,128]{2,1,0:T(8,128)} %bitcast.79, f32[2,40]{1,0:T(2,128)} %get-tuple-element.396), kind=kLoop, calls=%fused_computation.226 | loop fusion | flops 3276720 | bytes 7864960 | tf_op jit(solution)/shard_map/reduce_sum | solution.py:184
  273.5 82.3 %while.82 = (s32[]{:T(128)}, bf16[2,256,2560]{2,1,0:T(8,128)(2,1)}, f32[2,256,40]{1,0,2:T(2,128)}, bf16[2,256,128]{2,1,0:T(8,128)(2,1)}, bf16[2,256,128]{2,1,0:T...) while((s32[]{:T(128)}, bf16[2,256,2560]{2,1,0:T(8,128)(2,1)}, ...), condition=%wide.region_33.35_spmd, body=%wide.region_17.34_spmd.sunk | while | flops 1469551488 | bytes 47725560 | solution.py:201
  283.5 9.1 %fusion.258 = (f32[40,256]{1,0:T(8,128)}, f32[40,256]{1,0:T(8,128)}, f32[40,256]{1,0:T(8,128)S(1)}, bf16[256,256]{1,0:T(8,128)(2,1)S(1)}) fusion(f32[40,256]{1,0:T(8,128)S(1)} %get-tuple-element.1115, f32[256,256]{1,0:T(8,128)S(1)} %fusion.255, f32[40,256]{1,0:T(8,128)S(1)} %copy-done.12, pred[256,256]{1,0:T(8,128)(4,1)S(1)} %fusion.256, ...), kind=kOutput, calls=%fused_computation.105.clone.1 | convolution fusion | flops 377391104 | bytes 3284992 | tf_op jit(solution)/shard_map/while/body/eval_jaxpr/transpose(jvp(hts,shp->thp))/dot_general | solution.py:26
  301.4 2.5 reduce-window.113
  306.5 5.4 %fusion.257 = bf16[256,40,64]{0,2,1:T(8,128)(2,1)} fusion(bf16[256,40,64]{0,2,1:T(8,128)(2,1)S(1)} %bitcast.605, bf16[256,40,64]{0,2,1:T(8,128)(2,1)S(1)} %get-tuple-element.1114, f32[40]{0:T(128)} %get-tuple-element.1331, f32[256,40]{0,1:T(8,128)S(1)} %multiply_select_fusion.4, bf16[40,64,256]{2,1,0:T(8,128)(2,1)S(1)} %bitcast.604, ...), kind=kOutput, calls=%fused_computation.129.clone.1 | convolution fusion | flops 357171200 | bytes 5693600 | tf_op jit(solution)/shard_map/while/body/eval_jaxpr/transpose(jvp(hts,shp->thp))/dot_general | solution.py:26
  324.7 9.1 %fusion.258 = (f32[40,256]{1,0:T(8,128)}, f32[40,256]{1,0:T(8,128)}, f32[40,256]{1,0:T(8,128)S(1)}, bf16[256,256]{1,0:T(8,128)(2,1)S(1)}) fusion(f32[40,256]{1,0:T(8,128)S(1)} %get-tuple-element.1115, f32[256,256]{1,0:T(8,128)S(1)} %fusion.255, f32[40,256]{1,0:T(8,128)S(1)} %copy-done.12, pred[256,256]{1,0:T(8,128)(4,1)S(1)} %fusion.256, ...), kind=kOutput, calls=%fused_computation.105.clone.1 | convolution fusion | flops 377391104 | bytes 3284992 | tf_op jit(solution)/shard_map/while/body/eval_jaxpr/transpose(jvp(hts,shp->thp))/dot_general | solution.py:26
  347.6 5.4 %fusion.257 = bf16[256,40,64]{0,2,1:T(8,128)(2,1)} fusion(bf16[256,40,64]{0,2,1:T(8,128)(2,1)S(1)} %bitcast.605, bf16[256,40,64]{0,2,1:T(8,128)(2,1)S(1)} %get-tuple-element.1114, f32[40]{0:T(128)} %get-tuple-element.1331, f32[256,40]{0,1:T(8,128)S(1)} %multiply_select_fusion.4, bf16[40,64,256]{2,1,0:T(8,128)(2,1)S(1)} %bitcast.604, ...), kind=kOutput, calls=%fused_computation.129.clone.1 | convolution fusion | flops 357171200 | bytes 5693600 | tf_op jit(solution)/shard_map/while/body/eval_jaxpr/transpose(jvp(hts,shp->thp))/dot_general | solution.py:26
  (380 shorter events, 120.9 us)
Async XLA Ops:
  13.1 3.2 slice-start
  13.3 3.0 slice-start.1
  24.6 3.2 slice-start
  24.9 3.0 slice-start.1
  40.1 8.7 %copy-start.25 = (f32[2,40]{1,0:T(2,128)}, f32[2,40]{1,0:T(2,128)S(1)}, u32[]{:S(2)}) copy-start(f32[2,40]{1,0:T(2,128)S(1)} %get-tuple-element.390) | copy-start | bytes 964
  40.1 58.3 %copy-start.21 = (f32[2,40]{1,0:T(2,128)}, f32[2,40]{1,0:T(2,128)S(1)}, u32[]{:S(2)}) copy-start(f32[2,40]{1,0:T(2,128)S(1)} %get-tuple-element.1352) | copy-start | bytes 964
  40.2 7.4 %copy-start.32 = (u32[32]{0:T(128)S(1)}, u32[32]{0:T(128)}, u32[]{:S(2)}) copy-start(u32[32]{0:T(128)} %constant.222) | copy-start | bytes 388
  40.2 57.4 %all-to-all-start = ((f32[1,2560,128]{2,0,1:T(1,128)}), f32[1,2560,128]{2,0,1:T(1,128)S(1)}, u32[]{:S(2)}, u32[]{:S(2)}) async-start(f32[1,2560,128]{2,0,1:T(1,128)} %bitcast.66), calls=%async_computation | async-start | bytes 2621440 | tf_op jit(solution)/shard_map/all_to_all | solution.py:107
  107.5 31.8 %all-to-all-start.1 = ((f32[16,160,128]{2,1,0:T(8,128)}), f32[16,160,128]{2,1,0:T(8,128)}, u32[]{:S(2)}, u32[]{:S(2)}) async-start(f32[16,160,128]{2,1,0:T(8,128)} %concatenate.27), calls=%async_computation.1 | async-start | bytes 2621440 | tf_op jit(solution)/shard_map/all_to_all | solution.py:120
  112.1 27.2 %copy-start.8 = (f32[2,40,64,128]{3,2,1,0:T(8,128)S(1)}, f32[2,40,64,128]{3,2,1,0:T(8,128)}, u32[]{:S(2)}) copy-start(f32[2,40,64,128]{3,2,1,0:T(8,128)} %get-tuple-element.393) | copy-start | bytes 7864324
  112.1 27.2 %copy-start.26 = (f32[2,40]{1,0:T(2,128)S(1)}, f32[2,40]{1,0:T(2,128)}, u32[]{:S(2)}) copy-start(f32[2,40]{1,0:T(2,128)} %copy-done.25) | copy-start | bytes 964
  152.7 3.2 copy-start.7
  162.4 3.3 copy-start.7
  175.9 37.0 %copy-start.9 = (f32[2,40,64,128]{3,2,1,0:T(8,128)}, f32[2,40,64,128]{3,2,1,0:T(8,128)S(1)}, u32[]{:S(2)}) copy-start(f32[2,40,64,128]{3,2,1,0:T(8,128)S(1)} %get-tuple-element.398) | copy-start | bytes 7864324
  175.9 8.2 %copy-start.16 = (f32[16,160]{1,0:T(8,128)S(1)}, f32[16,160]{1,0:T(8,128)}, u32[]{:S(2)}) copy-start(f32[16,160]{1,0:T(8,128)} %copy-done.15) | copy-start | bytes 30724
  175.9 37.3 %copy-start.19 = (f32[8,160]{1,0:T(8,128)S(1)}, f32[8,160]{1,0:T(8,128)}, u32[]{:S(2)}) copy-start(f32[8,160]{1,0:T(8,128)} %copy-done.18) | copy-start | bytes 15364
  175.9 35.7 %all-to-all-start.2 = ((f32[1,2560,128]{2,0,1:T(1,128)}), f32[1,2560,128]{2,0,1:T(1,128)}, u32[]{:S(2)}, u32[]{:S(2)}) async-start(f32[1,2560,128]{2,0,1:T(1,128)} %bitcast.76), calls=%async_computation.2 | async-start | bytes 2621440 | tf_op jit(solution)/shard_map/all_to_all | solution.py:107
  215.3 4.8 %copy-start.20 = (f32[7,160]{1,0:T(8,128)S(1)}, f32[7,160]{1,0:T(8,128)}, u32[]{:S(2)}) copy-start(f32[7,160]{1,0:T(8,128)} %slice.316) | copy-start | bytes 13444
  229.4 38.2 %copy-start.2 = (f32[2,40,64,128]{3,2,1,0:T(8,128)S(1)}, f32[2,40,64,128]{3,2,1,0:T(8,128)}, u32[]{:S(2)}) copy-start(f32[2,40,64,128]{3,2,1,0:T(8,128)} %copy-done.1) | copy-start | bytes 7864324
  232.1 35.5 %all-to-all-start.3 = ((f32[16,160,128]{2,1,0:T(8,128)}), f32[16,160,128]{2,1,0:T(8,128)}, u32[]{:S(2)}, u32[]{:S(2)}) async-start(f32[16,160,128]{2,1,0:T(8,128)} %concatenate.31), calls=%async_computation.3 | async-start | bytes 2621440 | tf_op jit(solution)/shard_map/all_to_all | solution.py:120
  273.5 7.8 %copy-start.23 = (f32[2,40]{1,0:T(2,128)}, f32[2,40]{1,0:T(2,128)S(1)}, u32[]{:S(2)}) copy-start(f32[2,40]{1,0:T(2,128)S(1)} %get-tuple-element.1336) | copy-start | bytes 964 | tf_op jit(solution)/shard_map/while
  275.7 5.6 %copy-start.17 = (pred[256]{0:T(512)(128)(4,1)}, pred[256]{0:T(512)(128)(4,1)S(1)}, u32[]{:S(2)}) copy-start(pred[256]{0:T(512)(128)(4,1)S(1)} %get-tuple-element.1111) | copy-start | bytes 772 | tf_op jit(solution)/shard_map/while
  281.5 11.1 %copy-start.13 = (f32[40,256]{1,0:T(8,128)}, f32[40,256]{1,0:T(8,128)S(1)}, u32[]{:S(2)}) copy-start(f32[40,256]{1,0:T(8,128)S(1)} %get-tuple-element.1115) | copy-start | bytes 122884 | tf_op jit(solution)/shard_map/while
  283.3 9.4 %copy-start.10 = (pred[256,256]{1,0:T(8,128)(4,1)}, pred[256,256]{1,0:T(8,128)(4,1)S(1)}, u32[]{:S(2)}) copy-start(pred[256,256]{1,0:T(8,128)(4,1)S(1)} %fusion.256) | copy-start | bytes 196612 | tf_op jit(solution)/shard_map/while
  283.5 9.1 %copy-start.11 = (bf16[2,40,64,128]{3,2,1,0:T(8,128)(2,1)S(1)}, bf16[2,40,64,128]{3,2,1,0:T(8,128)(2,1)}, u32[]{:S(2)}) copy-start(bf16[2,40,64,128]{3,2,1,0:T(8,128)(2,1)} %get-tuple-element.1334) | copy-start | bytes 3932164 | tf_op jit(solution)/shard_map/while
  283.5 9.7 %copy-start.29 = (bf16[2,256,128]{2,1,0:T(8,128)(2,1)S(1)}, bf16[2,256,128]{2,1,0:T(8,128)(2,1)}, u32[]{:S(2)}) copy-start(bf16[2,256,128]{2,1,0:T(8,128)(2,1)} %get-tuple-element.1306) | copy-start | bytes 393220 | tf_op jit(solution)/shard_map/while
  314.6 7.8 %copy-start.23 = (f32[2,40]{1,0:T(2,128)}, f32[2,40]{1,0:T(2,128)S(1)}, u32[]{:S(2)}) copy-start(f32[2,40]{1,0:T(2,128)S(1)} %get-tuple-element.1336) | copy-start | bytes 964 | tf_op jit(solution)/shard_map/while
  316.8 5.6 %copy-start.17 = (pred[256]{0:T(512)(128)(4,1)}, pred[256]{0:T(512)(128)(4,1)S(1)}, u32[]{:S(2)}) copy-start(pred[256]{0:T(512)(128)(4,1)S(1)} %get-tuple-element.1111) | copy-start | bytes 772 | tf_op jit(solution)/shard_map/while
  322.6 11.1 %copy-start.13 = (f32[40,256]{1,0:T(8,128)}, f32[40,256]{1,0:T(8,128)S(1)}, u32[]{:S(2)}) copy-start(f32[40,256]{1,0:T(8,128)S(1)} %get-tuple-element.1115) | copy-start | bytes 122884 | tf_op jit(solution)/shard_map/while
  324.4 9.4 %copy-start.10 = (pred[256,256]{1,0:T(8,128)(4,1)}, pred[256,256]{1,0:T(8,128)(4,1)S(1)}, u32[]{:S(2)}) copy-start(pred[256,256]{1,0:T(8,128)(4,1)S(1)} %fusion.256) | copy-start | bytes 196612 | tf_op jit(solution)/shard_map/while
  324.6 9.1 %copy-start.11 = (bf16[2,40,64,128]{3,2,1,0:T(8,128)(2,1)S(1)}, bf16[2,40,64,128]{3,2,1,0:T(8,128)(2,1)}, u32[]{:S(2)}) copy-start(bf16[2,40,64,128]{3,2,1,0:T(8,128)(2,1)} %get-tuple-element.1334) | copy-start | bytes 3932164 | tf_op jit(solution)/shard_map/while
  324.7 9.7 %copy-start.29 = (bf16[2,256,128]{2,1,0:T(8,128)(2,1)S(1)}, bf16[2,256,128]{2,1,0:T(8,128)(2,1)}, u32[]{:S(2)}) copy-start(bf16[2,256,128]{2,1,0:T(8,128)(2,1)} %get-tuple-element.1306) | copy-start | bytes 393220 | tf_op jit(solution)/shard_map/while
  (24 other events, 37.4 us)
where the time goes:
time: 362 us; the launch traced here: 357 us
  waiting for transfers between devices  76.9 us (21%)
  other arithmetic  74.4 us (21%)
  local copies, waits for them, and re-layouts  73.8 us (20%)
  matrix products  50.6 us (14%)
  blocking collectives  48 us (13%)
  starting transfers between devices  28.2 us (8%)
    all_to_all x2, waiting for transfers between devices, relay_chain(): lax.all_to_all(shifted, 'seq', split_axis=0, concat_axis=1, tiled=True)  50 us
    unnamed x1, blocking collectives  48 us
    dot_general x6, matrix products, block_parts(): jnp.einsum('hts,shp->thp', weight, by_head, preferred_element_type=jnp.fl...  35.1 us
    all_to_all x2, waiting for transfers between devices, relay_chain(): lax.all_to_all(flattened, 'seq', split_axis=1, concat_axis=0, tiled=True)  26.9 us
    another operation x50, other arithmetic  21.3 us
    all_to_all x2, starting transfers between devices, relay_chain(): lax.all_to_all(flattened, 'seq', split_axis=1, concat_axis=0, tiled=True)  15.6 us
    all_to_all x2, starting transfers between devices, relay_chain(): lax.all_to_all(shifted, 'seq', split_axis=0, concat_axis=1, tiled=True)  12.6 us
    unnamed x42, local copies, waits for them, and re-layouts  11 us
  transfers between devices with their start and end apart: 4, of which 3 were waited for; matrix products, arithmetic and copies ran while one was open for 2% of the time, Pallas kernels for 0%

commit v1 on v0

v1 whole, which is shorter than its diff:
```python
import functools

import jax
import jax.numpy as jnp
from jax import lax
from jax.experimental import pallas as pl
from jax.experimental.pallas import tpu as pltpu
from jax.sharding import PartitionSpec as P

CHUNKS = 2
TILE = 256
VMEM_BYTES = 48 * 1024 * 1024

F32 = jnp.float32
BF16 = jnp.bfloat16


def dot_nn(left, right):
    return lax.dot_general(left, right, (((1,), (0,)), ((), ())), preferred_element_type=F32)


def dot_nt(left, right):
    return lax.dot_general(left, right, (((1,), (1,)), ((), ())), preferred_element_type=F32)


def halves(value):
    high = value.astype(BF16)
    return high, (value - high.astype(F32)).astype(BF16)


def sum_dot(matrix, value):
    first = value.astype(BF16)
    rest = value - first.astype(F32)
    second = rest.astype(BF16)
    third = (rest - second.astype(F32)).astype(BF16)
    return dot_nn(matrix, first) + dot_nn(matrix, second) + dot_nn(matrix, third)


def head_spread(head_count, first_column, columns, head_size):
    row = lax.broadcasted_iota(jnp.int32, (2 * head_count, columns), 0)
    row = jnp.where(row >= head_count, row - head_count, row)
    column = lax.broadcasted_iota(jnp.int32, (2 * head_count, columns), 1) + first_column
    return jnp.where(row == column // head_size, 1.0, 0.0).astype(BF16)


def head_collect(head_count, first_column, columns, head_size):
    row = lax.broadcasted_iota(jnp.int32, (columns, head_count), 0) + first_column
    column = lax.broadcasted_iota(jnp.int32, (columns, head_count), 1)
    return jnp.where(row // head_size == column, 1.0, 0.0).astype(BF16)


def triangle(rows, lower):
    first = lax.broadcasted_iota(jnp.int32, (rows, rows), 0)
    second = lax.broadcasted_iota(jnp.int32, (rows, rows), 1)
    return (first >= second) if lower else (first <= second)


def start_counts(starts_row):
    rows = starts_row.shape[1]
    flags = starts_row.astype(F32)
    column = jnp.sum(jnp.where(triangle(rows, True), flags, 0.0), axis=1, keepdims=True)
    spread = jnp.broadcast_to(flags, (8, rows)).astype(BF16)
    row = dot_nn(spread, triangle(rows, False).astype(F32).astype(BF16))[:1]
    return column, row


def softplus(value):
    return jnp.maximum(value, 0.0) + jnp.log1p(jnp.exp(-jnp.abs(value)))


def prep_kernel(
    head_size, raw_ref, rate_ref, starts_ref, query_ref, key_ref,
    lead_ref, tail_ref, leadt_ref, tailt_ref, grow_ref, fall_ref, decay_ref, last_ref,
):
    rows, head_count = raw_ref.shape
    step = softplus(raw_ref[...])
    lower = triangle(rows, True).astype(F32).astype(BF16)
    cumulative = sum_dot(lower, -step * rate_ref[...])
    count, _ = start_counts(starts_ref[...])
    lead = jnp.where(count == 0.0, query_ref[...].astype(F32), 0.0)
    tail = jnp.where(count == count[rows - 1 :, :], key_ref[...].astype(F32), 0.0)
    lead_ref[...] = lead.astype(BF16)
    tail_ref[...] = tail.astype(BF16)
    leadt_ref[...] = lead.T.astype(BF16)
    tailt_ref[...] = tail.T.astype(BF16)
    fall_ref[...] = jnp.concatenate(halves(jnp.exp(cumulative)), axis=1)
    grow_ref[...] = jnp.concatenate(halves(jnp.exp(-cumulative) * step), axis=1)
    last = jnp.broadcast_to(jnp.exp(cumulative[rows - 1 :, :]), (8, head_count))
    channels = decay_ref.shape[1]
    spread = head_spread(head_count, 0, channels, head_size)
    last_wide = dot_nn(jnp.concatenate(halves(last), axis=1), spread)[:1]
    last_ref[...] = last_wide
    decay_ref[...] = jnp.where(count[rows - 1 :, :] == 0.0, last_wide, 0.0)


def states_kernel(
    head_count, head_size, first, place_ref, in_ref, cot_ref, grow_ref, fall_ref, leadt_ref,
    tailt_ref, last_ref, send_ref, keep_ref,
):
    columns = in_ref.shape[1]
    spread = head_spread(head_count, first + pl.program_id(0) * columns, columns, head_size)
    grown = (dot_nn(grow_ref[...], spread) * in_ref[...].astype(F32)).astype(BF16)
    fallen = (dot_nn(fall_ref[...], spread) * cot_ref[...].astype(F32)).astype(BF16)
    state = dot_nn(tailt_ref[...], grown) * last_ref[...]
    direct = dot_nn(leadt_ref[...], fallen)
    low, mid = place_ref[0] == 0, place_ref[1] == 0
    half = state.shape[0] // 2
    quarter = half // 2
    for chain, value in enumerate((state, direct)):
        sent = jnp.where(low, value[half:], value[:half])
        kept = jnp.where(low, value[:half], value[half:])
        for ref, part in ((send_ref, sent), (keep_ref, kept)):
            ref[chain, 0] = jnp.where(mid, part[quarter:], part[:quarter])
            ref[chain, 1] = jnp.where(mid, part[:quarter], part[quarter:])


def scores_kernel(
    head_count, head_size, steps, starts_ref, query_ref, key_ref, in_ref, cot_ref, grow_ref,
    fall_ref, score_ref, scoret_ref, dquery_ref, dkey_ref, total_ref,
):
    columns = in_ref.shape[1]
    rows = in_ref.shape[0]
    step = pl.program_id(0)
    spread = head_spread(head_count, step * columns, columns, head_size)
    grown = (dot_nn(grow_ref[...], spread) * in_ref[...].astype(F32)).astype(BF16)
    fallen = (dot_nn(fall_ref[...], spread) * cot_ref[...].astype(F32)).astype(BF16)
    product = dot_nt(fallen, grown)

    @pl.when(step == 0)
    def _():
        total_ref[...] = product

    @pl.when(step > 0)
    def _():
        total_ref[...] += product

    @pl.when(step == steps - 1)
    def _():
        column, row = start_counts(starts_ref[...])
        same = column == row
        allowed = same & triangle(rows, True)
        score_ref[...] = jnp.where(allowed, dot_nt(query_ref[...], key_ref[...]), 0.0).astype(BF16)
        scoret_ref[...] = jnp.where(
            same & triangle(rows, False), dot_nt(key_ref[...], query_ref[...]), 0.0
        ).astype(BF16)
        grads = jnp.where(allowed, total_ref[...], 0.0)
        dquery_ref[...] = dot_nn(grads.astype(BF16), key_ref[...])
        dkey_ref[...] = dot_nn(grads.T.astype(BF16), query_ref[...])


def arranged(low, mid, took_ref, own_ref, chain):
    parts = []
    for ref in (own_ref, took_ref):
        first = jnp.where(mid, ref[chain, 1], ref[chain, 0])
        second = jnp.where(mid, ref[chain, 0], ref[chain, 1])
        parts.append(jnp.concatenate([first, second], axis=0))
    own, took = parts
    return jnp.concatenate([jnp.where(low, own, took), jnp.where(low, took, own)], axis=0)


def finish_kernel(
    head_count, head_size, first, steps, place_ref, in_ref, cot_ref, took_ref, own_ref, skip_ref,
    decay_ref, last_ref, grow_ref, fall_ref, lead_ref, tail_ref, score_ref, scoret_ref, starts_ref,
    raw_ref, rate_ref, dquery_in, dkey_in,
    out_ref, din_ref, dquery_ref, dkey_ref, draw_ref,
    rise_ref, sink_ref, edge_ref, dlead_ref, dtail_ref,
):
    rows, columns = in_ref.shape
    step = pl.program_id(0)
    start_column = first + step * columns
    low, mid = place_ref[0] == 0, place_ref[1] == 0
    entering = arranged(low, mid, took_ref, own_ref, 0)
    leaving = arranged(low, mid, took_ref, own_ref, 1)
    spread = head_spread(head_count, start_column, columns, head_size)
    grow = dot_nn(grow_ref[...], spread)
    fall = dot_nn(fall_ref[...], spread)
    in_wide = in_ref[...].astype(F32)
    cot_wide = cot_ref[...].astype(F32)
    grown = (grow * in_wide).astype(BF16)
    fallen = (fall * cot_wide).astype(BF16)
    entering_bf = entering.astype(BF16)
    leaving_bf = (leaving * last_ref[...]).astype(BF16)

    produced = dot_nn(score_ref[...], grown) + dot_nn(lead_ref[...], entering_bf)
    out_ref[...] = (fall * produced + skip_ref[...] * in_wide).astype(BF16)
    behind = dot_nn(tail_ref[...], leaving_bf)
    pulled = dot_nn(scoret_ref[...], fallen) + behind
    din_ref[...] = (grow * pulled + skip_ref[...] * cot_wide).astype(BF16)

    collect = head_collect(head_count, start_column, columns, head_size)

    def by_head(value):
        high, rest = halves(value)
        return dot_nn(high, collect) + dot_nn(rest, collect)

    grown_wide = grown.astype(F32)
    rise = by_head(fallen.astype(F32) * produced)
    sink = by_head(grown_wide * pulled)
    edge_row = jnp.sum(grown_wide * behind, axis=0, keepdims=True) + decay_ref[...] * jnp.sum(
        entering * leaving, axis=0, keepdims=True
    )
    edge = by_head(jnp.broadcast_to(edge_row, (8, columns)))
    dlead = dot_nt(fallen, entering_bf)
    dtail = dot_nt(grown, leaving_bf)

    @pl.when(step == 0)
    def _():
        rise_ref[...] = rise
        sink_ref[...] = sink
        edge_ref[...] = edge
        dlead_ref[...] = dlead
        dtail_ref[...] = dtail

    @pl.when(step > 0)
    def _():
        rise_ref[...] += rise
        sink_ref[...] += sink
        edge_ref[...] += edge
        dlead_ref[...] += dlead
        dtail_ref[...] += dtail

    @pl.when(step == steps - 1)
    def _():
        count, _ = start_counts(starts_ref[...])
        dquery_ref[...] = dquery_in[...] + jnp.where(count == 0.0, dlead_ref[...], 0.0)
        dkey_ref[...] = dkey_in[...] + jnp.where(count == count[rows - 1 :, :], dtail_ref[...], 0.0)
        upper = triangle(rows, False).astype(F32).astype(BF16)
        later = sum_dot(upper, rise_ref[...] - sink_ref[...]) + edge_ref[:1]
        raw = raw_ref[...]
        dstep = sink_ref[...] / softplus(raw) - rate_ref[...] * later
        draw_ref[...] = dstep / (1.0 + jnp.exp(-raw))


def whole(shape):
    return pl.BlockSpec(shape, lambda i, *_: (0,) * len(shape))


def params():
    return pltpu.CompilerParams(vmem_limit_bytes=VMEM_BYTES)


def cost(flops, count):
    return pl.CostEstimate(flops=flops, bytes_accessed=count, transcendentals=0)


def local(inputs, raw_steps, input_map, output_map, decay_rates, skip_gain, starts, cotangent):
    rows, channels = inputs.shape
    head_count = decay_rates.shape[0]
    head_size = channels // head_count
    state_size = input_map.shape[1]
    width = channels // CHUNKS
    tiles = width // TILE
    quarter = state_size // 4

    index = lax.axis_index("seq")
    size = lax.axis_size("seq")
    planes = size // 4
    core, side, plane = index % 2, (index // 2) % 2, index // 4
    place = jnp.stack([core, side]).astype(jnp.int32)
    first_core = core == 0
    first_side = side == 0
    starts_row = starts.reshape(1, rows)
    rate_row = decay_rates.reshape(1, head_count)
    skip_row = jnp.repeat(skip_gain, head_size).reshape(1, channels)

    def shape(dims, kind=F32):
        return jax.ShapeDtypeStruct(dims, kind)

    lead, tail, leadt, tailt, grow, fall, decay, last = pl.pallas_call(
        functools.partial(prep_kernel, head_size),
        out_shape=(
            shape((rows, state_size), BF16),
            shape((rows, state_size), BF16),
            shape((state_size, rows), BF16),
            shape((state_size, rows), BF16),
            shape((rows, 2 * head_count), BF16),
            shape((rows, 2 * head_count), BF16),
            shape((1, channels)),
            shape((1, channels)),
        ),
        compiler_params=params(),
        name="prep",
    )(raw_steps, rate_row, starts_row, output_map, input_map)

    def pieces(chunk):
        first = chunk * tiles
        tile = pl.BlockSpec((rows, TILE), lambda i, *_: (0, first + i))
        row = pl.BlockSpec((1, TILE), lambda i, *_: (0, first + i))
        part = pl.BlockSpec((2, 2, quarter, TILE), lambda i, *_: (0, 0, 0, i))
        return tile, row, part

    def device_states(chunk):
        tile, row, part = pieces(chunk)
        half = shape((2, 2, quarter, width))
        return pl.pallas_call(
            functools.partial(states_kernel, head_count, head_size, chunk * width),
            out_shape=(half, half),
            grid_spec=pltpu.PrefetchScalarGridSpec(
                num_scalar_prefetch=1,
                grid=(tiles,),
                in_specs=[
                    tile, tile, whole(grow.shape), whole(fall.shape), whole(leadt.shape),
                    whole(tailt.shape), row,
                ],
                out_specs=(part, part),
            ),
            compiler_params=params(),
            cost_estimate=cost(
                4 * rows * state_size * width + 8 * rows * head_count * width, 6 * rows * width
            ),
            name="states",
        )(place, inputs, cotangent, grow, fall, leadt, tailt, last)

    def swap(value, bit):
        return lax.ppermute(value, "seq", [(i, i ^ bit) for i in range(size)])

    decay_other = swap(decay, 1)
    decay_first = jnp.where(first_core, decay, decay_other)
    decay_second = jnp.where(first_core, decay_other, decay)
    chip_decay = decay * decay_other
    chip_other = swap(chip_decay, 2)
    side_first = jnp.where(first_side, chip_decay, chip_other)
    side_second = jnp.where(first_side, chip_other, chip_decay)
    plane_decay = chip_decay * chip_other

    levels = planes.bit_length() - 1
    before, after, group = [None], [None], plane_decay
    for level in range(levels - 1):
        other = swap(group, 4 << level)
        upper = (plane >> level) % 2 == 1
        ones = jnp.ones_like(group)
        before_now = jnp.where(upper, other, ones)
        after_now = jnp.where(upper, ones, other)
        if level:
            before_now, after_now = before[-1] * before_now, after[-1] * after_now
        before.append(before_now)
        after.append(after_now)
        group = group * other

    def level_perms(level):
        span = 1 << level
        perms = []
        for shift in range(span):
            pairs = []
            for base in range(0, planes, 2 * span):
                pairs.append((base + span - 1, base + span + shift))
                pairs.append((base + span, base + span - 1 - shift))
            perms.append([(4 * a + r, 4 * b + r) for a, b in pairs for r in range(4)])
        return perms

    def chain(chunk, sent, kept):
        cols = slice(chunk * width, (chunk + 1) * width)
        came = swap(sent, 1)
        d_first, d_second = decay_first[:, cols], decay_second[:, cols]
        s_first = jnp.where(first_core, kept[0], came[0])
        s_second = jnp.where(first_core, came[0], kept[0])
        g_first = jnp.where(first_core, kept[1], came[1])
        g_second = jnp.where(first_core, came[1], kept[1])
        chip = jnp.stack([d_second * s_first + s_second, g_first + d_first * g_second])
        side_sent, side_kept = chip[:, 0], chip[:, 1]
        side_came = swap(side_sent, 2)
        e_first, e_second = side_first[:, cols], side_second[:, cols]
        t_first = jnp.where(first_side, side_kept[0], side_came[0])
        t_second = jnp.where(first_side, side_came[0], side_kept[0])
        h_first = jnp.where(first_side, side_kept[1], side_came[1])
        h_second = jnp.where(first_side, side_came[1], side_kept[1])
        plane_state = e_second * t_first + t_second
        plane_direct = h_first + e_first * h_second
        p_decay = plane_decay[:, cols]
        entering = leaving = None
        for level in range(levels):
            upper = (plane >> level) % 2 == 1
            if level:
                payload = jnp.where(
                    upper, p_decay * leaving + plane_direct, p_decay * entering + plane_state
                )
            else:
                payload = jnp.where(upper, plane_direct, plane_state)
            taken = None
            for perm in level_perms(level):
                moved = lax.ppermute(payload, "seq", perm)
                taken = moved if taken is None else taken + moved
            if level:
                entering = entering + jnp.where(upper, before[level][:, cols] * taken, 0.0)
                leaving = leaving + jnp.where(upper, 0.0, after[level][:, cols] * taken)
            else:
                entering = jnp.where(upper, taken, 0.0)
                leaving = jnp.where(upper, 0.0, taken)
        through = e_first * entering + t_first
        through_back = e_second * leaving + h_second
        mine = jnp.stack(
            [
                jnp.where(first_side, entering, through),
                jnp.where(first_side, through_back, leaving),
            ]
        )
        theirs = jnp.stack(
            [
                jnp.where(first_side, through, entering),
                jnp.where(first_side, leaving, through_back),
            ]
        )
        chip_in = jnp.stack([swap(theirs, 2), mine], axis=1)
        inner = d_first * chip_in[0] + s_first
        inner_back = d_second * chip_in[1] + g_second
        own = jnp.stack(
            [
                jnp.where(first_core, chip_in[0], inner),
                jnp.where(first_core, inner_back, chip_in[1]),
            ]
        )
        give = jnp.stack(
            [
                jnp.where(first_core, inner, chip_in[0]),
                jnp.where(first_core, chip_in[1], inner_back),
            ]
        )
        return swap(give, 1), own

    score_tiles = channels // TILE
    all_tile = pl.BlockSpec((rows, TILE), lambda i, *_: (0, i))

    def scores():
        square = (rows, rows)
        return pl.pallas_call(
            functools.partial(scores_kernel, head_count, head_size, score_tiles),
            out_shape=(
                shape(square, BF16), shape(square, BF16),
                shape((rows, state_size)), shape((rows, state_size)),
            ),
            grid_spec=pltpu.PrefetchScalarGridSpec(
                num_scalar_prefetch=0,
                grid=(score_tiles,),
                in_specs=[
                    whole(starts_row.shape), whole(output_map.shape), whole(input_map.shape),
                    all_tile, all_tile, whole(grow.shape), whole(fall.shape),
                ],
                out_specs=(
                    whole(square), whole(square),
                    whole((rows, state_size)), whole((rows, state_size)),
                ),
                scratch_shapes=[pltpu.VMEM(square, F32)],
            ),
            compiler_params=params(),
            cost_estimate=cost(2 * rows * rows * channels, 4 * rows * channels),
            name="scores",
        )(starts_row, output_map, input_map, inputs, cotangent, grow, fall)

    def finish(chunk, took, own, out, din, dquery, dkey):
        tile, row, part = pieces(chunk)
        square = (rows, rows)
        flat = (rows, state_size)
        per_head = (rows, head_count)
        operands = (
            place, inputs, cotangent, took, own, skip_row, decay, last, grow, fall, lead, tail,
            score, scoret, starts_row, raw_steps, rate_row, dquery, dkey,
        )
        return pl.pallas_call(
            functools.partial(finish_kernel, head_count, head_size, chunk * width, tiles),
            out_shape=(
                shape((rows, width), BF16), shape((rows, width), BF16),
                shape(flat), shape(flat), shape(per_head),
            ),
            grid_spec=pltpu.PrefetchScalarGridSpec(
                num_scalar_prefetch=1,
                grid=(tiles,),
                in_specs=[
                    tile, tile, part, part, row, row, row, whole(grow.shape), whole(fall.shape),
                    whole(flat), whole(flat), whole(square), whole(square),
                    whole(starts_row.shape), whole(per_head), whole(rate_row.shape),
                    whole(flat), whole(flat),
                ],
                out_specs=(
                    pl.BlockSpec((rows, TILE), lambda i, *_: (0, i)),
                    pl.BlockSpec((rows, TILE), lambda i, *_: (0, i)),
                    whole(flat), whole(flat), whole(per_head),
                ),
                scratch_shapes=[
                    pltpu.VMEM(per_head, F32), pltpu.VMEM(per_head, F32),
                    pltpu.VMEM((8, head_count), F32),
                    pltpu.VMEM(flat, F32), pltpu.VMEM(flat, F32),
                ],
            ),
            compiler_params=params(),
            cost_estimate=cost(4 * rows * rows * width, 12 * rows * width),
            name="finish",
        )(*operands)

    states = [device_states(chunk) for chunk in range(CHUNKS)]
    score, scoret, dquery, dkey = scores()
    outs, dins, draw = [], [], None
    for chunk in range(CHUNKS):
        took, own = chain(chunk, *states[chunk])
        out, din, dquery, dkey, draw_now = finish(chunk, took, own, None, None, dquery, dkey)
        outs.append(out)
        dins.append(din)
        draw = draw_now if draw is None else draw + draw_now
    return (
        jnp.concatenate(outs, axis=1),
        jnp.concatenate(dins, axis=1),
        draw,
        dkey.astype(BF16),
        dquery.astype(BF16),
    )


def solution(mesh):
    sequence = P(("groups", "seq"), None)
    return jax.shard_map(
        local,
        mesh=mesh,
        in_specs=(
            sequence, sequence, sequence, sequence, P(), P(), P(("groups", "seq")), sequence,
        ),
        out_specs=(sequence,) * 5,
        check_vma=False,
    )
```

time: 362 us -> 125 us (0.35)
  local copies, waits for them, and re-layouts: 73.8 us -> 13.9 us
  other arithmetic: 74.4 us -> 17.7 us
  matrix products: 50.6 us -> 0 us
  waiting for transfers between devices: 76.9 us -> 27.3 us
  blocking collectives: 48 us -> 0 us
  Pallas kernels: 0 us -> 42.1 us
  starting transfers between devices: 28.2 us -> 20.3 us
    all_to_all x4 -> x0, waiting for transfers between devices: 76.9 us -> none  [the longest x2 50 us: relay_chain(): lax.all_to_all(shifted, 'seq', split_axis=0, concat_axis=1, tiled=True)]
    dot_general x29 -> x0, matrix products: 50.6 us -> none  [the longest x6 35.1 us: block_parts(): jnp.einsum('hts,shp->thp', weight, by_head, preferred_element_type=jnp.fl...]
    unnamed x1 -> x0, blocking collectives: 48 us -> none
    pallas_call x0 -> x6, Pallas kernels: none -> 42.1 us  [the longest x2 21.4 us: finish(): pl.pallas_call(functools.partial(finish_kernel, head_count, head_size, ch...]
    all_to_all x4 -> x0, starting transfers between devices: 28.2 us -> none  [the longest x2 15.6 us: relay_chain(): lax.all_to_all(flattened, 'seq', split_axis=1, concat_axis=0, tiled=True)]
    ppermute x0 -> x17, waiting for transfers between devices: none -> 27.3 us  [the longest x11 17.8 us: swap(): return lax.ppermute(value, 'seq', [(i, i ^ bit) for i in range(size)])]
    ppermute x0 -> x17, starting transfers between devices: none -> 20.3 us  [the longest x11 12.5 us: swap(): return lax.ppermute(value, 'seq', [(i, i ^ bit) for i in range(size)])]
    another operation x50 -> x13, other arithmetic: 21.3 us -> 3.52 us  [the longest x2 1.79 us: chain(): jnp.stack([jnp.where(first_core, inner, chip_in[0]), jnp.where(first_core...]
  transfers between devices with their start and end apart: 4 -> 17, of which waited for: 3 -> 9; matrix products, arithmetic and copies ran while one was open for 2% -> 10% of each run, Pallas kernels for 0% -> 25%
where the time goes in v1:
time: 125 us; the launch traced here: 122 us
  Pallas kernels  42.1 us (34%)
  waiting for transfers between devices  27.3 us (22%)
  starting transfers between devices  20.3 us (16%)
  other arithmetic  17.7 us (14%)
  local copies, waits for them, and re-layouts  13.9 us (11%)
    pallas_call x2, Pallas kernels, finish(): pl.pallas_call(functools.partial(finish_kernel, head_count, head_size, ch...  21.4 us
    ppermute x11, waiting for transfers between devices, swap(): return lax.ppermute(value, 'seq', [(i, i ^ bit) for i in range(size)])  17.8 us
    unnamed x60, local copies, waits for them, and re-layouts  12.7 us
    ppermute x11, starting transfers between devices, swap(): return lax.ppermute(value, 'seq', [(i, i ^ bit) for i in range(size)])  12.5 us
    pallas_call x2, Pallas kernels, device_states(): pl.pallas_call(functools.partial(states_kernel, head_count, head_size, ch...  10 us
    pallas_call x1, Pallas kernels, scores(): pl.pallas_call(functools.partial(scores_kernel, head_count, head_size, sc...  9.67 us
    ppermute x6, waiting for transfers between devices, chain(): moved = lax.ppermute(payload, 'seq', perm)  9.51 us
    ppermute x6, starting transfers between devices, chain(): moved = lax.ppermute(payload, 'seq', perm)  7.82 us
  transfers between devices with their start and end apart: 17, of which 9 were waited for; matrix products, arithmetic and copies ran while one was open for 10% of the time, Pallas kernels for 25%

profile of v1, /device:TPU:0, one launch (start us, length us, event | category | flops | bytes accessed | tf_op | source)
XLA Modules:
  0.0 122.5 jit_solution(7082727144034689922)
XLA Ops:
  6.5 1.7 %copy-done = bf16[512,2560]{1,0:T(8,128)(2,1)S(1)} copy-done((bf16[512,2560]{1,0:T(8,128)(2,1)S(1)}, bf16[512,2560]{1,0:T(8,128)(2,1)}, u32[]{:S(2)}) %copy-start) | copy-done | bytes 2621464
  8.2 5.0 %states.3 = (f32[2,2,32,1280]{3,2,1,0:T(8,128)S(1)}, f32[2,2,32,1280]{3,2,1,0:T(8,128)S(1)}) custom-call(s32[2]{0:T(128)S(1)} %pad_add_fusion.place_ref, bf16[512,2560]{1,0:T(8,128)(2,1)S(1)} %copy-done, bf16[512,2560]{1,0:T(8,128)(2,1)} %cot_ref.9, bf16[512,80]{1,0:T(8,128)(2,1)S(1)} %get-tuple-element.32.grow_ref, ...), custom_call_target="tpu_custom_call" | custom-call | flops 545259520 | bytes 3932160 | tf_op jit(solution)/shard_map/states/pallas_call | solution.py:295
  13.4 5.0 %states.2 = (f32[2,2,32,1280]{3,2,1,0:T(8,128)S(1)}, f32[2,2,32,1280]{3,2,1,0:T(8,128)S(1)}) custom-call(s32[2]{0:T(128)S(1)} %pad_add_fusion.place_ref, bf16[512,2560]{1,0:T(8,128)(2,1)S(1)} %copy-done, bf16[512,2560]{1,0:T(8,128)(2,1)} %cot_ref.9, bf16[512,80]{1,0:T(8,128)(2,1)S(1)} %get-tuple-element.32.grow_ref, ...), custom_call_target="tpu_custom_call" | custom-call | flops 545259520 | bytes 3932160 | tf_op jit(solution)/shard_map/states/pallas_call | solution.py:295
  19.7 2.6 %collective-permute-start.1 = (f32[1,2560]{1,0:T(1,128)S(1)}, f32[1,2560]{1,0:T(1,128)S(1)}, u32[]{:S(2)}, u32[]{:S(2)}) collective-permute-start(f32[1,2560]{1,0:T(1,128)S(1)} %get-tuple-element.111), channel_id=1, source_target_pairs={{0,2},{1,3},{2,0},{3,1},{4,6},{5,7},{6,4},{7,5},{8,10},{9,11},{10,... | collective-permute-start | bytes 30728 | tf_op jit(solution)/shard_map/ppermute | solution.py:315
  22.4 1.6 %collective-permute-done.1 = f32[1,2560]{1,0:T(1,128)S(1)} collective-permute-done((f32[1,2560]{1,0:T(1,128)S(1)}, f32[1,2560]{1,0:T(1,128)S(1)}, u32[]{:S(2)}, u32[]{:S(2)}) %collective-permute-start.1) | collective-permute-done | bytes 10272 | tf_op jit(solution)/shard_map/ppermute | solution.py:315
  24.0 2.1 %collective-permute-start.5 = (f32[1,2560]{1,0:T(1,128)S(1)}, f32[1,2560]{1,0:T(1,128)S(1)}, u32[]{:S(2)}, u32[]{:S(2)}) collective-permute-start(f32[1,2560]{1,0:T(1,128)S(1)} %get-tuple-element.106), channel_id=1, source_target_pairs={{0,4},{1,5},{2,6},{3,7},{4,0},{5,1},{6,2},{7,3},{8,12},{9,13},{10,... | collective-permute-start | bytes 30728 | tf_op jit(solution)/shard_map/ppermute | solution.py:315
  26.3 1.6 %collective-permute-done.5 = f32[1,2560]{1,0:T(1,128)S(1)} collective-permute-done((f32[1,2560]{1,0:T(1,128)S(1)}, f32[1,2560]{1,0:T(1,128)S(1)}, u32[]{:S(2)}, u32[]{:S(2)}) %collective-permute-start.5) | collective-permute-done | bytes 10272 | tf_op jit(solution)/shard_map/ppermute | solution.py:315
  27.9 1.2 select_add_fusion
  29.1 2.0 %collective-permute-start.11 = (f32[2,32,1280]{2,1,0:T(8,128)S(1)}, f32[2,32,1280]{2,1,0:T(8,128)S(1)}, u32[]{:S(2)}, u32[]{:S(2)}) collective-permute-start(f32[2,32,1280]{2,1,0:T(8,128)S(1)} %fusion.7), channel_id=1, source_target_pairs={{0,2},{1,3},{2,0},{3,1},{4,6},{5,7},{6,4},{7,5},{8,10},{9,11},{10,... | collective-permute-start | bytes 983048 | tf_op jit(solution)/shard_map/ppermute | solution.py:315
  33.4 6.5 %collective-permute-done.11 = f32[2,32,1280]{2,1,0:T(8,128)S(1)} collective-permute-done((f32[2,32,1280]{2,1,0:T(8,128)S(1)}, f32[2,32,1280]{2,1,0:T(8,128)S(1)}, u32[]{:S(2)}, u32[]{:S(2)}) %collective-permute-start.11) | collective-permute-done | bytes 327712 | tf_op jit(solution)/shard_map/ppermute | solution.py:315
  39.9 2.1 %collective-permute-start.12 = (f32[32,1280]{1,0:T(8,128)S(1)}, f32[32,1280]{1,0:T(8,128)S(1)}, u32[]{:S(2)}, u32[]{:S(2)}) collective-permute-start(f32[32,1280]{1,0:T(8,128)S(1)} %broadcast_select_fusion), channel_id=1, source_target_pairs={{0,4},{1,5},{2,6},{3,7},{4,0},{5,1},{6,2},{7,3},{8,12},{9,13},{10,... | collective-permute-start | bytes 491528 | tf_op jit(solution)/shard_map/ppermute | solution.py:381
  42.0 2.3 %collective-permute-done.3 = f32[2,32,1280]{2,1,0:T(8,128)S(1)} collective-permute-done((f32[2,32,1280]{2,1,0:T(8,128)S(1)}, f32[2,32,1280]{2,1,0:T(8,128)S(1)}, u32[]{:S(2)}, u32[]{:S(2)}) %collective-permute-start.3) | collective-permute-done | bytes 327712 | tf_op jit(solution)/shard_map/ppermute | solution.py:315
  44.4 1.8 %collective-permute-start.4 = (f32[32,1280]{1,0:T(8,128)S(1)}, f32[32,1280]{1,0:T(8,128)S(1)}, u32[]{:S(2)}, u32[]{:S(2)}) collective-permute-start(f32[32,1280]{1,0:T(8,128)S(1)} %broadcast_select_fusion.1), channel_id=1, source_target_pairs={{0,4},{1,5},{2,6},{3,7},{4,0},{5,1},{6,2},{7,3},{8,12},{9,13},{10,... | collective-permute-start | bytes 491528 | tf_op jit(solution)/shard_map/ppermute | solution.py:381
  46.3 1.3 %collective-permute-start.14 = (f32[32,1280]{1,0:T(8,128)S(1)}, f32[32,1280]{1,0:T(8,128)S(1)}, u32[]{:S(2)}, u32[]{:S(2)}) collective-permute-start(f32[32,1280]{1,0:T(8,128)S(1)} %add_select_fusion), channel_id=1, source_target_pairs={{4,12},{5,13},{6,14},{7,15},{8,0},{9,1},{10,2},{11,3},{20,28},{21,... | collective-permute-start | bytes 491528 | tf_op jit(solution)/shard_map/ppermute | solution.py:381
  48.3 3.2 %collective-permute-done.4 = f32[32,1280]{1,0:T(8,128)S(1)} collective-permute-done((f32[32,1280]{1,0:T(8,128)S(1)}, f32[32,1280]{1,0:T(8,128)S(1)}, u32[]{:S(2)}, u32[]{:S(2)}) %collective-permute-start.4) | collective-permute-done | bytes 163872 | tf_op jit(solution)/shard_map/ppermute | solution.py:381
  51.6 1.3 %collective-permute-start.7 = (f32[32,1280]{1,0:T(8,128)S(1)}, f32[32,1280]{1,0:T(8,128)S(1)}, u32[]{:S(2)}, u32[]{:S(2)}) collective-permute-start(f32[32,1280]{1,0:T(8,128)S(1)} %add_select_fusion.1), channel_id=1, source_target_pairs={{4,12},{5,13},{6,14},{7,15},{8,0},{9,1},{10,2},{11,3},{20,28},{21,... | collective-permute-start | bytes 491528 | tf_op jit(solution)/shard_map/ppermute | solution.py:381
  53.6 2.6 %collective-permute-done.14 = f32[32,1280]{1,0:T(8,128)S(1)} collective-permute-done((f32[32,1280]{1,0:T(8,128)S(1)}, f32[32,1280]{1,0:T(8,128)S(1)}, u32[]{:S(2)}, u32[]{:S(2)}) %collective-permute-start.14) | collective-permute-done | bytes 163872 | tf_op jit(solution)/shard_map/ppermute | solution.py:381
  56.4 2.5 %collective-permute-start.15 = (f32[2,32,1280]{2,1,0:T(8,128)S(1)}, f32[2,32,1280]{2,1,0:T(8,128)S(1)}, u32[]{:S(2)}, u32[]{:S(2)}) collective-permute-start(f32[2,32,1280]{2,1,0:T(8,128)S(1)} %pad_maximum_fusion.11), channel_id=1, source_target_pairs={{0,2},{1,3},{2,0},{3,1},{4,6},{5,7},{6,4},{7,5},{8,10},{9,11},{10,... | collective-permute-start | bytes 983048 | tf_op jit(solution)/shard_map/ppermute | solution.py:315
  58.8 3.6 %collective-permute-done.7 = f32[32,1280]{1,0:T(8,128)S(1)} collective-permute-done((f32[32,1280]{1,0:T(8,128)S(1)}, f32[32,1280]{1,0:T(8,128)S(1)}, u32[]{:S(2)}, u32[]{:S(2)}) %collective-permute-start.7) | collective-permute-done | bytes 163872 | tf_op jit(solution)/shard_map/ppermute | solution.py:381
  62.6 1.6 %collective-permute-start.8 = (f32[2,32,1280]{2,1,0:T(8,128)S(1)}, f32[2,32,1280]{2,1,0:T(8,128)S(1)}, u32[]{:S(2)}, u32[]{:S(2)}) collective-permute-start(f32[2,32,1280]{2,1,0:T(8,128)S(1)} %pad_maximum_fusion.10), channel_id=1, source_target_pairs={{0,2},{1,3},{2,0},{3,1},{4,6},{5,7},{6,4},{7,5},{8,10},{9,11},{10,... | collective-permute-start | bytes 983048 | tf_op jit(solution)/shard_map/ppermute | solution.py:315
  64.4 5.9 %collective-permute-done.8 = f32[2,32,1280]{2,1,0:T(8,128)S(1)} collective-permute-done((f32[2,32,1280]{2,1,0:T(8,128)S(1)}, f32[2,32,1280]{2,1,0:T(8,128)S(1)}, u32[]{:S(2)}, u32[]{:S(2)}) %collective-permute-start.8) | collective-permute-done | bytes 327712 | tf_op jit(solution)/shard_map/ppermute | solution.py:315
  70.3 1.2 bitcast_select_fusion.5
  72.5 2.2 %fusion.11 = (f32[1,2,32,1280]{3,2,1,0:T(8,128)}, f32[1,2,32,1280]{3,2,1,0:T(8,128)S(1)}, f32[1,2,32,1280]{3,2,1,0:T(8,128)S(1)}, f32[1,2,32,1280]{3,2,1,0:T(8,128)}) fusion(f32[1280]{0:T(1024)S(1)} %get-tuple-element.114, pred[]{:T(512)S(6)} %eq.23, f32[2,1,32,1280]{3,2,0,1:T(8,128)S(1)} %maximum_bitcast_fusion.1, f32[2,1,32,1280]{3,2,0,1:T(8,128)S(1)} %bitcast.243, ...), kind=kLoop, calls=%fused_computation.42 | loop fusion | flops 1228800 | bytes 3287041 | tf_op jit(solution)/shard_map/jit(_where)/select_n | solution.py:408
  75.9 9.7 %scores.1 = (bf16[512,512]{1,0:T(8,128)(2,1)S(1)}, bf16[512,512]{1,0:T(8,128)(2,1)S(1)}, f32[512,128]{1,0:T(8,128)S(1)}, f32[512,128]{1,0:T(8,128)S(1)}) custom-call(s32[1,512]{1,0:T(1,128)S(1)} %bitcast.236, bf16[512,128]{1,0:T(8,128)(2,1)S(1)} %copy-done.12, bf16[512,128]{1,0:T(8,128)(2,1)S(1)} %copy-done.14, bf16[512,2560]{1,0:T(8,128)(2,1)S(1)} %copy-done.1, ...), custom_call_target="tpu_custom_call" | custom-call | flops 1342177280 | bytes 5242880 | tf_op jit(solution)/shard_map/scores/pallas_call | solution.py:425
  88.1 1.2 pad_maximum_fusion.5.own_ref
  90.3 1.1 copy-done.10
  91.4 10.6 %finish.2 = (bf16[512,1280]{1,0:T(8,128)(2,1)S(1)}, bf16[512,1280]{1,0:T(8,128)(2,1)}, f32[512,128]{1,0:T(8,128)S(1)}, f32[512,128]{1,0:T(8,128)S(1)}, f32[512,40]{1,0:T(8,128)S(1)}) custom-call(s32[2]{0:T(128)S(1)} %copy-done.23, bf16[512,2560]{1,0:T(8,128)(2,1)} %in_ref.9, bf16[512,2560]{1,0:T(8,128)(2,1)} %cot_ref.9, f32[2,2,32,1280]{3,2,1,0:T(8,128)S(1)} %copy-done.10, ...), custom_call_target="tpu_custom_call" | custom-call | flops 1342177280 | bytes 7864320 | tf_op jit(solution)/shard_map/finish/pallas_call | solution.py:458
  102.0 10.8 %finish.3 = (bf16[512,1280]{1,0:T(8,128)(2,1)S(1)}, bf16[512,1280]{1,0:T(8,128)(2,1)}, f32[512,128]{1,0:T(8,128)S(1)}, f32[512,128]{1,0:T(8,128)S(1)}, f32[512,40]{1,0:T(8,128)S(1)}) custom-call(s32[2]{0:T(128)S(1)} %copy-done.23, bf16[512,2560]{1,0:T(8,128)(2,1)} %in_ref.9, bf16[512,2560]{1,0:T(8,128)(2,1)} %cot_ref.9, ...), custom_call_target="tpu_custom_call" | custom-call | flops 1342177280 | bytes 7864320 | tf_op jit(solution)/shard_map/finish/pallas_call | solution.py:458
  112.8 1.1 copy-done.8
  115.3 1.6 %convert_element_type.6 = bf16[512,128]{1,0:T(8,128)(2,1)} convert(f32[512,128]{1,0:T(8,128)} %copy-done.17) | non-fusion elementwise | flops 65536 | bytes 393216 | tf_op jit(solution)/shard_map/convert_element_type | solution.py:502
  117.6 3.1 %pad_maximum_fusion = bf16[512,2560]{1,0:T(8,128)(2,1)} fusion(bf16[512,1280]{1,0:T(8,128)(2,1)} %copy-done.8, bf16[512,1280]{1,0:T(8,128)(2,1)S(1)} %get-tuple-element.45), kind=kLoop, calls=%fused_computation | loop fusion | flops 5242880 | bytes 5242880 | tf_op jit(solution)/shard_map/concatenate | solution.py:499
  120.8 1.7 %pad_maximum_fusion.1 = bf16[512,2560]{1,0:T(8,128)(2,1)} fusion(bf16[512,1280]{1,0:T(8,128)(2,1)S(1)} %copy-done.27, bf16[512,1280]{1,0:T(8,128)(2,1)S(1)} %copy-done.26), kind=kLoop, calls=%fused_computation.1 | loop fusion | flops 5242880 | bytes 5242880 | tf_op jit(solution)/shard_map/concatenate | solution.py:500
  (107 shorter events, 19.6 us)
Async XLA Ops:
  5.8 13.9 %copy-start.18 = (f32[1,2560]{1,0:T(1,128)}, f32[1,2560]{1,0:T(1,128)S(1)}, u32[]{:S(2)}) copy-start(f32[1,2560]{1,0:T(1,128)S(1)} %get-tuple-element.31.decay_ref) | copy-start | bytes 30724
  5.9 13.9 %collective-permute-start = (f32[1,2560]{1,0:T(1,128)S(1)}, f32[1,2560]{1,0:T(1,128)S(1)}, u32[]{:S(2)}, u32[]{:S(2)}) collective-permute-start(f32[1,2560]{1,0:T(1,128)S(1)} %get-tuple-element.31.decay_ref), channel_id=1, source_target_pairs={{0,1},{1,0},{2,3},{3,2},{4,5},{5,4},{6,7},{7,6},{8,9},{9,8},{10,11... | collective-permute-start | bytes 30728 | tf_op jit(solution)/shard_map/ppermute | solution.py:315
  6.5 6.9 %copy-start.22 = (s32[2]{0:T(128)}, s32[2]{0:T(128)S(1)}, u32[]{:S(2)}) copy-start(s32[2]{0:T(128)S(1)} %pad_add_fusion.place_ref) | copy-start | bytes 28
  13.2 14.7 %copy-start.2 = (f32[2,2,32,1280]{3,2,1,0:T(8,128)}, f32[2,2,32,1280]{3,2,1,0:T(8,128)S(1)}, u32[]{:S(2)}) copy-start(f32[2,2,32,1280]{3,2,1,0:T(8,128)S(1)} %get-tuple-element.46) | copy-start | bytes 1966084
  13.2 14.7 %collective-permute-start.10 = (f32[2,2,32,1280]{3,2,1,0:T(8,128)S(1)}, f32[2,2,32,1280]{3,2,1,0:T(8,128)}, u32[]{:S(2)}, u32[]{:S(2)}) collective-permute-start(f32[2,2,32,1280]{3,2,1,0:T(8,128)S(1)} %get-tuple-element.47), channel_id=1, source_target_pairs={{0,1},{1,0},{2,3},{3,2},{4,5},{5,4},{6,7},{7,6},{8,9},{9,8},{10,11... | collective-permute-start | bytes 1966088 | tf_op jit(solution)/shard_map/ppermute | solution.py:315
  19.3 11.9 %collective-permute-start.2 = (f32[2,2,32,1280]{3,2,0,1:T(8,128)}, f32[2,2,32,1280]{3,2,0,1:T(8,128)}, u32[]{:S(2)}, u32[]{:S(2)}) collective-permute-start(f32[2,2,32,1280]{3,2,0,1:T(8,128)} %copy.15), channel_id=1, source_target_pairs={{0,1},{1,0},{2,3},{3,2},{4,5},{5,4},{6,7},{7,6},{8,9},{9,8},{10,11... | collective-permute-start | bytes 1966088 | tf_op jit(solution)/shard_map/ppermute | solution.py:315
  19.7 4.3 %collective-permute-start.1 = (f32[1,2560]{1,0:T(1,128)S(1)}, f32[1,2560]{1,0:T(1,128)S(1)}, u32[]{:S(2)}, u32[]{:S(2)}) collective-permute-start(f32[1,2560]{1,0:T(1,128)S(1)} %get-tuple-element.111), channel_id=1, source_target_pairs={{0,2},{1,3},{2,0},{3,1},{4,6},{5,7},{6,4},{7,5},{8,10},{9,11},{10,... | collective-permute-start | bytes 30728 | tf_op jit(solution)/shard_map/ppermute | solution.py:315
  24.0 3.8 %collective-permute-start.5 = (f32[1,2560]{1,0:T(1,128)S(1)}, f32[1,2560]{1,0:T(1,128)S(1)}, u32[]{:S(2)}, u32[]{:S(2)}) collective-permute-start(f32[1,2560]{1,0:T(1,128)S(1)} %get-tuple-element.106), channel_id=1, source_target_pairs={{0,4},{1,5},{2,6},{3,7},{4,0},{5,1},{6,2},{7,3},{8,12},{9,13},{10,... | collective-permute-start | bytes 30728 | tf_op jit(solution)/shard_map/ppermute | solution.py:315
  29.1 10.7 %collective-permute-start.11 = (f32[2,32,1280]{2,1,0:T(8,128)S(1)}, f32[2,32,1280]{2,1,0:T(8,128)S(1)}, u32[]{:S(2)}, u32[]{:S(2)}) collective-permute-start(f32[2,32,1280]{2,1,0:T(8,128)S(1)} %fusion.7), channel_id=1, source_target_pairs={{0,2},{1,3},{2,0},{3,1},{4,6},{5,7},{6,4},{7,5},{8,10},{9,11},{10,... | collective-permute-start | bytes 983048 | tf_op jit(solution)/shard_map/ppermute | solution.py:315
  33.3 11.0 %collective-permute-start.3 = (f32[2,32,1280]{2,1,0:T(8,128)S(1)}, f32[2,32,1280]{2,1,0:T(8,128)S(1)}, u32[]{:S(2)}, u32[]{:S(2)}) collective-permute-start(f32[2,32,1280]{2,1,0:T(8,128)S(1)} %fusion.8), channel_id=1, source_target_pairs={{0,2},{1,3},{2,0},{3,1},{4,6},{5,7},{6,4},{7,5},{8,10},{9,11},{10,... | collective-permute-start | bytes 983048 | tf_op jit(solution)/shard_map/ppermute | solution.py:315
  39.9 6.3 %collective-permute-start.12 = (f32[32,1280]{1,0:T(8,128)S(1)}, f32[32,1280]{1,0:T(8,128)S(1)}, u32[]{:S(2)}, u32[]{:S(2)}) collective-permute-start(f32[32,1280]{1,0:T(8,128)S(1)} %broadcast_select_fusion), channel_id=1, source_target_pairs={{0,4},{1,5},{2,6},{3,7},{4,0},{5,1},{6,2},{7,3},{8,12},{9,13},{10,... | collective-permute-start | bytes 491528 | tf_op jit(solution)/shard_map/ppermute | solution.py:381
  44.4 7.1 %collective-permute-start.4 = (f32[32,1280]{1,0:T(8,128)S(1)}, f32[32,1280]{1,0:T(8,128)S(1)}, u32[]{:S(2)}, u32[]{:S(2)}) collective-permute-start(f32[32,1280]{1,0:T(8,128)S(1)} %broadcast_select_fusion.1), channel_id=1, source_target_pairs={{0,4},{1,5},{2,6},{3,7},{4,0},{5,1},{6,2},{7,3},{8,12},{9,13},{10,... | collective-permute-start | bytes 491528 | tf_op jit(solution)/shard_map/ppermute | solution.py:381
  46.3 9.9 %collective-permute-start.14 = (f32[32,1280]{1,0:T(8,128)S(1)}, f32[32,1280]{1,0:T(8,128)S(1)}, u32[]{:S(2)}, u32[]{:S(2)}) collective-permute-start(f32[32,1280]{1,0:T(8,128)S(1)} %add_select_fusion), channel_id=1, source_target_pairs={{4,12},{5,13},{6,14},{7,15},{8,0},{9,1},{10,2},{11,3},{20,28},{21,... | collective-permute-start | bytes 491528 | tf_op jit(solution)/shard_map/ppermute | solution.py:381
  47.6 8.6 %collective-permute-start.13 = (f32[32,1280]{1,0:T(8,128)S(1)}, f32[32,1280]{1,0:T(8,128)S(1)}, u32[]{:S(2)}, u32[]{:S(2)}) collective-permute-start(f32[32,1280]{1,0:T(8,128)S(1)} %add_select_fusion), channel_id=1, source_target_pairs={{4,8},{5,9},{6,10},{7,11},{8,4},{9,5},{10,6},{11,7},{20,24},{21,25... | collective-permute-start | bytes 491528 | tf_op jit(solution)/shard_map/ppermute | solution.py:381
  51.6 10.8 %collective-permute-start.7 = (f32[32,1280]{1,0:T(8,128)S(1)}, f32[32,1280]{1,0:T(8,128)S(1)}, u32[]{:S(2)}, u32[]{:S(2)}) collective-permute-start(f32[32,1280]{1,0:T(8,128)S(1)} %add_select_fusion.1), channel_id=1, source_target_pairs={{4,12},{5,13},{6,14},{7,15},{8,0},{9,1},{10,2},{11,3},{20,28},{21,... | collective-permute-start | bytes 491528 | tf_op jit(solution)/shard_map/ppermute | solution.py:381
  52.9 9.5 %collective-permute-start.6 = (f32[32,1280]{1,0:T(8,128)S(1)}, f32[32,1280]{1,0:T(8,128)S(1)}, u32[]{:S(2)}, u32[]{:S(2)}) collective-permute-start(f32[32,1280]{1,0:T(8,128)S(1)} %add_select_fusion.1), channel_id=1, source_target_pairs={{4,8},{5,9},{6,10},{7,11},{8,4},{9,5},{10,6},{11,7},{20,24},{21,25... | collective-permute-start | bytes 491528 | tf_op jit(solution)/shard_map/ppermute | solution.py:381
  56.4 16.1 %collective-permute-start.15 = (f32[2,32,1280]{2,1,0:T(8,128)S(1)}, f32[2,32,1280]{2,1,0:T(8,128)S(1)}, u32[]{:S(2)}, u32[]{:S(2)}) collective-permute-start(f32[2,32,1280]{2,1,0:T(8,128)S(1)} %pad_maximum_fusion.11), channel_id=1, source_target_pairs={{0,2},{1,3},{2,0},{3,1},{4,6},{5,7},{6,4},{7,5},{8,10},{9,11},{10,... | collective-permute-start | bytes 983048 | tf_op jit(solution)/shard_map/ppermute | solution.py:315
  62.6 7.7 %collective-permute-start.8 = (f32[2,32,1280]{2,1,0:T(8,128)S(1)}, f32[2,32,1280]{2,1,0:T(8,128)S(1)}, u32[]{:S(2)}, u32[]{:S(2)}) collective-permute-start(f32[2,32,1280]{2,1,0:T(8,128)S(1)} %pad_maximum_fusion.10), channel_id=1, source_target_pairs={{0,2},{1,3},{2,0},{3,1},{4,6},{5,7},{6,4},{7,5},{8,10},{9,11},{10,... | collective-permute-start | bytes 983048 | tf_op jit(solution)/shard_map/ppermute | solution.py:315
  64.3 8.2 %copy-start.3 = (f32[2,2,32,1280]{3,2,1,0:T(8,128)S(1)}, f32[2,2,32,1280]{3,2,1,0:T(8,128)}, u32[]{:S(2)}) copy-start(f32[2,2,32,1280]{3,2,1,0:T(8,128)} %copy-done.2) | copy-start | bytes 1966084
  72.4 3.6 %copy-start.1 = (bf16[512,2560]{1,0:T(8,128)(2,1)S(1)}, bf16[512,2560]{1,0:T(8,128)(2,1)}, u32[]{:S(2)}) copy-start(bf16[512,2560]{1,0:T(8,128)(2,1)} %in_ref.9) | copy-start | bytes 7864324
  72.4 3.6 %copy-start.12 = (bf16[512,128]{1,0:T(8,128)(2,1)S(1)}, bf16[512,128]{1,0:T(8,128)(2,1)}, u32[]{:S(2)}) copy-start(bf16[512,128]{1,0:T(8,128)(2,1)} %query_ref.3) | copy-start | bytes 393220
  72.4 3.6 %copy-start.14 = (bf16[512,128]{1,0:T(8,128)(2,1)S(1)}, bf16[512,128]{1,0:T(8,128)(2,1)}, u32[]{:S(2)}) copy-start(bf16[512,128]{1,0:T(8,128)(2,1)} %key_ref.3) | copy-start | bytes 393220
  72.4 3.6 %copy-start.21 = (s32[512]{0:T(512)S(1)}, s32[512]{0:T(512)}, u32[]{:S(2)}) copy-start(s32[512]{0:T(512)} %param.14) | copy-start | bytes 6148
  72.4 17.0 %collective-permute-start.9 = (f32[2,2,32,1280]{3,2,1,0:T(8,128)}, f32[2,2,32,1280]{3,2,1,0:T(8,128)S(1)}, u32[]{:S(2)}, u32[]{:S(2)}) collective-permute-start(f32[2,2,32,1280]{3,2,1,0:T(8,128)} %pad_maximum_fusion.2), channel_id=1, source_target_pairs={{0,1},{1,0},{2,3},{3,2},{4,5},{5,4},{6,7},{7,6},{8,9},{9,8},{10,11... | collective-permute-start | bytes 1966088 | tf_op jit(solution)/shard_map/ppermute | solution.py:315
  75.6 12.4 %copy-start.28 = (f32[40]{0:T(128)S(1)}, f32[40]{0:T(128)}, u32[]{:S(2)}) copy-start(f32[40]{0:T(128)} %param.13) | copy-start | bytes 484
  75.6 26.4 %collective-permute-start.16 = (f32[2,2,32,1280]{3,2,1,0:T(8,128)}, f32[2,2,32,1280]{3,2,1,0:T(8,128)}, u32[]{:S(2)}, u32[]{:S(2)}) collective-permute-start(f32[2,2,32,1280]{3,2,1,0:T(8,128)} %pad_maximum_fusion.4), channel_id=1, source_target_pairs={{0,1},{1,0},{2,3},{3,2},{4,5},{5,4},{6,7},{7,6},{8,9},{9,8},{10,11... | collective-permute-start | bytes 1966088 | tf_op jit(solution)/shard_map/ppermute | solution.py:315
  88.0 2.3 %copy-start.19 = (f32[1,2560]{1,0:T(1,128)S(1)}, f32[1,2560]{1,0:T(1,128)}, u32[]{:S(2)}) copy-start(f32[1,2560]{1,0:T(1,128)} %copy-done.18) | copy-start | bytes 30724
  88.0 2.3 %copy-start.23 = (s32[2]{0:T(128)S(1)}, s32[2]{0:T(128)}, u32[]{:S(2)}) copy-start(s32[2]{0:T(128)} %copy-done.22) | copy-start | bytes 28
  88.0 2.3 %copy-start.25 = (f32[40]{0:T(128)S(1)}, f32[40]{0:T(128)}, u32[]{:S(2)}) copy-start(f32[40]{0:T(128)} %param.12) | copy-start | bytes 484
  88.0 2.2 %copy-start.7 = (bf16[512,512]{1,0:T(8,128)(2,1)S(1)}, bf16[512,512]{1,0:T(8,128)(2,1)}, u32[]{:S(2)}) copy-start(bf16[512,512]{1,0:T(8,128)(2,1)} %copy-done.6) | copy-start | bytes 1572868
  117.6 3.1 %copy-start.26 = (bf16[512,1280]{1,0:T(8,128)(2,1)S(1)}, bf16[512,1280]{1,0:T(8,128)(2,1)}, u32[]{:S(2)}) copy-start(bf16[512,1280]{1,0:T(8,128)(2,1)} %get-tuple-element.51) | copy-start | bytes 3932164
  117.6 3.1 %copy-start.27 = (bf16[512,1280]{1,0:T(8,128)(2,1)S(1)}, bf16[512,1280]{1,0:T(8,128)(2,1)}, u32[]{:S(2)}) copy-start(bf16[512,1280]{1,0:T(8,128)(2,1)} %get-tuple-element.52) | copy-start | bytes 3932164
  (14 other events, 15.3 us)

commit v2 on v1

v2 whole, which is shorter than its diff:
```python
import functools

import jax
import jax.numpy as jnp
from jax import lax
from jax.experimental import pallas as pl
from jax.experimental.pallas import tpu as pltpu
from jax.sharding import PartitionSpec as P

CHUNKS = 2
TILE = 640
VMEM_BYTES = 24 * 1024 * 1024

F32 = jnp.float32
BF16 = jnp.bfloat16


def dot_nn(left, right):
    return lax.dot_general(left, right, (((1,), (0,)), ((), ())), preferred_element_type=F32)


def dot_nt(left, right):
    return lax.dot_general(left, right, (((1,), (1,)), ((), ())), preferred_element_type=F32)


def halves(value):
    high = value.astype(BF16)
    return high, (value - high.astype(F32)).astype(BF16)


def sum_dot(matrix, value):
    first = value.astype(BF16)
    rest = value - first.astype(F32)
    second = rest.astype(BF16)
    third = (rest - second.astype(F32)).astype(BF16)
    return dot_nn(matrix, first) + dot_nn(matrix, second) + dot_nn(matrix, third)


def head_spread(head_count, first_column, columns, head_size):
    row = lax.broadcasted_iota(jnp.int32, (2 * head_count, columns), 0)
    row = jnp.where(row >= head_count, row - head_count, row)
    column = lax.broadcasted_iota(jnp.int32, (2 * head_count, columns), 1) + first_column
    offset = column - row * head_size
    return jnp.where((offset >= 0) & (offset < head_size), 1.0, 0.0).astype(BF16)


def head_collect(head_count, first_column, columns, head_size):
    row = lax.broadcasted_iota(jnp.int32, (columns, head_count), 0) + first_column
    column = lax.broadcasted_iota(jnp.int32, (columns, head_count), 1)
    offset = row - column * head_size
    return jnp.where((offset >= 0) & (offset < head_size), 1.0, 0.0).astype(BF16)


def triangle(rows, lower):
    first = lax.broadcasted_iota(jnp.int32, (rows, rows), 0)
    second = lax.broadcasted_iota(jnp.int32, (rows, rows), 1)
    return (first >= second) if lower else (first <= second)


def start_counts(starts_row):
    rows = starts_row.shape[1]
    flags = starts_row.astype(F32)
    column = jnp.sum(jnp.where(triangle(rows, True), flags, 0.0), axis=1, keepdims=True)
    spread = jnp.broadcast_to(flags, (8, rows)).astype(BF16)
    row = dot_nn(spread, triangle(rows, False).astype(F32).astype(BF16))[:1]
    return column, row


def softplus(value):
    return jnp.maximum(value, 0.0) + jnp.log1p(jnp.exp(-jnp.abs(value)))


def sum_dot_left(value, matrix):
    first = value.astype(BF16)
    rest = value - first.astype(F32)
    second = rest.astype(BF16)
    third = (rest - second.astype(F32)).astype(BF16)
    return dot_nn(first, matrix) + dot_nn(second, matrix) + dot_nn(third, matrix)


def prep_kernel(
    head_size, raw_ref, rate_ref, starts_ref, query_ref, key_ref,
    lead_ref, tail_ref, leadt_ref, tailt_ref, grow_ref, fall_ref, decay_ref, last_ref,
):
    head_count, rows = raw_ref.shape
    step = softplus(raw_ref[...])
    upper = triangle(rows, False).astype(F32).astype(BF16)
    cumulative = sum_dot_left(-step * rate_ref[...], upper)
    count, _ = start_counts(starts_ref[...])
    lead = jnp.where(count == 0.0, query_ref[...].astype(F32), 0.0)
    tail = jnp.where(count == count[rows - 1 :, :], key_ref[...].astype(F32), 0.0)
    lead_ref[...] = lead.astype(BF16)
    tail_ref[...] = tail.astype(BF16)
    leadt_ref[...] = lead.T.astype(BF16)
    tailt_ref[...] = tail.T.astype(BF16)
    fall = jnp.exp(cumulative).T
    fall_ref[...] = jnp.concatenate(halves(fall), axis=1)
    grow_ref[...] = jnp.concatenate(halves((jnp.exp(-cumulative) * step).T), axis=1)
    last = jnp.broadcast_to(fall[rows - 1 :, :], (8, head_count))
    channels = decay_ref.shape[1]
    spread = head_spread(head_count, 0, channels, head_size)
    last_wide = dot_nn(jnp.concatenate(halves(last), axis=1), spread)[:1]
    last_ref[...] = last_wide
    decay_ref[...] = jnp.where(count[rows - 1 :, :] == 0.0, last_wide, 0.0)


def place():
    index = lax.axis_index("seq")
    return (index & 1) == 0, (index & 2) == 0, index >> 2


def joined(first, own_decay, other_decay, own, came):
    one = jnp.ones_like(own_decay)
    forward = (
        jnp.where(first, other_decay, one) * own[0] + jnp.where(first, one, own_decay) * came[0]
    )
    backward = (
        jnp.where(first, one, other_decay) * own[1] + jnp.where(first, own_decay, one) * came[1]
    )
    return forward, backward


def split_pair(first, own_decay, other_decay, own, came, entering, leaving, put_own, put_other):
    @pl.when(first)
    def _():
        put_own(0, entering)
        put_other(0, own_decay * entering + own[0])
        put_other(1, leaving)
        put_own(1, other_decay * leaving + came[1])

    @pl.when(jnp.logical_not(first))
    def _():
        put_other(0, entering)
        put_own(0, other_decay * entering + came[0])
        put_own(1, leaving)
        put_other(1, own_decay * leaving + own[1])


def chip_kernel(
    columns, kept_ref, came_ref, own_ref, other_ref, sent_ref, side_ref, chip_ref=None
):
    first, _, _ = place()
    forward, backward = joined(
        first, own_ref[:, columns], other_ref[:, columns], kept_ref, came_ref
    )
    for chain, value in enumerate((forward, backward)):
        sent_ref[chain] = value[0]
        side_ref[chain] = value[1]
    if chip_ref is not None:
        chip_ref[...] = own_ref[...] * other_ref[...]


def plane_kernel(
    columns, kept_ref, came_ref, own_ref, other_ref, pay_ref, both_ref, plane_ref=None
):
    _, first, plane = place()
    forward, backward = joined(
        first, own_ref[:, columns], other_ref[:, columns], kept_ref, came_ref
    )
    both_ref[0] = forward
    both_ref[1] = backward
    pay_ref[...] = jnp.where((plane & 1) == 1, backward, forward)
    if plane_ref is not None:
        plane_ref[...] = own_ref[...] * other_ref[...]


def absorb(columns, level, plane, taken_refs, others, enter_ref):
    upper = ((plane >> level) & 1) == 1
    taken = taken_refs[0][...]
    for ref in taken_refs[1:]:
        taken = taken + ref[...]
    if level == 0:
        zero = jnp.zeros_like(taken)
        return jnp.where(upper, taken, zero), jnp.where(upper, zero, taken)
    before = after = None
    for lower, ref in enumerate(others[:level]):
        other = ref[:, columns]
        above = ((plane >> lower) & 1) == 1
        one = jnp.ones_like(other)
        first = jnp.where(above, other, one)
        second = jnp.where(above, one, other)
        before = first if before is None else before * first
        after = second if after is None else after * second
    zero = jnp.zeros_like(before)
    return (
        enter_ref[0] + jnp.where(upper, before, zero) * taken,
        enter_ref[1] + jnp.where(upper, zero, after) * taken,
    )


def level_kernel(columns, level, taken_count, *refs):
    taken, refs = refs[:taken_count], refs[taken_count:]
    others, refs = refs[:level], refs[level:]
    enter_ref = None
    if level:
        enter_ref, refs = refs[0], refs[1:]
    both_ref, decay_ref, pay_ref, next_ref = refs
    _, _, plane = place()
    entering, leaving = absorb(columns, level, plane, taken, others, enter_ref)
    next_ref[0] = entering
    next_ref[1] = leaving
    upper = ((plane >> (level + 1)) & 1) == 1
    decay = decay_ref[:, columns]

    @pl.when(upper)
    def _():
        pay_ref[...] = decay * leaving + both_ref[1]

    @pl.when(jnp.logical_not(upper))
    def _():
        pay_ref[...] = decay * entering + both_ref[0]


def top_kernel(columns, level, taken_count, *refs):
    taken, refs = refs[:taken_count], refs[taken_count:]
    others, refs = refs[:level], refs[level:]
    enter_ref = None
    if level:
        enter_ref, refs = refs[0], refs[1:]
    kept_ref, came_ref, own_ref, other_ref, theirs_ref, mine_ref = refs
    _, first, plane = place()
    entering, leaving = absorb(columns, level, plane, taken, others, enter_ref)

    def put_own(chain, value):
        mine_ref[chain] = value

    def put_other(chain, value):
        theirs_ref[chain] = value

    split_pair(
        first, own_ref[:, columns], other_ref[:, columns], kept_ref, came_ref, entering, leaving,
        put_own, put_other,
    )


def device_kernel(
    columns, back_ref, mine_ref, kept_ref, came_ref, own_ref, other_ref, give_ref, stay_ref
):
    first, _, _ = place()
    for slot, source in enumerate((back_ref, mine_ref)):

        def put_own(chain, value, slot=slot):
            stay_ref[chain, slot] = value

        def put_other(chain, value, slot=slot):
            give_ref[chain, slot] = value

        split_pair(
            first, own_ref[:, columns], other_ref[:, columns], kept_ref.at[:, slot],
            came_ref.at[:, slot], source[0], source[1], put_own, put_other,
        )


def states_kernel(
    head_count, head_size, first, in_ref, cot_ref, grow_ref, fall_ref, leadt_ref, tailt_ref,
    last_ref, send_ref, keep_ref,
):
    columns = in_ref.shape[1]
    spread = head_spread(head_count, first + pl.program_id(0) * columns, columns, head_size)
    grown = (dot_nn(grow_ref[...], spread) * in_ref[...].astype(F32)).astype(BF16)
    fallen = (dot_nn(fall_ref[...], spread) * cot_ref[...].astype(F32)).astype(BF16)
    state = dot_nn(tailt_ref[...], grown) * last_ref[...]
    direct = dot_nn(leadt_ref[...], fallen)
    low, mid, _ = place()
    half = state.shape[0] // 2
    quarter = half // 2
    for chain, value in enumerate((state, direct)):
        sent = jnp.where(low, value[half:], value[:half])
        kept = jnp.where(low, value[:half], value[half:])
        for ref, part in ((send_ref, sent), (keep_ref, kept)):
            ref[chain, 0] = jnp.where(mid, part[quarter:], part[:quarter])
            ref[chain, 1] = jnp.where(mid, part[:quarter], part[quarter:])


def scores_kernel(
    head_count, head_size, steps, starts_ref, query_ref, key_ref, in_ref, cot_ref, grow_ref,
    fall_ref, score_ref, scoret_ref, dquery_ref, dkey_ref, total_ref,
):
    columns = in_ref.shape[1]
    rows = in_ref.shape[0]
    step = pl.program_id(0)
    spread = head_spread(head_count, step * columns, columns, head_size)
    grown = (dot_nn(grow_ref[...], spread) * in_ref[...].astype(F32)).astype(BF16)
    fallen = (dot_nn(fall_ref[...], spread) * cot_ref[...].astype(F32)).astype(BF16)
    product = dot_nt(fallen, grown)

    @pl.when(step == 0)
    def _():
        total_ref[...] = product

    @pl.when(step > 0)
    def _():
        total_ref[...] += product

    @pl.when(step == steps - 1)
    def _():
        column, row = start_counts(starts_ref[...])
        same = column == row
        allowed = same & triangle(rows, True)
        score_ref[...] = jnp.where(allowed, dot_nt(query_ref[...], key_ref[...]), 0.0).astype(BF16)
        scoret_ref[...] = jnp.where(
            same & triangle(rows, False), dot_nt(key_ref[...], query_ref[...]), 0.0
        ).astype(BF16)
        grads = jnp.where(allowed, total_ref[...], 0.0)
        dquery_ref[...] = dot_nn(grads.astype(BF16), key_ref[...])
        dkey_ref[...] = dot_nn(grads.T.astype(BF16), query_ref[...])


def arranged(low, mid, took_ref, own_ref, chain):
    parts = []
    for ref in (own_ref, took_ref):
        first = jnp.where(mid, ref[chain, 1], ref[chain, 0])
        second = jnp.where(mid, ref[chain, 0], ref[chain, 1])
        parts.append(jnp.concatenate([first, second], axis=0))
    own, took = parts
    return jnp.concatenate([jnp.where(low, own, took), jnp.where(low, took, own)], axis=0)


def finish_kernel(
    head_count, head_size, first, steps, prior, in_ref, cot_ref, took_ref, own_ref, skip_ref,
    decay_ref, last_ref, grow_ref, fall_ref, lead_ref, tail_ref, score_ref, scoret_ref, starts_ref,
    raw_ref, rate_ref, dquery_in, dkey_in, *refs,
):
    if prior:
        draw_in, refs = refs[0], refs[3:]
    (
        out_ref, din_ref, dquery_ref, dkey_ref, draw_ref,
        rise_ref, sink_ref, edge_ref, dlead_ref, dtail_ref,
    ) = refs
    rows, columns = in_ref.shape
    step = pl.program_id(0)
    start_column = first + step * columns
    low, mid, _ = place()
    entering = arranged(low, mid, took_ref, own_ref, 0)
    leaving = arranged(low, mid, took_ref, own_ref, 1)
    spread = head_spread(head_count, start_column, columns, head_size)
    grow = dot_nn(grow_ref[...], spread)
    fall = dot_nn(fall_ref[...], spread)
    in_wide = in_ref[...].astype(F32)
    cot_wide = cot_ref[...].astype(F32)
    grown = (grow * in_wide).astype(BF16)
    fallen = (fall * cot_wide).astype(BF16)
    entering_bf = entering.astype(BF16)
    leaving_bf = (leaving * last_ref[...]).astype(BF16)

    produced = dot_nn(score_ref[...], grown) + dot_nn(lead_ref[...], entering_bf)
    out_ref[...] = (fall * produced + skip_ref[...] * in_wide).astype(BF16)
    behind = dot_nn(tail_ref[...], leaving_bf)
    pulled = dot_nn(scoret_ref[...], fallen) + behind
    din_ref[...] = (grow * pulled + skip_ref[...] * cot_wide).astype(BF16)

    collect = head_collect(head_count, start_column, columns, head_size)

    def by_head(value):
        return dot_nn(value.astype(BF16), collect)

    grown_wide = grown.astype(F32)
    rise = by_head(fallen.astype(F32) * produced)
    sink = by_head(grown_wide * pulled)
    edge_row = jnp.sum(grown_wide * behind, axis=0, keepdims=True) + decay_ref[...] * jnp.sum(
        entering * leaving, axis=0, keepdims=True
    )
    high, rest = halves(jnp.broadcast_to(edge_row, (8, columns)))
    edge = dot_nn(high, collect) + dot_nn(rest, collect)
    dlead = dot_nt(fallen, entering_bf)
    dtail = dot_nt(grown, leaving_bf)

    @pl.when(step == 0)
    def _():
        rise_ref[...] = rise
        sink_ref[...] = sink
        edge_ref[...] = edge
        dlead_ref[...] = dlead
        dtail_ref[...] = dtail

    @pl.when(step > 0)
    def _():
        rise_ref[...] += rise
        sink_ref[...] += sink
        edge_ref[...] += edge
        dlead_ref[...] += dlead
        dtail_ref[...] += dtail

    @pl.when(step == steps - 1)
    def _():
        count, _ = start_counts(starts_ref[...])
        dquery = dquery_in[...] + jnp.where(count == 0.0, dlead_ref[...], 0.0)
        dkey = dkey_in[...] + jnp.where(count == count[rows - 1 :, :], dtail_ref[...], 0.0)
        dquery_ref[...] = dquery.astype(dquery_ref.dtype)
        dkey_ref[...] = dkey.astype(dkey_ref.dtype)
        upper = triangle(rows, False).astype(F32).astype(BF16)
        later = sum_dot(upper, rise_ref[...] - sink_ref[...]) + edge_ref[:1]
        raw = raw_ref[...]
        dstep = sink_ref[...].T / softplus(raw) - rate_ref[...] * later.T
        draw = dstep / (1.0 + jnp.exp(-raw))
        draw_ref[...] = draw_in[...] + draw if prior else draw


def whole(shape):
    return pl.BlockSpec(shape, lambda i, *_: (0,) * len(shape))


def params():
    return pltpu.CompilerParams(vmem_limit_bytes=VMEM_BYTES)


def cost(flops, count):
    return pl.CostEstimate(flops=flops, bytes_accessed=count, transcendentals=0)


def local(inputs, raw_steps, input_map, output_map, decay_rates, skip_gain, starts, cotangent):
    rows, channels = inputs.shape
    head_count = decay_rates.shape[0]
    head_size = channels // head_count
    state_size = input_map.shape[1]
    width = channels // CHUNKS
    tiles = width // TILE
    quarter = state_size // 4

    size = lax.axis_size("seq")
    planes = size // 4
    levels = planes.bit_length() - 1
    starts_row = starts.reshape(1, rows)
    rate_column = decay_rates.reshape(head_count, 1)
    raw_turned = raw_steps.T
    skip_row = jnp.repeat(skip_gain, head_size).reshape(1, channels)

    def shape(dims, kind=F32):
        return jax.ShapeDtypeStruct(dims, kind)

    lead, tail, leadt, tailt, grow, fall, decay, last = pl.pallas_call(
        functools.partial(prep_kernel, head_size),
        out_shape=(
            shape((rows, state_size), BF16),
            shape((rows, state_size), BF16),
            shape((state_size, rows), BF16),
            shape((state_size, rows), BF16),
            shape((rows, 2 * head_count), BF16),
            shape((rows, 2 * head_count), BF16),
            shape((1, channels)),
            shape((1, channels)),
        ),
        compiler_params=params(),
        name="prep",
    )(raw_turned, rate_column, starts_row, output_map, input_map)

    def pieces(chunk):
        first = chunk * tiles
        tile = pl.BlockSpec((rows, TILE), lambda i, *_: (0, first + i))
        row = pl.BlockSpec((1, TILE), lambda i, *_: (0, first + i))
        part = pl.BlockSpec((2, 2, quarter, TILE), lambda i, *_: (0, 0, 0, i))
        return tile, row, part

    def device_states(chunk):
        tile, row, part = pieces(chunk)
        half = shape((2, 2, quarter, width))
        return pl.pallas_call(
            functools.partial(states_kernel, head_count, head_size, chunk * width),
            out_shape=(half, half),
            grid=(tiles,),
            in_specs=[
                tile, tile, whole(grow.shape), whole(fall.shape), whole(leadt.shape),
                whole(tailt.shape), row,
            ],
            out_specs=(part, part),
            compiler_params=params(),
            cost_estimate=cost(
                4 * rows * state_size * width + 8 * rows * head_count * width, 6 * rows * width
            ),
            name="states",
        )(inputs, cotangent, grow, fall, leadt, tailt, last)

    def swap(value, bit):
        return lax.ppermute(value, "seq", [(i, i ^ bit) for i in range(size)])

    def level_perms(level):
        span = 1 << level
        perms = []
        for shift in range(span):
            pairs = []
            for base in range(0, planes, 2 * span):
                pairs.append((base + span - 1, base + span + shift))
                pairs.append((base + span, base + span - 1 - shift))
            perms.append([(4 * a + r, 4 * b + r) for a, b in pairs for r in range(4)])
        return perms

    def small(kernel, out_shape, name, *operands):
        return pl.pallas_call(
            kernel, out_shape=out_shape, compiler_params=params(), name=name
        )(*operands)

    flat_shape = shape((quarter, width))
    pair_shape = shape((2, quarter, width))
    four_shape = shape((2, 2, quarter, width))
    row_shape = shape((1, channels))
    score_tiles = channels // TILE
    all_tile = pl.BlockSpec((rows, TILE), lambda i, *_: (0, i))

    def scores(input_values):
        square = (rows, rows)
        return pl.pallas_call(
            functools.partial(scores_kernel, head_count, head_size, score_tiles),
            out_shape=(
                shape(square, BF16), shape(square, BF16),
                shape((rows, state_size)), shape((rows, state_size)),
            ),
            grid=(score_tiles,),
            in_specs=[
                whole(starts_row.shape), whole(output_map.shape), whole(input_map.shape),
                all_tile, all_tile, whole(grow.shape), whole(fall.shape),
            ],
            out_specs=(
                whole(square), whole(square),
                whole((rows, state_size)), whole((rows, state_size)),
            ),
            scratch_shapes=[pltpu.VMEM(square, F32)],
            compiler_params=params(),
            cost_estimate=cost(2 * rows * rows * channels, 4 * rows * channels),
            name="scores",
        )(starts_row, output_map, input_map, input_values, cotangent, grow, fall)

    def finish(chunk, took, own, sofar):
        tile, row, part = pieces(chunk)
        square = (rows, rows)
        flat = (rows, state_size)
        by_head = (head_count, rows)
        final = chunk == CHUNKS - 1
        prior = chunk > 0
        out, din, dquery, dkey, draw = sofar
        operands = [
            inputs, cotangent, took, own, skip_row, decay, last, grow, fall, lead, tail,
            score, scoret, starts_row, raw_turned, rate_column, dquery, dkey,
        ]
        in_specs = [
            tile, tile, part, part, row, row, row, whole(grow.shape), whole(fall.shape),
            whole(flat), whole(flat), whole(square), whole(square),
            whole(starts_row.shape), whole(by_head), whole(rate_column.shape),
            whole(flat), whole(flat),
        ]
        aliases = {}
        if prior:
            operands += [draw, out, din]
            in_specs += [whole(by_head), pl.BlockSpec(memory_space=pl.ANY)] + [
                pl.BlockSpec(memory_space=pl.ANY)
            ]
            aliases = {19: 0, 20: 1}
        kind = BF16 if final else F32
        return pl.pallas_call(
            functools.partial(finish_kernel, head_count, head_size, chunk * width, tiles, prior),
            out_shape=(
                shape((rows, channels), BF16), shape((rows, channels), BF16),
                shape(flat, kind), shape(flat, kind), shape(by_head),
            ),
            grid=(tiles,),
            in_specs=in_specs,
            out_specs=(tile, tile, whole(flat), whole(flat), whole(by_head)),
            scratch_shapes=[
                pltpu.VMEM((rows, head_count), F32), pltpu.VMEM((rows, head_count), F32),
                pltpu.VMEM((8, head_count), F32),
                pltpu.VMEM(flat, F32), pltpu.VMEM(flat, F32),
            ],
            input_output_aliases=aliases,
            compiler_params=params(),
            cost_estimate=cost(4 * rows * rows * width, 12 * rows * width),
            name="finish",
        )(*operands)

    every = range(CHUNKS)
    span = [slice(chunk * width, (chunk + 1) * width) for chunk in every]

    sent, kept, came = [None] * CHUNKS, [None] * CHUNKS, [None] * CHUNKS
    decay_other = swap(decay, 1)
    for k in every:
        sent[k], kept[k] = device_states(k)
        came[k] = swap(sent[k], 1)

    side_sent, side_kept, side_came = [None] * CHUNKS, [None] * CHUNKS, [None] * CHUNKS
    for k in every:
        made = small(
            functools.partial(chip_kernel, span[k]),
            (pair_shape, pair_shape) + ((row_shape,) if k == 0 else ()),
            "chip", kept[k], came[k], decay, decay_other,
        )
        side_sent[k], side_kept[k] = made[:2]
        if k == 0:
            chip_decay = made[2]
            chip_other = swap(chip_decay, 2)
        side_came[k] = swap(side_sent[k], 2)

    late = lax.optimization_barrier((inputs, *side_sent))
    score, scoret, dquery, dkey = scores(late[0])
    score, scoret, dquery, dkey, side_came[0] = lax.optimization_barrier(
        (score, scoret, dquery, dkey, side_came[0])
    )

    pay, both = [None] * CHUNKS, [None] * CHUNKS
    others = []
    taken, enter = [None] * CHUNKS, [None] * CHUNKS
    for k in every:
        made = small(
            functools.partial(plane_kernel, span[k]),
            (flat_shape, pair_shape) + ((row_shape,) if k == 0 else ()),
            "plane", side_kept[k], side_came[k], chip_decay, chip_other,
        )
        pay[k], both[k] = made[:2]
        if k == 0:
            plane_decay = group = made[2]
            for level in range(levels - 1):
                other = swap(group, 4 << level)
                others.append(other)
                group = group * other
    for level in range(levels):
        for k in every:
            taken[k] = [lax.ppermute(pay[k], "seq", perm) for perm in level_perms(level)]
        if level == levels - 1:
            break
        for k in every:
            operands = taken[k] + others[:level] + ([enter[k]] if level else [])
            pay[k], enter[k] = small(
                functools.partial(level_kernel, span[k], level, len(taken[k])),
                (flat_shape, pair_shape), "level", *operands, both[k], plane_decay,
            )
    back, mine = [None] * CHUNKS, [None] * CHUNKS
    for k in every:
        operands = taken[k] + others[: levels - 1] + ([enter[k]] if levels > 1 else [])
        theirs, mine[k] = small(
            functools.partial(top_kernel, span[k], levels - 1, len(taken[k])),
            (pair_shape, pair_shape), "top", *operands, side_kept[k], side_came[k],
            chip_decay, chip_other,
        )
        back[k] = swap(theirs, 2)
    took, own = [None] * CHUNKS, [None] * CHUNKS
    for k in every:
        give, own[k] = small(
            functools.partial(device_kernel, span[k]), (four_shape, four_shape), "device",
            back[k], mine[k], kept[k], came[k], decay, decay_other,
        )
        took[k] = swap(give, 1)
    sofar = (None, None, dquery, dkey, None)
    for k in every:
        sofar = finish(k, took[k], own[k], sofar)
    out, din, dquery, dkey, draw = sofar
    return out, din, draw.T, dkey, dquery


def solution(mesh):
    sequence = P(("groups", "seq"), None)
    return jax.shard_map(
        local,
        mesh=mesh,
        in_specs=(
            sequence, sequence, sequence, sequence, P(), P(), P(("groups", "seq")), sequence,
        ),
        out_specs=(sequence,) * 5,
        check_vma=False,
    )
```

time: 125 us -> 99.5 us (0.80); the launches traced: 122 us -> 98.7 us
  other arithmetic: 17.7 us -> 0 us
  Pallas kernels: 42.1 us -> 30.2 us
  local copies, waits for them, and re-layouts: 13.9 us -> 19.8 us
  starting transfers between devices: 20.3 us -> 24.5 us
  waiting for transfers between devices: 27.3 us -> 23.2 us
    pallas_call x2, Pallas kernels: 10 us -> 3.71 us  [device_states(): pl.pallas_call(functools.partial(states_kernel, head_count, head_size, ch...]
    ppermute x11, starting transfers between devices: 12.5 us -> 18.4 us  [swap(): return lax.ppermute(value, 'seq', [(i, i ^ bit) for i in range(size)])]
    concatenate x2 -> x0, other arithmetic: 4.83 us -> none  [the longest x1 3.14 us: local(): jnp.concatenate(outs, axis=1)]
    unnamed x60 -> x56, local copies, waits for them, and re-layouts: 12.7 us -> 17.5 us
    pallas_call x1, Pallas kernels: 9.67 us -> 5.38 us  [scores(): pl.pallas_call(functools.partial(scores_kernel, head_count, head_size, sc...]
    ppermute x6, waiting for transfers between devices: 9.51 us -> 5.22 us  [local(): lax.ppermute(pay[k], 'seq', perm)]
    pallas_call x2, Pallas kernels: 21.4 us -> 17.4 us  [finish(): pl.pallas_call(functools.partial(finish_kernel, head_count, head_size, ch...]
    select_n x8 -> x0, other arithmetic: 3.75 us -> none  [the longest x2 3.44 us: chain(): jnp.where(first_core, chip_in[0], inner)]
  transfers between devices with their start and end apart: 17 -> 17, of which waited for: 9 -> 8; matrix products, arithmetic and copies ran while one was open for 10% -> 2% of each run, Pallas kernels for 25% -> 19%
where the time goes in v2:
time: 99.5 us; the launch traced here: 98.7 us
  Pallas kernels  30.2 us (30%)
  starting transfers between devices  24.5 us (25%)
  waiting for transfers between devices  23.2 us (23%)
  local copies, waits for them, and re-layouts  19.8 us (20%)
  between operations  1.01 us (1%)
    ppermute x11, starting transfers between devices, swap(): return lax.ppermute(value, 'seq', [(i, i ^ bit) for i in range(size)])  18.4 us
    ppermute x11, waiting for transfers between devices, swap(): return lax.ppermute(value, 'seq', [(i, i ^ bit) for i in range(size)])  18 us
    unnamed x56, local copies, waits for them, and re-layouts  17.5 us
    pallas_call x2, Pallas kernels, finish(): pl.pallas_call(functools.partial(finish_kernel, head_count, head_size, ch...  17.4 us
    ppermute x6, starting transfers between devices, local(): lax.ppermute(pay[k], 'seq', perm)  6.08 us
    pallas_call x1, Pallas kernels, scores(): pl.pallas_call(functools.partial(scores_kernel, head_count, head_size, sc...  5.38 us
    ppermute x6, waiting for transfers between devices, local(): lax.ppermute(pay[k], 'seq', perm)  5.22 us
    pallas_call x2, Pallas kernels, device_states(): pl.pallas_call(functools.partial(states_kernel, head_count, head_size, ch...  3.71 us
  transfers between devices with their start and end apart: 17, of which 8 were waited for; matrix products, arithmetic and copies ran while one was open for 2% of the time, Pallas kernels for 19%

profile of v2, /device:TPU:0, one launch (start us, length us, event | category | flops | bytes accessed | tf_op | source)
XLA Modules:
  0.0 98.7 jit_solution(4976642754908858236)
XLA Ops:
  2.3 0.9 copy-done.17
  3.2 0.9 copy-done.19
  6.3 1.8 %copy-done = bf16[512,2560]{1,0:T(8,128)(2,1)S(1)} copy-done((bf16[512,2560]{1,0:T(8,128)(2,1)S(1)}, bf16[512,2560]{1,0:T(8,128)(2,1)}, u32[]{:S(2)}) %copy-start) | copy-done | bytes 2621464
  8.1 1.7 %copy-done.2 = bf16[512,2560]{1,0:T(8,128)(2,1)S(1)} copy-done((bf16[512,2560]{1,0:T(8,128)(2,1)S(1)}, bf16[512,2560]{1,0:T(8,128)(2,1)}, u32[]{:S(2)}) %copy-start.2) | copy-done | bytes 2621464
  9.8 1.9 %states.3 = (f32[2,2,32,1280]{3,2,1,0:T(8,128)S(1)}, f32[2,2,32,1280]{3,2,1,0:T(8,128)S(1)}) custom-call(bf16[512,2560]{1,0:T(8,128)(2,1)S(1)} %copy-done, bf16[512,2560]{1,0:T(8,128)(2,1)S(1)} %copy-done.2, bf16[512,80]{1,0:T(8,128)(2,1)S(1)} %get-tuple-element.59.grow_ref, bf16[512,80]{1,0:T(8,128)(2,1)S(1)} %get-tuple-element.60.fall_ref, ...), custom_call_target="tpu_custom_call" | custom-call | flops 545259520 | bytes 3932160 | tf_op jit(solution)/shard_map/states/pallas_call | solution.py:457
  12.2 1.9 %states.2 = (f32[2,2,32,1280]{3,2,1,0:T(8,128)S(1)}, f32[2,2,32,1280]{3,2,1,0:T(8,128)S(1)}) custom-call(bf16[512,2560]{1,0:T(8,128)(2,1)S(1)} %copy-done, bf16[512,2560]{1,0:T(8,128)(2,1)S(1)} %copy-done.2, bf16[512,80]{1,0:T(8,128)(2,1)S(1)} %get-tuple-element.59.grow_ref, bf16[512,80]{1,0:T(8,128)(2,1)S(1)} %get-tuple-element.60.fall_ref, ...), custom_call_target="tpu_custom_call" | custom-call | flops 545259520 | bytes 3932160 | tf_op jit(solution)/shard_map/states/pallas_call | solution.py:457
  14.6 1.6 %collective-permute-done.1.other_ref = f32[1,2560]{1,0:T(1,128)S(1)} collective-permute-done((f32[1,2560]{1,0:T(1,128)S(1)}, f32[1,2560]{1,0:T(1,128)S(1)}, u32[]{:S(2)}, u32[]{:S(2)}) %collective-permute-start.1) | collective-permute-done | bytes 10272 | tf_op jit(solution)/shard_map/ppermute | solution.py:474
  16.3 2.7 %collective-permute-start.6 = (f32[2,32,1280]{2,1,0:T(8,128)S(1)}, f32[2,32,1280]{2,1,0:T(8,128)S(1)}, u32[]{:S(2)}, u32[]{:S(2)}) collective-permute-start(f32[2,32,1280]{2,1,0:T(8,128)S(1)} %get-tuple-element.75), channel_id=1, source_target_pairs={{0,2},{1,3},{2,0},{3,1},{4,6},{5,7},{6,4},{7,5},{8,10},{9,11},{10,... | collective-permute-start | bytes 983048 | tf_op jit(solution)/shard_map/ppermute | solution.py:474
  19.3 2.0 %collective-permute-start.4 = (f32[1,2560]{1,0:T(1,128)S(1)}, f32[1,2560]{1,0:T(1,128)S(1)}, u32[]{:S(2)}, u32[]{:S(2)}) collective-permute-start(f32[1,2560]{1,0:T(1,128)S(1)} %get-tuple-element.71.own_ref.refs_6_), channel_id=1, source_target_pairs={{0,2},{1,3},{2,0},{3,1},{4,6},{5,7},{6,4},{7,5},{8,10},{9,11},{10,... | collective-permute-start | bytes 30728 | tf_op jit(solution)/shard_map/ppermute | solution.py:474
  21.3 5.4 %scores.1 = (bf16[512,512]{1,0:T(8,128)(2,1)S(1)}, bf16[512,512]{1,0:T(8,128)(2,1)S(1)}, f32[512,128]{1,0:T(8,128)S(1)}, f32[512,128]{1,0:T(8,128)S(1)}) custom-call(s32[1,512]{1,0:T(1,128)S(1)} %bitcast.8, bf16[512,128]{1,0:T(8,128)(2,1)S(1)} %copy-done.18, bf16[512,128]{1,0:T(8,128)(2,1)S(1)} %copy-done.20, bf16[512,2560]{1,0:T(8,128)(2,1)S(1)} %copy-done.1, ...), custom_call_target="tpu_custom_call" | custom-call | flops 1342177280 | bytes 5242880 | tf_op jit(solution)/shard_map/scores/pallas_call | solution.py:501
  27.6 6.9 %collective-permute-done.4.other_ref.refs_7_ = f32[1,2560]{1,0:T(1,128)S(1)} collective-permute-done((f32[1,2560]{1,0:T(1,128)S(1)}, f32[1,2560]{1,0:T(1,128)S(1)}, u32[]{:S(2)}, u32[]{:S(2)}) %collective-permute-start.4) | collective-permute-done | bytes 10272 | tf_op jit(solution)/shard_map/ppermute | solution.py:474
  34.6 1.9 %collective-permute-start.12 = (f32[32,1280]{1,0:T(8,128)S(1)}, f32[32,1280]{1,0:T(8,128)S(1)}, u32[]{:S(2)}, u32[]{:S(2)}) collective-permute-start(f32[32,1280]{1,0:T(8,128)S(1)} %get-tuple-element.93), channel_id=1, source_target_pairs={{0,4},{1,5},{2,6},{3,7},{4,0},{5,1},{6,2},{7,3},{8,12},{9,13},{10,... | collective-permute-start | bytes 491528 | tf_op jit(solution)/shard_map/ppermute | solution.py:614
  36.9 4.9 %collective-permute-done.12.refs_0_ = f32[32,1280]{1,0:T(8,128)S(1)} collective-permute-done((f32[32,1280]{1,0:T(8,128)S(1)}, f32[32,1280]{1,0:T(8,128)S(1)}, u32[]{:S(2)}, u32[]{:S(2)}) %collective-permute-start.12) | collective-permute-done | bytes 163872 | tf_op jit(solution)/shard_map/ppermute | solution.py:614
  41.9 1.3 %collective-permute-start.14 = (f32[32,1280]{1,0:T(8,128)S(1)}, f32[32,1280]{1,0:T(8,128)S(1)}, u32[]{:S(2)}, u32[]{:S(2)}) collective-permute-start(f32[32,1280]{1,0:T(8,128)S(1)} %get-tuple-element.95), channel_id=1, source_target_pairs={{4,12},{5,13},{6,14},{7,15},{8,0},{9,1},{10,2},{11,3},{20,28},{21,... | collective-permute-start | bytes 491528 | tf_op jit(solution)/shard_map/ppermute | solution.py:614
  44.2 1.3 %collective-permute-start.8 = (f32[32,1280]{1,0:T(8,128)S(1)}, f32[32,1280]{1,0:T(8,128)S(1)}, u32[]{:S(2)}, u32[]{:S(2)}) collective-permute-start(f32[32,1280]{1,0:T(8,128)S(1)} %get-tuple-element.83), channel_id=1, source_target_pairs={{4,12},{5,13},{6,14},{7,15},{8,0},{9,1},{10,2},{11,3},{20,28},{21,... | collective-permute-start | bytes 491528 | tf_op jit(solution)/shard_map/ppermute | solution.py:614
  46.2 9.3 %collective-permute-start.9 = (f32[1,2560]{1,0:T(1,128)S(1)}, f32[1,2560]{1,0:T(1,128)S(1)}, u32[]{:S(2)}, u32[]{:S(2)}) collective-permute-start(f32[1,2560]{1,0:T(1,128)S(1)} %get-tuple-element.82.refs_2_), channel_id=1, source_target_pairs={{0,4},{1,5},{2,6},{3,7},{4,0},{5,1},{6,2},{7,3},{8,12},{9,13},{10,... | collective-permute-start | bytes 30728 | tf_op jit(solution)/shard_map/ppermute | solution.py:474
  55.5 1.8 %collective-permute-done.9.refs_2_ = f32[1,2560]{1,0:T(1,128)S(1)} collective-permute-done((f32[1,2560]{1,0:T(1,128)S(1)}, f32[1,2560]{1,0:T(1,128)S(1)}, u32[]{:S(2)}, u32[]{:S(2)}) %collective-permute-start.9) | collective-permute-done | bytes 10272 | tf_op jit(solution)/shard_map/ppermute | solution.py:474
  57.4 1.6 %collective-permute-start.15 = (f32[2,32,1280]{2,1,0:T(8,128)S(1)}, f32[2,32,1280]{2,1,0:T(8,128)S(1)}, u32[]{:S(2)}, u32[]{:S(2)}) collective-permute-start(f32[2,32,1280]{2,1,0:T(8,128)S(1)} %get-tuple-element.97), channel_id=1, source_target_pairs={{0,2},{1,3},{2,0},{3,1},{4,6},{5,7},{6,4},{7,5},{8,10},{9,11},{10,... | collective-permute-start | bytes 983048 | tf_op jit(solution)/shard_map/ppermute | solution.py:474
  59.1 1.6 %collective-permute-start.10 = (f32[2,32,1280]{2,1,0:T(8,128)S(1)}, f32[2,32,1280]{2,1,0:T(8,128)S(1)}, u32[]{:S(2)}, u32[]{:S(2)}) collective-permute-start(f32[2,32,1280]{2,1,0:T(8,128)S(1)} %get-tuple-element.85), channel_id=1, source_target_pairs={{0,2},{1,3},{2,0},{3,1},{4,6},{5,7},{6,4},{7,5},{8,10},{9,11},{10,... | collective-permute-start | bytes 983048 | tf_op jit(solution)/shard_map/ppermute | solution.py:474
  60.7 5.8 %collective-permute-done.15.back_ref = f32[2,32,1280]{2,1,0:T(8,128)S(1)} collective-permute-done((f32[2,32,1280]{2,1,0:T(8,128)S(1)}, f32[2,32,1280]{2,1,0:T(8,128)S(1)}, u32[]{:S(2)}, u32[]{:S(2)}) %collective-permute-start.15) | collective-permute-done | bytes 327712 | tf_op jit(solution)/shard_map/ppermute | solution.py:474
  66.5 1.0 %device.3 = (f32[2,2,32,1280]{3,2,1,0:T(8,128)}, f32[2,2,32,1280]{3,2,1,0:T(8,128)S(1)}) custom-call(f32[2,32,1280]{2,1,0:T(8,128)S(1)} %collective-permute-done.15.back_ref, f32[2,32,1280]{2,1,0:T(8,128)S(1)} %get-tuple-element.98.mine_ref, f32[2,2,32,1280]{3,2,1,0:T(8,128)S(1)} %get-tuple-element.69.kept_ref, ...), custom_call_target="tpu_custom_call" | custom-call | tf_op jit(solution)/shard_map/device/pallas_call | solution.py:488
  68.3 1.7 %collective-permute-done.10.back_ref = f32[2,32,1280]{2,1,0:T(8,128)S(1)} collective-permute-done((f32[2,32,1280]{2,1,0:T(8,128)S(1)}, f32[2,32,1280]{2,1,0:T(8,128)S(1)}, u32[]{:S(2)}, u32[]{:S(2)}) %collective-permute-start.10) | collective-permute-done | bytes 327712 | tf_op jit(solution)/shard_map/ppermute | solution.py:474
  70.0 1.2 %device.2 = (f32[2,2,32,1280]{3,2,1,0:T(8,128)}, f32[2,2,32,1280]{3,2,1,0:T(8,128)S(1)}) custom-call(f32[2,32,1280]{2,1,0:T(8,128)S(1)} %collective-permute-done.10.back_ref, f32[2,32,1280]{2,1,0:T(8,128)S(1)} %get-tuple-element.86.mine_ref, f32[2,2,32,1280]{3,2,1,0:T(8,128)S(1)} %get-tuple-element.64.kept_ref, ...), custom_call_target="tpu_custom_call" | custom-call | tf_op jit(solution)/shard_map/device/pallas_call | solution.py:488
  73.6 1.7 %copy-done.4 = bf16[512,2560]{1,0:T(8,128)(2,1)S(1)} copy-done((bf16[512,2560]{1,0:T(8,128)(2,1)S(1)}, bf16[512,2560]{1,0:T(8,128)(2,1)}, u32[]{:S(2)}) %copy-start.4) | copy-done | bytes 2621464
  75.3 1.0 %copy-done.6 = bf16[512,512]{1,0:T(8,128)(2,1)S(1)} copy-done((bf16[512,512]{1,0:T(8,128)(2,1)S(1)}, bf16[512,512]{1,0:T(8,128)(2,1)}, u32[]{:S(2)}) %copy-start.6) | copy-done | bytes 524312
  76.4 1.1 %copy-done.12 = f32[2,2,32,1280]{3,2,1,0:T(8,128)S(1)} copy-done((f32[2,2,32,1280]{3,2,1,0:T(8,128)S(1)}, f32[2,2,32,1280]{3,2,1,0:T(8,128)}, u32[]{:S(2)}) %copy-start.12) | copy-done | bytes 655384
  77.4 0.9 copy-done.14
  78.3 0.9 copy-done.16
  79.2 0.9 copy-done.22
  80.2 0.9 copy-done.24
  81.2 8.7 %finish.2 = (bf16[512,2560]{1,0:T(8,128)(2,1)}, bf16[512,2560]{1,0:T(8,128)(2,1)}, f32[512,128]{1,0:T(8,128)S(1)}, f32[512,128]{1,0:T(8,128)S(1)}, f32[40,512]{1,0:T(8,128)S(1)}) custom-call(bf16[512,2560]{1,0:T(8,128)(2,1)S(1)} %copy-done.1, bf16[512,2560]{1,0:T(8,128)(2,1)S(1)} %copy-done.4, f32[2,2,32,1280]{3,2,1,0:T(8,128)} %collective-permute-done.16.took_ref, ...), custom_call_target="tpu_custom_call" | custom-call | flops 1342177280 | bytes 7864320 | tf_op jit(solution)/shard_map/finish/pallas_call | solution.py:548
  89.8 8.7 %finish.3 = (bf16[512,2560]{1,0:T(8,128)(2,1)}, bf16[512,2560]{1,0:T(8,128)(2,1)}, bf16[512,128]{1,0:T(8,128)(2,1)}, bf16[512,128]{1,0:T(8,128)(2,1)}, f32[40,512]{1,0:T(8,128)}) custom-call(bf16[512,2560]{1,0:T(8,128)(2,1)S(1)} %copy-done.1, bf16[512,2560]{1,0:T(8,128)(2,1)S(1)} %copy-done.4, ...), custom_call_target="tpu_custom_call", output_to_operand_aliasing={{0}: (19, {}), {1}: (20, {})} | custom-call | flops 1342177280 | bytes 7864320 | tf_op jit(solution)/shard_map/finish/pallas_call | solution.py:548
  (77 shorter events, 11.8 us)
Async XLA Ops:
  6.3 5.4 %copy-start.13 = (bf16[512,128]{1,0:T(8,128)(2,1)}, bf16[512,128]{1,0:T(8,128)(2,1)S(1)}, u32[]{:S(2)}) copy-start(bf16[512,128]{1,0:T(8,128)(2,1)S(1)} %get-tuple-element.89.lead_ref) | copy-start | bytes 393220
  6.3 1.8 %copy-start = (bf16[512,2560]{1,0:T(8,128)(2,1)S(1)}, bf16[512,2560]{1,0:T(8,128)(2,1)}, u32[]{:S(2)}) copy-start(bf16[512,2560]{1,0:T(8,128)(2,1)} %in_ref.8) | copy-start | bytes 7864324
  8.0 1.7 %copy-start.2 = (bf16[512,2560]{1,0:T(8,128)(2,1)S(1)}, bf16[512,2560]{1,0:T(8,128)(2,1)}, u32[]{:S(2)}) copy-start(bf16[512,2560]{1,0:T(8,128)(2,1)} %cot_ref.9) | copy-start | bytes 7864324
  11.7 4.6 %collective-permute-start.3 = (f32[2,2,32,1280]{3,2,1,0:T(8,128)S(1)}, f32[2,2,32,1280]{3,2,1,0:T(8,128)S(1)}, u32[]{:S(2)}, u32[]{:S(2)}) collective-permute-start(f32[2,2,32,1280]{3,2,1,0:T(8,128)S(1)} %get-tuple-element.70), channel_id=1, source_target_pairs={{0,1},{1,0},{2,3},{3,2},{4,5},{5,4},{6,7},{7,6},{8,9},{9,8},{10,11... | collective-permute-start | bytes 1966088 | tf_op jit(solution)/shard_map/ppermute | solution.py:474
  12.2 9.1 %copy-start.3 = (bf16[512,2560]{1,0:T(8,128)(2,1)S(1)}, bf16[512,2560]{1,0:T(8,128)(2,1)}, u32[]{:S(2)}) copy-start(bf16[512,2560]{1,0:T(8,128)(2,1)} %cot_ref.9) | copy-start | bytes 7864324
  12.2 9.1 %copy-start.18 = (bf16[512,128]{1,0:T(8,128)(2,1)S(1)}, bf16[512,128]{1,0:T(8,128)(2,1)}, u32[]{:S(2)}) copy-start(bf16[512,128]{1,0:T(8,128)(2,1)} %query_ref.3) | copy-start | bytes 393220
  12.2 9.1 %copy-start.20 = (bf16[512,128]{1,0:T(8,128)(2,1)S(1)}, bf16[512,128]{1,0:T(8,128)(2,1)}, u32[]{:S(2)}) copy-start(bf16[512,128]{1,0:T(8,128)(2,1)} %key_ref.3) | copy-start | bytes 393220
  14.0 7.3 %copy-start.1 = (bf16[512,2560]{1,0:T(8,128)(2,1)S(1)}, bf16[512,2560]{1,0:T(8,128)(2,1)}, u32[]{:S(2)}) copy-start(bf16[512,2560]{1,0:T(8,128)(2,1)} %in_ref.8) | copy-start | bytes 7864324
  14.1 7.3 %copy-start.26 = (s32[512]{0:T(512)S(1)}, s32[512]{0:T(512)}, u32[]{:S(2)}) copy-start(s32[512]{0:T(512)} %param.14) | copy-start | bytes 6148
  14.1 5.0 %collective-permute-start = (f32[2,2,32,1280]{3,2,1,0:T(8,128)S(1)}, f32[2,2,32,1280]{3,2,1,0:T(8,128)S(1)}, u32[]{:S(2)}, u32[]{:S(2)}) collective-permute-start(f32[2,2,32,1280]{3,2,1,0:T(8,128)S(1)} %get-tuple-element.65), channel_id=1, source_target_pairs={{0,1},{1,0},{2,3},{3,2},{4,5},{5,4},{6,7},{7,6},{8,9},{9,8},{10,11... | collective-permute-start | bytes 1966088 | tf_op jit(solution)/shard_map/ppermute | solution.py:474
  14.2 2.0 %collective-permute-start.1 = (f32[1,2560]{1,0:T(1,128)S(1)}, f32[1,2560]{1,0:T(1,128)S(1)}, u32[]{:S(2)}, u32[]{:S(2)}) collective-permute-start(f32[1,2560]{1,0:T(1,128)S(1)} %get-tuple-element.66.own_ref.decay_ref), channel_id=1, source_target_pairs={{0,1},{1,0},{2,3},{3,2},{4,5},{5,4},{6,7},{7,6},{8,9},{9,8},{10,11... | collective-permute-start | bytes 30728 | tf_op jit(solution)/shard_map/ppermute | solution.py:474
  16.3 11.3 %collective-permute-start.6 = (f32[2,32,1280]{2,1,0:T(8,128)S(1)}, f32[2,32,1280]{2,1,0:T(8,128)S(1)}, u32[]{:S(2)}, u32[]{:S(2)}) collective-permute-start(f32[2,32,1280]{2,1,0:T(8,128)S(1)} %get-tuple-element.75), channel_id=1, source_target_pairs={{0,2},{1,3},{2,0},{3,1},{4,6},{5,7},{6,4},{7,5},{8,10},{9,11},{10,... | collective-permute-start | bytes 983048 | tf_op jit(solution)/shard_map/ppermute | solution.py:474
  19.2 17.3 %collective-permute-start.2 = (f32[2,32,1280]{2,1,0:T(8,128)S(1)}, f32[2,32,1280]{2,1,0:T(8,128)S(1)}, u32[]{:S(2)}, u32[]{:S(2)}) collective-permute-start(f32[2,32,1280]{2,1,0:T(8,128)S(1)} %get-tuple-element.68), channel_id=1, source_target_pairs={{0,2},{1,3},{2,0},{3,1},{4,6},{5,7},{6,4},{7,5},{8,10},{9,11},{10,... | collective-permute-start | bytes 983048 | tf_op jit(solution)/shard_map/ppermute | solution.py:474
  19.3 15.2 %collective-permute-start.4 = (f32[1,2560]{1,0:T(1,128)S(1)}, f32[1,2560]{1,0:T(1,128)S(1)}, u32[]{:S(2)}, u32[]{:S(2)}) collective-permute-start(f32[1,2560]{1,0:T(1,128)S(1)} %get-tuple-element.71.own_ref.refs_6_), channel_id=1, source_target_pairs={{0,2},{1,3},{2,0},{3,1},{4,6},{5,7},{6,4},{7,5},{8,10},{9,11},{10,... | collective-permute-start | bytes 30728 | tf_op jit(solution)/shard_map/ppermute | solution.py:474
  27.4 39.1 %copy-start.23 = (f32[512,128]{1,0:T(8,128)}, f32[512,128]{1,0:T(8,128)S(1)}, u32[]{:S(2)}) copy-start(f32[512,128]{1,0:T(8,128)S(1)} %get-tuple-element.102.dkey_in) | copy-start | bytes 786436
  27.4 40.1 %copy-start.5 = (bf16[512,512]{1,0:T(8,128)(2,1)}, bf16[512,512]{1,0:T(8,128)(2,1)S(1)}, u32[]{:S(2)}) copy-start(bf16[512,512]{1,0:T(8,128)(2,1)S(1)} %get-tuple-element.92.scoret_ref) | copy-start | bytes 1572868
  34.6 7.2 %collective-permute-start.12 = (f32[32,1280]{1,0:T(8,128)S(1)}, f32[32,1280]{1,0:T(8,128)S(1)}, u32[]{:S(2)}, u32[]{:S(2)}) collective-permute-start(f32[32,1280]{1,0:T(8,128)S(1)} %get-tuple-element.93), channel_id=1, source_target_pairs={{0,4},{1,5},{2,6},{3,7},{4,0},{5,1},{6,2},{7,3},{8,12},{9,13},{10,... | collective-permute-start | bytes 491528 | tf_op jit(solution)/shard_map/ppermute | solution.py:614
  36.6 7.5 %collective-permute-start.5 = (f32[32,1280]{1,0:T(8,128)S(1)}, f32[32,1280]{1,0:T(8,128)S(1)}, u32[]{:S(2)}, u32[]{:S(2)}) collective-permute-start(f32[32,1280]{1,0:T(8,128)S(1)} %get-tuple-element.72), channel_id=1, source_target_pairs={{0,4},{1,5},{2,6},{3,7},{4,0},{5,1},{6,2},{7,3},{8,12},{9,13},{10,... | collective-permute-start | bytes 491528 | tf_op jit(solution)/shard_map/ppermute | solution.py:614
  41.9 15.4 %collective-permute-start.14 = (f32[32,1280]{1,0:T(8,128)S(1)}, f32[32,1280]{1,0:T(8,128)S(1)}, u32[]{:S(2)}, u32[]{:S(2)}) collective-permute-start(f32[32,1280]{1,0:T(8,128)S(1)} %get-tuple-element.95), channel_id=1, source_target_pairs={{4,12},{5,13},{6,14},{7,15},{8,0},{9,1},{10,2},{11,3},{20,28},{21,... | collective-permute-start | bytes 491528 | tf_op jit(solution)/shard_map/ppermute | solution.py:614
  43.2 14.1 %collective-permute-start.13 = (f32[32,1280]{1,0:T(8,128)S(1)}, f32[32,1280]{1,0:T(8,128)S(1)}, u32[]{:S(2)}, u32[]{:S(2)}) collective-permute-start(f32[32,1280]{1,0:T(8,128)S(1)} %get-tuple-element.95), channel_id=1, source_target_pairs={{4,8},{5,9},{6,10},{7,11},{8,4},{9,5},{10,6},{11,7},{20,24},{21,25... | collective-permute-start | bytes 491528 | tf_op jit(solution)/shard_map/ppermute | solution.py:614
  44.2 14.8 %collective-permute-start.8 = (f32[32,1280]{1,0:T(8,128)S(1)}, f32[32,1280]{1,0:T(8,128)S(1)}, u32[]{:S(2)}, u32[]{:S(2)}) collective-permute-start(f32[32,1280]{1,0:T(8,128)S(1)} %get-tuple-element.83), channel_id=1, source_target_pairs={{4,12},{5,13},{6,14},{7,15},{8,0},{9,1},{10,2},{11,3},{20,28},{21,... | collective-permute-start | bytes 491528 | tf_op jit(solution)/shard_map/ppermute | solution.py:614
  45.5 13.5 %collective-permute-start.7 = (f32[32,1280]{1,0:T(8,128)S(1)}, f32[32,1280]{1,0:T(8,128)S(1)}, u32[]{:S(2)}, u32[]{:S(2)}) collective-permute-start(f32[32,1280]{1,0:T(8,128)S(1)} %get-tuple-element.83), channel_id=1, source_target_pairs={{4,8},{5,9},{6,10},{7,11},{8,4},{9,5},{10,6},{11,7},{20,24},{21,25... | collective-permute-start | bytes 491528 | tf_op jit(solution)/shard_map/ppermute | solution.py:614
  46.2 11.1 %collective-permute-start.9 = (f32[1,2560]{1,0:T(1,128)S(1)}, f32[1,2560]{1,0:T(1,128)S(1)}, u32[]{:S(2)}, u32[]{:S(2)}) collective-permute-start(f32[1,2560]{1,0:T(1,128)S(1)} %get-tuple-element.82.refs_2_), channel_id=1, source_target_pairs={{0,4},{1,5},{2,6},{3,7},{4,0},{5,1},{6,2},{7,3},{8,12},{9,13},{10,... | collective-permute-start | bytes 30728 | tf_op jit(solution)/shard_map/ppermute | solution.py:474
  57.4 9.1 %collective-permute-start.15 = (f32[2,32,1280]{2,1,0:T(8,128)S(1)}, f32[2,32,1280]{2,1,0:T(8,128)S(1)}, u32[]{:S(2)}, u32[]{:S(2)}) collective-permute-start(f32[2,32,1280]{2,1,0:T(8,128)S(1)} %get-tuple-element.97), channel_id=1, source_target_pairs={{0,2},{1,3},{2,0},{3,1},{4,6},{5,7},{6,4},{7,5},{8,10},{9,11},{10,... | collective-permute-start | bytes 983048 | tf_op jit(solution)/shard_map/ppermute | solution.py:474
  59.0 13.1 %copy-start.27 = (f32[40]{0:T(128)S(1)}, f32[40]{0:T(128)}, u32[]{:S(2)}) copy-start(f32[40]{0:T(128)} %param.13) | copy-start | bytes 484
  59.0 14.6 %copy-start.8 = (f32[512,40]{0,1:T(8,128)S(1)}, f32[512,40]{0,1:T(8,128)}, u32[]{:S(2)}) copy-start(f32[512,40]{0,1:T(8,128)} %param.9) | copy-start | bytes 245764
  59.1 10.9 %collective-permute-start.10 = (f32[2,32,1280]{2,1,0:T(8,128)S(1)}, f32[2,32,1280]{2,1,0:T(8,128)S(1)}, u32[]{:S(2)}, u32[]{:S(2)}) collective-permute-start(f32[2,32,1280]{2,1,0:T(8,128)S(1)} %get-tuple-element.85), channel_id=1, source_target_pairs={{0,2},{1,3},{2,0},{3,1},{4,6},{5,7},{6,4},{7,5},{8,10},{9,11},{10,... | collective-permute-start | bytes 983048 | tf_op jit(solution)/shard_map/ppermute | solution.py:474
  68.3 5.2 %collective-permute-start.16 = (f32[2,2,32,1280]{3,2,1,0:T(8,128)}, f32[2,2,32,1280]{3,2,1,0:T(8,128)}, u32[]{:S(2)}, u32[]{:S(2)}) collective-permute-start(f32[2,2,32,1280]{3,2,1,0:T(8,128)} %get-tuple-element.99), channel_id=1, source_target_pairs={{0,1},{1,0},{2,3},{3,2},{4,5},{5,4},{6,7},{7,6},{8,9},{9,8},{10,11... | collective-permute-start | bytes 1966088 | tf_op jit(solution)/shard_map/ppermute | solution.py:474
  72.1 17.8 %collective-permute-start.11 = (f32[2,2,32,1280]{3,2,1,0:T(8,128)}, f32[2,2,32,1280]{3,2,1,0:T(8,128)}, u32[]{:S(2)}, u32[]{:S(2)}) collective-permute-start(f32[2,2,32,1280]{3,2,1,0:T(8,128)} %get-tuple-element.87), channel_id=1, source_target_pairs={{0,1},{1,0},{2,3},{3,2},{4,5},{5,4},{6,7},{7,6},{8,9},{9,8},{10,11... | collective-permute-start | bytes 1966088 | tf_op jit(solution)/shard_map/ppermute | solution.py:474
  73.6 1.7 %copy-start.4 = (bf16[512,2560]{1,0:T(8,128)(2,1)S(1)}, bf16[512,2560]{1,0:T(8,128)(2,1)}, u32[]{:S(2)}) copy-start(bf16[512,2560]{1,0:T(8,128)(2,1)} %cot_ref.9) | copy-start | bytes 7864324
  76.3 1.1 %copy-start.12 = (f32[2,2,32,1280]{3,2,1,0:T(8,128)S(1)}, f32[2,2,32,1280]{3,2,1,0:T(8,128)}, u32[]{:S(2)}) copy-start(f32[2,2,32,1280]{3,2,1,0:T(8,128)} %copy-done.11) | copy-start | bytes 1966084
  81.1 8.7 %copy-start.10 = (f32[2,2,32,1280]{3,2,1,0:T(8,128)S(1)}, f32[2,2,32,1280]{3,2,1,0:T(8,128)}, u32[]{:S(2)}) copy-start(f32[2,2,32,1280]{3,2,1,0:T(8,128)} %copy-done.9) | copy-start | bytes 1966084
  (13 other events, 11.2 us)

commit v3 on v2

v3 whole, which is shorter than its diff:
```python
import functools

import jax
import jax.numpy as jnp
from jax import lax
from jax.experimental import pallas as pl
from jax.experimental.pallas import tpu as pltpu
from jax.sharding import PartitionSpec as P

CHUNKS = 2
TILE = 640
VMEM_BYTES = 28 * 1024 * 1024

F32 = jnp.float32
BF16 = jnp.bfloat16


def dot_nn(left, right):
    return lax.dot_general(left, right, (((1,), (0,)), ((), ())), preferred_element_type=F32)


def dot_nt(left, right):
    return lax.dot_general(left, right, (((1,), (1,)), ((), ())), preferred_element_type=F32)


def halves(value):
    high = value.astype(BF16)
    return high, (value - high.astype(F32)).astype(BF16)


def sum_dot(matrix, value):
    first = value.astype(BF16)
    rest = value - first.astype(F32)
    second = rest.astype(BF16)
    third = (rest - second.astype(F32)).astype(BF16)
    return dot_nn(matrix, first) + dot_nn(matrix, second) + dot_nn(matrix, third)


def head_spread(depth, offset, head_count, first_column, columns, head_size):
    row = lax.broadcasted_iota(jnp.int32, (depth, columns), 0) - offset
    held = (row >= 0) & (row < 2 * head_count)
    row = jnp.where(row >= head_count, row - head_count, row)
    column = lax.broadcasted_iota(jnp.int32, (depth, columns), 1) + first_column
    inside = column - row * head_size
    return jnp.where(held & (inside >= 0) & (inside < head_size), 1.0, 0.0).astype(BF16)


def head_collect(head_count, first_column, columns, head_size):
    row = lax.broadcasted_iota(jnp.int32, (columns, head_count), 0) + first_column
    column = lax.broadcasted_iota(jnp.int32, (columns, head_count), 1)
    offset = row - column * head_size
    return jnp.where((offset >= 0) & (offset < head_size), 1.0, 0.0).astype(BF16)


def triangle(rows, lower):
    first = lax.broadcasted_iota(jnp.int32, (rows, rows), 0)
    second = lax.broadcasted_iota(jnp.int32, (rows, rows), 1)
    return (first >= second) if lower else (first <= second)


def start_counts(starts_row):
    rows = starts_row.shape[1]
    flags = starts_row.astype(F32)
    column = jnp.sum(jnp.where(triangle(rows, True), flags, 0.0), axis=1, keepdims=True)
    spread = jnp.broadcast_to(flags, (8, rows)).astype(BF16)
    row = dot_nn(spread, triangle(rows, False).astype(F32).astype(BF16))[:1]
    return column, row


def softplus(value):
    return jnp.maximum(value, 0.0) + jnp.log1p(jnp.exp(-jnp.abs(value)))


def sum_dot_left(value, matrix):
    first = value.astype(BF16)
    rest = value - first.astype(F32)
    second = rest.astype(BF16)
    third = (rest - second.astype(F32)).astype(BF16)
    return dot_nn(first, matrix) + dot_nn(second, matrix) + dot_nn(third, matrix)


def fetch(pairs, sems):
    copies = [
        pltpu.make_async_copy(source, target, sems.at[i])
        for i, (source, target) in enumerate(pairs)
    ]
    for copy in copies:
        copy.start()
    return copies


def prep_kernel(
    head_size, raw_hbm, rate_hbm, skip_hbm, starts_hbm, query_hbm, key_hbm,
    heads_ref, maps_ref, turned_ref, rows_ref, decay_ref,
    raw_ref, rate_ref, skip_ref, starts_ref, query_ref, key_ref, sems,
):
    copies = fetch(
        [
            (raw_hbm, raw_ref), (rate_hbm, rate_ref), (skip_hbm, skip_ref),
            (starts_hbm, starts_ref), (query_hbm, query_ref), (key_hbm, key_ref),
        ],
        sems,
    )
    head_count, rows = raw_ref.shape
    upper = triangle(rows, False).astype(F32).astype(BF16)
    for copy in copies:
        copy.wait()
    step = softplus(raw_ref[...])
    rate = jnp.broadcast_to(rate_ref[...], (8, head_count)).T[:, :1]
    cumulative = sum_dot_left(-step * rate, upper)
    count, _ = start_counts(starts_ref[...])
    in_lead = count == 0.0
    in_tail = count == count[rows - 1 :, :]
    state_size = query_ref.shape[1]
    lead = jnp.where(in_lead, query_ref[...].astype(F32), 0.0)
    tail = jnp.where(in_tail, key_ref[...].astype(F32), 0.0)
    maps_ref[:, :state_size] = lead.astype(BF16)
    maps_ref[:, state_size:] = tail.astype(BF16)
    turned_ref[:state_size] = lead.T.astype(BF16)
    turned_ref[state_size:] = tail.T.astype(BF16)
    fall = jnp.exp(cumulative).T
    grow = (jnp.exp(-cumulative) * step).T
    heads_ref[...] = jnp.concatenate(
        halves(fall)
        + halves(grow)
        + (
            jnp.where(in_lead, 1.0, 0.0).astype(BF16),
            jnp.where(in_tail, 1.0, 0.0).astype(BF16),
        ),
        axis=1,
    )
    channels = rows_ref.shape[1]
    spread = head_spread(2 * head_count, 0, head_count, 0, channels, head_size)

    def wide(value):
        return dot_nn(
            jnp.concatenate(halves(jnp.broadcast_to(value, (8, head_count))), axis=1), spread
        )[:1]

    last = wide(fall[rows - 1 :, :])
    decay = jnp.where(count[rows - 1 :, :] == 0.0, last, 0.0)
    rows_ref[0:1, :] = decay
    rows_ref[1:2, :] = last
    rows_ref[2:3, :] = wide(skip_ref[...])
    decay_ref[...] = decay


def place():
    index = lax.axis_index("seq")
    return (index & 1) == 0, (index & 2) == 0, index >> 2


def joined(first, own_decay, other_decay, own, came):
    one = jnp.ones_like(own_decay)
    forward = (
        jnp.where(first, other_decay, one) * own[0] + jnp.where(first, one, own_decay) * came[0]
    )
    backward = (
        jnp.where(first, one, other_decay) * own[1] + jnp.where(first, own_decay, one) * came[1]
    )
    return forward, backward


def split_pair(first, own_decay, other_decay, own, came, entering, leaving, put_own, put_other):
    @pl.when(first)
    def _():
        put_own(0, entering)
        put_other(0, own_decay * entering + own[0])
        put_other(1, leaving)
        put_own(1, other_decay * leaving + came[1])

    @pl.when(jnp.logical_not(first))
    def _():
        put_other(0, entering)
        put_own(0, other_decay * entering + came[0])
        put_own(1, leaving)
        put_other(1, own_decay * leaving + own[1])


def chip_kernel(
    columns, kept_ref, came_ref, own_ref, other_ref, *refs,
):
    if len(refs) > 2:
        chip_ref, chip_other_ref, sent_ref, side_ref, plane_ref = refs
        plane_ref[...] = chip_ref[...] * chip_other_ref[...]
    else:
        sent_ref, side_ref = refs
    first, _, _ = place()
    forward, backward = joined(
        first, own_ref[:, columns], other_ref[:, columns], kept_ref, came_ref
    )
    for chain, value in enumerate((forward, backward)):
        sent_ref[chain] = value[0]
        side_ref[chain] = value[1]


def plane_kernel(columns, kept_ref, came_ref, own_ref, other_ref, pay_ref, both_ref):
    _, first, plane = place()
    forward, backward = joined(
        first, own_ref[:, columns], other_ref[:, columns], kept_ref, came_ref
    )
    both_ref[0] = forward
    both_ref[1] = backward
    pay_ref[...] = jnp.where((plane & 1) == 1, backward, forward)


def absorb(columns, level, plane, taken_refs, others, enter_ref):
    upper = ((plane >> level) & 1) == 1
    taken = taken_refs[0][...]
    for ref in taken_refs[1:]:
        taken = taken + ref[...]
    if level == 0:
        zero = jnp.zeros_like(taken)
        return jnp.where(upper, taken, zero), jnp.where(upper, zero, taken)
    before = after = None
    for lower, ref in enumerate(others[:level]):
        other = ref[:, columns]
        above = ((plane >> lower) & 1) == 1
        one = jnp.ones_like(other)
        first = jnp.where(above, other, one)
        second = jnp.where(above, one, other)
        before = first if before is None else before * first
        after = second if after is None else after * second
    zero = jnp.zeros_like(before)
    return (
        enter_ref[0] + jnp.where(upper, before, zero) * taken,
        enter_ref[1] + jnp.where(upper, zero, after) * taken,
    )


def level_kernel(columns, level, taken_count, *refs):
    taken, refs = refs[:taken_count], refs[taken_count:]
    others, refs = refs[:level], refs[level:]
    enter_ref = None
    if level:
        enter_ref, refs = refs[0], refs[1:]
    both_ref, decay_ref, pay_ref, next_ref = refs
    _, _, plane = place()
    entering, leaving = absorb(columns, level, plane, taken, others, enter_ref)
    next_ref[0] = entering
    next_ref[1] = leaving
    upper = ((plane >> (level + 1)) & 1) == 1
    decay = decay_ref[:, columns]

    @pl.when(upper)
    def _():
        pay_ref[...] = decay * leaving + both_ref[1]

    @pl.when(jnp.logical_not(upper))
    def _():
        pay_ref[...] = decay * entering + both_ref[0]


def top_kernel(columns, level, taken_count, *refs):
    taken, refs = refs[:taken_count], refs[taken_count:]
    others, refs = refs[:level], refs[level:]
    enter_ref = None
    if level:
        enter_ref, refs = refs[0], refs[1:]
    kept_ref, came_ref, own_ref, other_ref, theirs_ref, mine_ref = refs
    _, first, plane = place()
    entering, leaving = absorb(columns, level, plane, taken, others, enter_ref)

    def put_own(chain, value):
        mine_ref[chain] = value

    def put_other(chain, value):
        theirs_ref[chain] = value

    split_pair(
        first, own_ref[:, columns], other_ref[:, columns], kept_ref, came_ref, entering, leaving,
        put_own, put_other,
    )


def device_kernel(
    columns, back_ref, mine_ref, kept_ref, came_ref, own_ref, other_ref, give_ref, stay_ref
):
    first, _, _ = place()
    for slot, source in enumerate((back_ref, mine_ref)):

        def put_own(chain, value, slot=slot):
            stay_ref[chain, slot] = value

        def put_other(chain, value, slot=slot):
            give_ref[chain, slot] = value

        split_pair(
            first, own_ref[:, columns], other_ref[:, columns], kept_ref.at[:, slot],
            came_ref.at[:, slot], source[0], source[1], put_own, put_other,
        )


def scale_columns(heads_ref, head_count, head_size, first, columns):
    heads = heads_ref[...]
    depth = heads.shape[1]
    args = (head_count, first, columns, head_size)
    fall = dot_nn(heads, head_spread(depth, 0, *args))
    grow = dot_nn(heads, head_spread(depth, 2 * head_count, *args))
    return fall, grow


def load_tiles(in_hbm, cot_hbm, in_ref, cot_ref, sems, first, tile):
    found = []
    for i in range(in_ref.shape[1] // tile):
        here = pl.ds(first + i * tile, tile)
        there = pl.ds(i * tile, tile)
        pair = []
        for j, (source, target) in enumerate(((in_hbm, in_ref), (cot_hbm, cot_ref))):
            copy = pltpu.make_async_copy(
                source.at[:, here], target.at[:, there], sems.at[2 * i + j]
            )
            copy.start()
            pair.append(copy)
        found.append(pair)
    return found


def states_kernel(
    head_count, head_size, first_column, tile, in_hbm, cot_hbm, heads_ref, turned_ref, rows_ref,
    send_ref, keep_ref, in_ref, cot_ref, sems,
):
    copies = load_tiles(in_hbm, cot_hbm, in_ref, cot_ref, sems, first_column, tile)
    low, mid, _ = place()
    state_size = turned_ref.shape[0] // 2
    for i, pair in enumerate(copies):
        here = slice(i * tile, (i + 1) * tile)
        there = slice(first_column + i * tile, first_column + (i + 1) * tile)
        fall, grow = scale_columns(heads_ref, head_count, head_size, there.start, tile)
        for copy in pair:
            copy.wait()
        grown = (grow * in_ref[:, here].astype(F32)).astype(BF16)
        fallen = (fall * cot_ref[:, here].astype(F32)).astype(BF16)
        state = dot_nn(turned_ref[state_size:], grown) * rows_ref[1:2, there]
        direct = dot_nn(turned_ref[:state_size], fallen)
        half = state_size // 2
        quarter = half // 2
        for chain, value in enumerate((state, direct)):
            sent = jnp.where(low, value[half:], value[:half])
            kept = jnp.where(low, value[:half], value[half:])
            for ref, part in ((send_ref, sent), (keep_ref, kept)):
                ref[chain, 0, :, here] = jnp.where(mid, part[quarter:], part[:quarter])
                ref[chain, 1, :, here] = jnp.where(mid, part[:quarter], part[quarter:])


def local_kernel(
    head_count, head_size, first_column, tile, initial, final, in_hbm, cot_hbm, heads_ref, rows_ref,
    starts_ref, query_ref, key_ref, *refs,
):
    if not initial:
        score_ref, scoret_ref, total_in, refs = *refs[:3], refs[3:]
    (out_ref, din_ref, grown_ref, fallen_ref, sums_ref), refs = refs[:5], refs[5:]
    if initial:
        (score_ref, scoret_ref), refs = refs[:2], refs[2:]
    (total_out, *key_out), (in_ref, cot_ref, sems) = refs[:-3], refs[-3:]
    copies = load_tiles(in_hbm, cot_hbm, in_ref, cot_ref, sems, first_column, tile)
    rows = in_ref.shape[0]
    if initial or final:
        column, row = start_counts(starts_ref[...])
        same = column == row
        allowed = same & triangle(rows, True)
    if initial:
        score_ref[...] = jnp.where(allowed, dot_nt(query_ref[...], key_ref[...]), 0.0).astype(BF16)
        scoret_ref[...] = jnp.where(
            same & triangle(rows, False), dot_nt(key_ref[...], query_ref[...]), 0.0
        ).astype(BF16)
    total = None if initial else total_in[...]
    rise = sink = None
    for i, pair in enumerate(copies):
        here = slice(i * tile, (i + 1) * tile)
        there = slice(first_column + i * tile, first_column + (i + 1) * tile)
        fall, grow = scale_columns(heads_ref, head_count, head_size, there.start, tile)
        collect = head_collect(head_count, there.start, tile, head_size)
        for copy in pair:
            copy.wait()
        in_wide = in_ref[:, here].astype(F32)
        cot_wide = cot_ref[:, here].astype(F32)
        skip = rows_ref[2:3, there]
        grown = (grow * in_wide).astype(BF16)
        fallen = (fall * cot_wide).astype(BF16)
        grown_ref[:, here] = grown
        fallen_ref[:, here] = fallen
        product = dot_nt(fallen, grown)
        total = product if total is None else total + product
        produced = dot_nn(score_ref[...], grown)
        out_ref[:, here] = fall * produced + skip * in_wide
        rise_now = dot_nn((fallen.astype(F32) * produced).astype(BF16), collect)
        pulled = dot_nn(scoret_ref[...], fallen)
        din_ref[:, here] = grow * pulled + skip * cot_wide
        sink_now = dot_nn((grown.astype(F32) * pulled).astype(BF16), collect)
        rise = rise_now if rise is None else rise + rise_now
        sink = sink_now if sink is None else sink + sink_now
    sums_ref[0] = rise
    sums_ref[1] = sink
    if final:
        grads = jnp.where(allowed, total, 0.0)
        total_out[...] = dot_nn(grads.astype(BF16), key_ref[...])
        key_out[0][...] = dot_nn(grads.T.astype(BF16), query_ref[...])
    else:
        total_out[...] = total


def arranged(low, mid, took_ref, own_ref, chain):
    parts = []
    for ref in (own_ref, took_ref):
        first = jnp.where(mid, ref[chain, 1], ref[chain, 0])
        second = jnp.where(mid, ref[chain, 0], ref[chain, 1])
        parts.append(jnp.concatenate([first, second], axis=0))
    own, took = parts
    return jnp.concatenate([jnp.where(low, own, took), jnp.where(low, took, own)], axis=0)


def finish_kernel(
    head_count, head_size, first_column, steps, prior, local_out_ref, local_din_ref, grown_ref,
    fallen_ref, took_ref, own_ref, rows_ref, heads_ref, maps_ref, sums_ref, raw_ref, rate_ref,
    dquery_in, dkey_in, *refs,
):
    if prior:
        draw_in, refs = refs[0], refs[3:]
    out_ref, din_ref, dquery_ref, dkey_ref, draw_ref, rise_ref, sink_ref, edge_ref, dmap_ref = refs
    rows, columns = grown_ref.shape
    state_size = maps_ref.shape[1] // 2
    step = pl.program_id(0)
    start_column = first_column + step * columns
    low, mid, _ = place()
    entering = arranged(low, mid, took_ref, own_ref, 0)
    leaving = arranged(low, mid, took_ref, own_ref, 1)
    fall, grow = scale_columns(heads_ref, head_count, head_size, start_column, columns)
    grown = grown_ref[...]
    fallen = fallen_ref[...]
    entering_bf = entering.astype(BF16)
    leaving_bf = (leaving * rows_ref[1:2, :]).astype(BF16)
    reached = dot_nn(maps_ref[:, :state_size], entering_bf)
    behind = dot_nn(maps_ref[:, state_size:], leaving_bf)
    out_ref[...] = (local_out_ref[...] + fall * reached).astype(BF16)
    din_ref[...] = (local_din_ref[...] + grow * behind).astype(BF16)
    collect = head_collect(head_count, start_column, columns, head_size)
    rise = dot_nn((fallen.astype(F32) * reached).astype(BF16), collect)
    pulled = grown.astype(F32) * behind
    sink = dot_nn(pulled.astype(BF16), collect)
    edge_row = jnp.sum(pulled, axis=0, keepdims=True) + rows_ref[0:1, :] * jnp.sum(
        entering * leaving, axis=0, keepdims=True
    )
    high, rest = halves(jnp.broadcast_to(edge_row, (8, columns)))
    edge = dot_nn(high, collect) + dot_nn(rest, collect)
    dlead = dot_nt(fallen, entering_bf)
    dtail = dot_nt(grown, leaving_bf)

    @pl.when(step == 0)
    def _():
        rise_ref[...] = sums_ref[0] + rise
        sink_ref[...] = sums_ref[1] + sink
        edge_ref[...] = edge
        dmap_ref[:, :state_size] = dlead
        dmap_ref[:, state_size:] = dtail

    @pl.when(step > 0)
    def _():
        rise_ref[...] += rise
        sink_ref[...] += sink
        edge_ref[...] += edge
        dmap_ref[:, :state_size] += dlead
        dmap_ref[:, state_size:] += dtail

    @pl.when(step == steps - 1)
    def _():
        in_lead = heads_ref[:, 4 * head_count : 4 * head_count + 1].astype(F32) > 0.5
        in_tail = heads_ref[:, 4 * head_count + 1 : 4 * head_count + 2].astype(F32) > 0.5
        dquery_ref[...] = (
            dquery_in[...] + jnp.where(in_lead, dmap_ref[:, :state_size], 0.0)
        ).astype(dquery_ref.dtype)
        dkey_ref[...] = (
            dkey_in[...] + jnp.where(in_tail, dmap_ref[:, state_size:], 0.0)
        ).astype(dkey_ref.dtype)
        lower = triangle(rows, True).astype(F32).astype(BF16)
        sink_turned = sink_ref[...].T
        later = sum_dot_left(rise_ref[...].T - sink_turned, lower) + edge_ref[...].T[:, :1]
        raw = raw_ref[...]
        rate = jnp.broadcast_to(rate_ref[...], (8, head_count)).T[:, :1]
        draw = (sink_turned / softplus(raw) - rate * later) / (1.0 + jnp.exp(-raw))
        draw_ref[...] = draw_in[...] + draw if prior else draw


def whole(shape):
    return pl.BlockSpec(shape, lambda i, *_: (0,) * len(shape))


def params():
    return pltpu.CompilerParams(vmem_limit_bytes=VMEM_BYTES)


def cost(flops, count):
    return pl.CostEstimate(flops=flops, bytes_accessed=count, transcendentals=0)


HBM = pl.BlockSpec(memory_space=pltpu.HBM)
NEAR = pl.BlockSpec(memory_space=pltpu.VMEM)


def local(inputs, raw_steps, input_map, output_map, decay_rates, skip_gain, starts, cotangent):
    rows, channels = inputs.shape
    head_count = decay_rates.shape[0]
    head_size = channels // head_count
    state_size = input_map.shape[1]
    width = channels // CHUNKS
    tiles = width // TILE
    quarter = state_size // 4

    size = lax.axis_size("seq")
    planes = size // 4
    levels = planes.bit_length() - 1
    starts_row = starts.reshape(1, rows)
    rate_row = decay_rates.reshape(1, head_count)
    skip_heads = skip_gain.reshape(1, head_count)
    raw_turned = raw_steps.T

    def far(value):
        return pltpu.with_memory_space_constraint(value, pltpu.HBM)

    def shape(dims, kind=F32):
        return jax.ShapeDtypeStruct(dims, kind)

    heads, maps, turned, wide_rows, decay = pl.pallas_call(
        functools.partial(prep_kernel, head_size),
        out_shape=(
            shape((rows, 4 * head_count + 2), BF16),
            shape((rows, 2 * state_size), BF16),
            shape((2 * state_size, rows), BF16),
            shape((8, channels)),
            shape((1, channels)),
        ),
        in_specs=[HBM] * 6,
        scratch_shapes=[
            pltpu.VMEM((head_count, rows), F32), pltpu.VMEM((1, head_count), F32),
            pltpu.VMEM((1, head_count), F32), pltpu.VMEM((1, rows), jnp.int32),
            pltpu.VMEM((rows, state_size), BF16), pltpu.VMEM((rows, state_size), BF16),
            pltpu.SemaphoreType.DMA((6,)),
        ],
        compiler_params=params(),
        name="prep",
    )(*(far(v) for v in (raw_turned, rate_row, skip_heads, starts_row, output_map, input_map)))

    flat_shape = shape((quarter, width))
    pair_shape = shape((2, quarter, width))
    four_shape = shape((2, 2, quarter, width))
    row_shape = shape((1, channels))
    tile_scratch = [
        pltpu.VMEM((rows, width), BF16), pltpu.VMEM((rows, width), BF16),
        pltpu.SemaphoreType.DMA((2 * tiles,)),
    ]

    def device_states(chunk, rows_value):
        return pl.pallas_call(
            functools.partial(states_kernel, head_count, head_size, chunk * width, TILE),
            out_shape=(four_shape, four_shape),
            in_specs=[HBM, HBM, NEAR, NEAR, NEAR],
            scratch_shapes=tile_scratch,
            compiler_params=params(),
            cost_estimate=cost(1000, 1000),
            name="states",
        )(far(inputs), far(cotangent), heads, turned, rows_value)

    def swap(value, bit):
        return lax.ppermute(value, "seq", [(i, i ^ bit) for i in range(size)])

    def level_perms(level):
        span = 1 << level
        perms = []
        for shift in range(span):
            pairs = []
            for base in range(0, planes, 2 * span):
                pairs.append((base + span - 1, base + span + shift))
                pairs.append((base + span, base + span - 1 - shift))
            perms.append([(4 * a + r, 4 * b + r) for a, b in pairs for r in range(4)])
        return perms

    def small(kernel, out_shape, name, *operands):
        return pl.pallas_call(
            kernel, out_shape=out_shape, compiler_params=params(), name=name
        )(*operands)

    def block_parts(chunk, heads_value, sofar):
        initial = chunk == 0
        final = chunk == CHUNKS - 1
        square = (rows, rows)
        block = (rows, width)
        outs = [
            shape(block), shape(block), shape(block, BF16), shape(block, BF16),
            shape((2, rows, head_count)),
        ]
        if initial:
            outs += [shape(square, BF16), shape(square, BF16)]
        outs += [shape((rows, state_size))] * 2 if final else [shape(square)]
        operands = [
            far(inputs), far(cotangent), heads_value, wide_rows, starts_row, output_map, input_map,
        ] + list(sofar)
        made = pl.pallas_call(
            functools.partial(
                local_kernel, head_count, head_size, chunk * width, TILE, initial, final
            ),
            out_shape=tuple(outs),
            in_specs=[HBM, HBM] + [NEAR] * (len(operands) - 2),
            scratch_shapes=tile_scratch,
            compiler_params=params(),
            cost_estimate=cost(1000, 1000),
            name="block",
        )(*operands)
        if final:
            return made[:5], tuple(made[-2:])
        if initial:
            return made[:5], tuple(made[5:])
        return made[:5], (sofar[0], sofar[1], made[5])

    def finish(chunk, block, took, own, grads, prior):
        tile = pl.BlockSpec((rows, TILE), lambda i: (0, i))
        placed = pl.BlockSpec((rows, TILE), lambda i: (0, chunk * tiles + i))
        row = pl.BlockSpec((8, TILE), lambda i: (0, chunk * tiles + i))
        part = pl.BlockSpec((2, 2, quarter, TILE), lambda i: (0, 0, 0, i))
        flat = (rows, state_size)
        by_head = (head_count, rows)
        operands = [
            *block[:4], took, own, wide_rows, heads, maps, block[4], raw_turned, rate_row, *grads,
        ]
        in_specs = [
            tile, tile, tile, tile, part, part, row, whole(heads.shape), whole(maps.shape),
            whole(block[4].shape), whole(by_head), whole(rate_row.shape), whole(flat), whole(flat),
        ]
        aliases = {}
        if prior:
            operands += list(prior)
            in_specs += [whole(by_head)] + [pl.BlockSpec(memory_space=pl.ANY)] * 2
            aliases = {15: 0, 16: 1}
        kind = BF16 if chunk == CHUNKS - 1 else F32
        return pl.pallas_call(
            functools.partial(
                finish_kernel, head_count, head_size, chunk * width, tiles, bool(prior)
            ),
            out_shape=(
                shape((rows, channels), BF16), shape((rows, channels), BF16),
                shape(flat, kind), shape(flat, kind), shape(by_head),
            ),
            grid=(tiles,),
            in_specs=in_specs,
            out_specs=(placed, placed, whole(flat), whole(flat), whole(by_head)),
            scratch_shapes=[
                pltpu.VMEM((rows, head_count), F32), pltpu.VMEM((rows, head_count), F32),
                pltpu.VMEM((8, head_count), F32), pltpu.VMEM((rows, 2 * state_size), F32),
            ],
            input_output_aliases=aliases,
            compiler_params=params(),
            cost_estimate=cost(1000, 1000),
            name="finish",
        )(*operands)

    every = range(CHUNKS)
    span = [slice(chunk * width, (chunk + 1) * width) for chunk in every]
    tie = lax.optimization_barrier

    sent, kept, came = [None] * CHUNKS, [None] * CHUNKS, [None] * CHUNKS
    decay_other = swap(decay, 1)
    rows_now = wide_rows
    for k in every:
        sent[k], kept[k] = device_states(k, rows_now)
        came[k] = swap(sent[k], 1)
        if k == 0:
            ready = tie((decay_other, sent[0]))
            chip_decay = decay * ready[0]
            chip_other = swap(chip_decay, 2)
            rows_now = tie((wide_rows, chip_decay))[0]

    order = [sent[-1]]

    def follow(value):
        return tie((value, order[0]))[0]

    side_sent, side_kept, side_came = [None] * CHUNKS, [None] * CHUNKS, [None] * CHUNKS
    for k in every:
        made = small(
            functools.partial(chip_kernel, span[k]),
            (pair_shape, pair_shape) + ((row_shape,) if k == 0 else ()),
            "chip", follow(kept[k]), came[k], decay, decay_other,
            *((chip_decay, chip_other) if k == 0 else ()),
        )
        side_sent[k], side_kept[k] = made[:2]
        order[0] = side_sent[k]
        if k == 0:
            plane_decay = group = made[2]
            others = []
            for level in range(levels - 1):
                other = swap(group, 4 << level)
                others.append(other)
                group = group * other
        side_came[k] = swap(side_sent[k], 2)

    blocks = [None] * CHUNKS
    blocks[0], sofar = block_parts(0, follow(heads), ())
    order[0] = sofar[0]

    pay, both = [None] * CHUNKS, [None] * CHUNKS
    taken, enter = [None] * CHUNKS, [None] * CHUNKS
    for k in every:
        pay[k], both[k] = small(
            functools.partial(plane_kernel, span[k]), (flat_shape, pair_shape), "plane",
            follow(side_kept[k]), side_came[k], chip_decay, chip_other,
        )
        order[0] = pay[k]
        taken[k] = [lax.ppermute(pay[k], "seq", perm) for perm in level_perms(0)]
        if k + 1 < CHUNKS:
            blocks[k + 1], sofar = block_parts(k + 1, follow(heads), sofar)
            order[0] = blocks[k + 1][4]
    for level in range(levels - 1):
        for k in every:
            operands = taken[k] + others[:level] + ([enter[k]] if level else [])
            pay[k], enter[k] = small(
                functools.partial(level_kernel, span[k], level, len(taken[k])),
                (flat_shape, pair_shape), "level", *operands, follow(both[k]), plane_decay,
            )
            order[0] = pay[k]
            taken[k] = [lax.ppermute(pay[k], "seq", perm) for perm in level_perms(level + 1)]
    back, mine = [None] * CHUNKS, [None] * CHUNKS
    for k in every:
        operands = taken[k] + others[: levels - 1] + ([enter[k]] if levels > 1 else [])
        theirs, mine[k] = small(
            functools.partial(top_kernel, span[k], levels - 1, len(taken[k])),
            (pair_shape, pair_shape), "top", *operands, follow(side_kept[k]), side_came[k],
            chip_decay, chip_other,
        )
        order[0] = theirs
        back[k] = swap(theirs, 2)
    prior = ()
    grads = sofar
    for k in every:
        give, own = small(
            functools.partial(device_kernel, span[k]), (four_shape, four_shape), "device",
            back[k], follow(mine[k]), kept[k], came[k], decay, decay_other,
        )
        took = swap(give, 1)
        out, din, dquery, dkey, draw = finish(k, blocks[k], took, own, grads, prior)
        grads = (dquery, dkey)
        order[0] = draw
        prior = (draw, out, din)
    return out, din, draw.T, dkey, dquery


def solution(mesh):
    sequence = P(("groups", "seq"), None)
    return jax.shard_map(
        local,
        mesh=mesh,
        in_specs=(
            sequence, sequence, sequence, sequence, P(), P(), P(("groups", "seq")), sequence,
        ),
        out_specs=(sequence,) * 5,
        check_vma=False,
    )
```

time: 99.5 us -> 77.3 us (0.78)
  the two profiles are of different devices: /device:TPU:0 before, /device:TPU:9 now
where the time goes in v3:
time: 77.3 us; the launch traced here: 77 us
  Pallas kernels  33.1 us (43%)
  starting transfers between devices  24.7 us (32%)
  waiting for transfers between devices  18.1 us (23%)
  between operations  0.98 us (1%)
    ppermute x11, starting transfers between devices, swap(): return lax.ppermute(value, 'seq', [(i, i ^ bit) for i in range(size)])  14.1 us
    pallas_call x2, Pallas kernels, finish(): pl.pallas_call(functools.partial(finish_kernel, head_count, head_size, ch...  13 us
    pallas_call x2, Pallas kernels, block_parts(): pl.pallas_call(functools.partial(local_kernel, head_count, head_size, chu...  11.8 us
    ppermute x11, waiting for transfers between devices, swap(): return lax.ppermute(value, 'seq', [(i, i ^ bit) for i in range(size)])  11 us
    ppermute x4, starting transfers between devices, local(): lax.ppermute(pay[k], 'seq', perm)  9.5 us
    ppermute x4, waiting for transfers between devices, local(): lax.ppermute(pay[k], 'seq', perm)  7.14 us
    pallas_call x2, Pallas kernels, device_states(): pl.pallas_call(functools.partial(states_kernel, head_count, head_size, ch...  5.23 us
    pallas_call x1, Pallas kernels, local(): pl.pallas_call(functools.partial(prep_kernel, head_size), out_shape=(shap...  2.08 us
  transfers between devices with their start and end apart: 17, of which 11 were waited for; matrix products, arithmetic and copies ran while one was open for 0% of the time, Pallas kernels for 28%

profile of v3, /device:TPU:9, one launch (start us, length us, event | category | flops | bytes accessed | tf_op | source)
XLA Modules:
  0.0 77.0 jit_solution(1663423608354542294)
XLA Ops:
  0.6 2.1 %prep.1 = (bf16[512,162]{1,0:T(8,128)(2,1)S(1)}, bf16[512,256]{1,0:T(8,128)(2,1)S(1)}, bf16[256,512]{1,0:T(8,128)(2,1)S(1)}, f32[8,2560]{1,0:T(8,128)S(1)}, f32[1,2560]{1,0:T(1,128)S(1)}) custom-call(f32[40,512]{1,0:T(8,128)} %bitcast.5, f32[1,40]{1,0:T(1,128)} %bitcast.11, f32[1,40]{1,0:T(1,128)} %bitcast.14, s32[1,512]{1,0:T(1,128)} %bitcast.8, ...), custom_call_target="tpu_custom_call" | custom-call | tf_op jit(solution)/shard_map/prep/pallas_call | solution.py:523
  2.7 2.6 %states.2 = (f32[2,2,32,1280]{3,2,1,0:T(8,128)S(1)}, f32[2,2,32,1280]{3,2,1,0:T(8,128)S(1)}) custom-call(bf16[512,2560]{1,0:T(8,128)(2,1)} %in_hbm.7, bf16[512,2560]{1,0:T(8,128)(2,1)} %cot_hbm.7, bf16[512,162]{1,0:T(8,128)(2,1)S(1)} %get-tuple-element.93.heads_ref, bf16[256,512]{1,0:T(8,128)(2,1)S(1)} %get-tuple-element.75.turned_ref, ...), custom_call_target="tpu_custom_call" | custom-call | flops 1000 | bytes 1000 | tf_op jit(solution)/shard_map/states/pallas_call | solution.py:553
  5.3 0.7 collective-permute-start.1
  6.2 1.7 %collective-permute-done.other_ref = f32[1,2560]{1,0:T(1,128)S(1)} collective-permute-done((f32[1,2560]{1,0:T(1,128)S(1)}, f32[1,2560]{1,0:T(1,128)S(1)}, u32[]{:S(2)}, u32[]{:S(2)}) %collective-permute-start) | collective-permute-done | bytes 10272 | tf_op jit(solution)/shard_map/ppermute | solution.py:564
  7.8 2.6 %states.3 = (f32[2,2,32,1280]{3,2,1,0:T(8,128)S(1)}, f32[2,2,32,1280]{3,2,1,0:T(8,128)S(1)}) custom-call(bf16[512,2560]{1,0:T(8,128)(2,1)} %in_hbm.7, bf16[512,2560]{1,0:T(8,128)(2,1)} %cot_hbm.7, bf16[512,162]{1,0:T(8,128)(2,1)S(1)} %get-tuple-element.93.heads_ref, bf16[256,512]{1,0:T(8,128)(2,1)S(1)} %get-tuple-element.75.turned_ref, ...), custom_call_target="tpu_custom_call" | custom-call | flops 1000 | bytes 1000 | tf_op jit(solution)/shard_map/states/pallas_call | solution.py:553
  10.5 0.4 collective-permute-start.3
  10.9 1.2 %collective-permute-start.2 = (f32[1,2560]{1,0:T(1,128)S(1)}, f32[1,2560]{1,0:T(1,128)S(1)}, u32[]{:S(2)}, u32[]{:S(2)}) collective-permute-start(f32[1,2560]{1,0:T(1,128)S(1)} %mul.3.refs_0_.own_ref.refs_6_), channel_id=1, source_target_pairs={{0,2},{1,3},{2,0},{3,1},{4,6},{5,7},{6,4},{7,5},{8,10},{9,11},{10,... | collective-permute-start | bytes 30728 | tf_op jit(solution)/shard_map/ppermute | solution.py:564
  12.2 1.3 %collective-permute-done.2.refs_1_.other_ref.refs_7_ = f32[1,2560]{1,0:T(1,128)S(1)} collective-permute-done((f32[1,2560]{1,0:T(1,128)S(1)}, f32[1,2560]{1,0:T(1,128)S(1)}, u32[]{:S(2)}, u32[]{:S(2)}) %collective-permute-start.2) | collective-permute-done | bytes 10272 | tf_op jit(solution)/shard_map/ppermute | solution.py:564
  13.5 1.3 %collective-permute-start.4 = (f32[2,32,1280]{2,1,0:T(8,128)S(1)}, f32[2,32,1280]{2,1,0:T(8,128)S(1)}, u32[]{:S(2)}, u32[]{:S(2)}) collective-permute-start(f32[2,32,1280]{2,1,0:T(8,128)S(1)} %get-tuple-element.86), channel_id=1, source_target_pairs={{0,2},{1,3},{2,0},{3,1},{4,6},{5,7},{6,4},{7,5},{8,10},{9,11},{10,... | collective-permute-start | bytes 983048 | tf_op jit(solution)/shard_map/ppermute | solution.py:564
  14.9 0.3 collective-permute-start.5
  15.2 5.7 %block.2 = (f32[512,1280]{1,0:T(8,128)S(1)}, f32[512,1280]{1,0:T(8,128)S(1)}, bf16[512,1280]{1,0:T(8,128)(2,1)S(1)}, bf16[512,1280]{1,0:T(8,128)(2,1)S(1)}, f32[...) custom-call(bf16[512,2560]{1,0:T(8,128)(2,1)} %in_hbm.7, ...), custom_call_target="tpu_custom_call" | custom-call | flops 1000 | bytes 1000 | tf_op jit(solution)/shard_map/block/pallas_call | solution.py:597
  20.9 0.6 collective-permute-done.4.came_ref.refs_5_
  21.6 0.3 collective-permute-start.7
  21.9 6.1 %block.3 = (f32[512,1280]{1,0:T(8,128)S(1)}, f32[512,1280]{1,0:T(8,128)S(1)}, bf16[512,1280]{1,0:T(8,128)(2,1)S(1)}, bf16[512,1280]{1,0:T(8,128)(2,1)S(1)}, f32[...) custom-call(bf16[512,2560]{1,0:T(8,128)(2,1)} %in_hbm.7, bf16[512,2560]{1,0:T(8,128)(2,1)} %cot_hbm.7, ...), custom_call_target="tpu_custom_call" | custom-call | flops 1000 | bytes 1000 | tf_op jit(solution)/shard_map/block/pallas_call | solution.py:597
  28.0 0.5 collective-permute-done.5.came_ref.refs_5_
  28.6 0.8 collective-permute-start.6
  29.4 4.4 %collective-permute-start.12 = (f32[32,1280]{1,0:T(8,128)S(1)}, f32[32,1280]{1,0:T(8,128)S(1)}, u32[]{:S(2)}, u32[]{:S(2)}) collective-permute-start(f32[32,1280]{1,0:T(8,128)S(1)} %get-tuple-element.108), channel_id=1, source_target_pairs={{4,12},{5,13},{6,14},{7,15},{8,0},{9,1},{10,2},{11,3},{20,28},{21,... | collective-permute-start | bytes 491528 | tf_op jit(solution)/shard_map/ppermute | solution.py:719
  33.8 1.9 %collective-permute-start.11 = (f32[32,1280]{1,0:T(8,128)S(1)}, f32[32,1280]{1,0:T(8,128)S(1)}, u32[]{:S(2)}, u32[]{:S(2)}) collective-permute-start(f32[32,1280]{1,0:T(8,128)S(1)} %get-tuple-element.108), channel_id=1, source_target_pairs={{4,8},{5,9},{6,10},{7,11},{8,4},{9,5},{10,6},{11,7},{20,24},{21,25... | collective-permute-start | bytes 491528 | tf_op jit(solution)/shard_map/ppermute | solution.py:719
  35.9 2.4 %collective-permute-done.10.refs_2_ = f32[1,2560]{1,0:T(1,128)S(1)} collective-permute-done((f32[1,2560]{1,0:T(1,128)S(1)}, f32[1,2560]{1,0:T(1,128)S(1)}, u32[]{:S(2)}, u32[]{:S(2)}) %collective-permute-start.10) | collective-permute-done | bytes 10272 | tf_op jit(solution)/shard_map/ppermute | solution.py:564
  38.3 3.0 %collective-permute-done.11.refs_0_ = f32[32,1280]{1,0:T(8,128)S(1)} collective-permute-done((f32[32,1280]{1,0:T(8,128)S(1)}, f32[32,1280]{1,0:T(8,128)S(1)}, u32[]{:S(2)}, u32[]{:S(2)}) %collective-permute-start.11) | collective-permute-done | bytes 163872 | tf_op jit(solution)/shard_map/ppermute | solution.py:719
  41.5 0.8 %collective-permute-start.14 = (f32[2,32,1280]{2,1,0:T(8,128)S(1)}, f32[2,32,1280]{2,1,0:T(8,128)S(1)}, u32[]{:S(2)}, u32[]{:S(2)}) collective-permute-start(f32[2,32,1280]{2,1,0:T(8,128)S(1)} %get-tuple-element.114), channel_id=1, source_target_pairs={{0,2},{1,3},{2,0},{3,1},{4,6},{5,7},{6,4},{7,5},{8,10},{9,11},{10,... | collective-permute-start | bytes 983048 | tf_op jit(solution)/shard_map/ppermute | solution.py:564
  42.3 1.3 %collective-permute-start.9 = (f32[32,1280]{1,0:T(8,128)S(1)}, f32[32,1280]{1,0:T(8,128)S(1)}, u32[]{:S(2)}, u32[]{:S(2)}) collective-permute-start(f32[32,1280]{1,0:T(8,128)S(1)} %get-tuple-element.110), channel_id=1, source_target_pairs={{4,12},{5,13},{6,14},{7,15},{8,0},{9,1},{10,2},{11,3},{20,28},{21,... | collective-permute-start | bytes 491528 | tf_op jit(solution)/shard_map/ppermute | solution.py:719
  43.6 1.9 %collective-permute-start.8 = (f32[32,1280]{1,0:T(8,128)S(1)}, f32[32,1280]{1,0:T(8,128)S(1)}, u32[]{:S(2)}, u32[]{:S(2)}) collective-permute-start(f32[32,1280]{1,0:T(8,128)S(1)} %get-tuple-element.110), channel_id=1, source_target_pairs={{4,8},{5,9},{6,10},{7,11},{8,4},{9,5},{10,6},{11,7},{20,24},{21,25... | collective-permute-start | bytes 491528 | tf_op jit(solution)/shard_map/ppermute | solution.py:719
  45.5 0.3 collective-permute-done.9.refs_1_
  45.9 3.8 %collective-permute-done.8.refs_0_ = f32[32,1280]{1,0:T(8,128)S(1)} collective-permute-done((f32[32,1280]{1,0:T(8,128)S(1)}, f32[32,1280]{1,0:T(8,128)S(1)}, u32[]{:S(2)}, u32[]{:S(2)}) %collective-permute-start.8) | collective-permute-done | bytes 163872 | tf_op jit(solution)/shard_map/ppermute | solution.py:719
  50.0 8.2 %collective-permute-start.15 = (f32[2,2,32,1280]{3,2,1,0:T(8,128)S(1)}, f32[2,2,32,1280]{3,2,1,0:T(8,128)S(1)}, u32[]{:S(2)}, u32[]{:S(2)}) collective-permute-start(f32[2,2,32,1280]{3,2,1,0:T(8,128)S(1)} %get-tuple-element.124), channel_id=1, source_target_pairs={{0,1},{1,0},{2,3},{3,2},{4,5},{5,4},{6,7},{7,6},{8,9},{9,8},{10,11... | collective-permute-start | bytes 1966088 | tf_op jit(solution)/shard_map/ppermute | solution.py:564
  58.2 1.7 %collective-permute-done.15.took_ref = f32[2,2,32,1280]{3,2,1,0:T(8,128)S(1)} collective-permute-done((f32[2,2,32,1280]{3,2,1,0:T(8,128)S(1)}, f32[2,2,32,1280]{3,2,1,0:T(8,128)S(1)}, u32[]{:S(2)}, u32[]{:S(2)}) %collective-permute-start.15) | collective-permute-done | bytes 655392 | tf_op jit(solution)/shard_map/ppermute | solution.py:564
  59.9 6.5 %finish.2 = (bf16[512,2560]{1,0:T(8,128)(2,1)}, bf16[512,2560]{1,0:T(8,128)(2,1)}, f32[512,128]{1,0:T(8,128)S(1)}, f32[512,128]{1,0:T(8,128)S(1)}, f32[40,512]{1,0:T(8,128)S(1)}) custom-call(f32[512,1280]{1,0:T(8,128)S(1)} %get-tuple-element.118.local_out_ref, f32[512,1280]{1,0:T(8,128)S(1)} %get-tuple-element.119.local_din_ref, ...), custom_call_target="tpu_custom_call" | custom-call | flops 1000 | bytes 1000 | tf_op jit(solution)/shard_map/finish/pallas_call | solution.py:634
  66.4 1.1 %collective-permute-done.13.back_ref = f32[2,32,1280]{2,1,0:T(8,128)S(1)} collective-permute-done((f32[2,32,1280]{2,1,0:T(8,128)S(1)}, f32[2,32,1280]{2,1,0:T(8,128)S(1)}, u32[]{:S(2)}, u32[]{:S(2)}) %collective-permute-start.13) | collective-permute-done | bytes 327712 | tf_op jit(solution)/shard_map/ppermute | solution.py:564
  67.6 0.9 %collective-permute-start.16 = (f32[2,2,32,1280]{3,2,1,0:T(8,128)S(1)}, f32[2,2,32,1280]{3,2,1,0:T(8,128)S(1)}, u32[]{:S(2)}, u32[]{:S(2)}) collective-permute-start(f32[2,2,32,1280]{3,2,1,0:T(8,128)S(1)} %get-tuple-element.132), channel_id=1, source_target_pairs={{0,1},{1,0},{2,3},{3,2},{4,5},{5,4},{6,7},{7,6},{8,9},{9,8},{10,11... | collective-permute-start | bytes 1966088 | tf_op jit(solution)/shard_map/ppermute | solution.py:564
  68.5 1.7 %collective-permute-done.16.took_ref = f32[2,2,32,1280]{3,2,1,0:T(8,128)S(1)} collective-permute-done((f32[2,2,32,1280]{3,2,1,0:T(8,128)S(1)}, f32[2,2,32,1280]{3,2,1,0:T(8,128)S(1)}, u32[]{:S(2)}, u32[]{:S(2)}) %collective-permute-start.16) | collective-permute-done | bytes 655392 | tf_op jit(solution)/shard_map/ppermute | solution.py:564
  70.3 6.6 %finish.3 = (bf16[512,2560]{1,0:T(8,128)(2,1)}, bf16[512,2560]{1,0:T(8,128)(2,1)}, bf16[512,128]{1,0:T(8,128)(2,1)}, bf16[512,128]{1,0:T(8,128)(2,1)}, f32[40,512]{1,0:T(8,128)}) custom-call(f32[512,1280]{1,0:T(8,128)S(1)} %get-tuple-element.96.local_out_ref, ...), custom_call_target="tpu_custom_call", output_to_operand_aliasing={{0}: (15, {}), {1}: (16, {})} | custom-call | flops 1000 | bytes 1000 | tf_op jit(solution)/shard_map/finish/pallas_call | solution.py:634
  (30 shorter events, 1.2 us)
Async XLA Ops:
  5.3 8.1 %collective-permute-start.1 = (f32[2,2,32,1280]{3,2,1,0:T(8,128)S(1)}, f32[2,2,32,1280]{3,2,1,0:T(8,128)S(1)}, u32[]{:S(2)}, u32[]{:S(2)}) collective-permute-start(f32[2,2,32,1280]{3,2,1,0:T(8,128)S(1)} %get-tuple-element.79), channel_id=1, source_target_pairs={{0,1},{1,0},{2,3},{3,2},{4,5},{5,4},{6,7},{7,6},{8,9},{9,8},{10,11... | collective-permute-start | bytes 1966088 | tf_op jit(solution)/shard_map/ppermute | solution.py:564
  6.1 1.7 %collective-permute-start = (f32[1,2560]{1,0:T(1,128)S(1)}, f32[1,2560]{1,0:T(1,128)S(1)}, u32[]{:S(2)}, u32[]{:S(2)}) collective-permute-start(f32[1,2560]{1,0:T(1,128)S(1)} %get-tuple-element.78.own_ref), channel_id=1, source_target_pairs={{0,1},{1,0},{2,3},{3,2},{4,5},{5,4},{6,7},{7,6},{8,9},{9,8},{10,11... | collective-permute-start | bytes 30728 | tf_op jit(solution)/shard_map/ppermute | solution.py:564
  10.5 4.8 %copy-start = (bf16[512,128]{1,0:T(8,128)(2,1)S(1)}, bf16[512,128]{1,0:T(8,128)(2,1)}, u32[]{:S(2)}) copy-start(bf16[512,128]{1,0:T(8,128)(2,1)} %query_ref.3) | copy-start | bytes 393220
  10.5 4.8 %copy-start.1 = (bf16[512,128]{1,0:T(8,128)(2,1)S(1)}, bf16[512,128]{1,0:T(8,128)(2,1)}, u32[]{:S(2)}) copy-start(bf16[512,128]{1,0:T(8,128)(2,1)} %key_ref.3) | copy-start | bytes 393220
  10.5 4.8 %copy-start.3 = (s32[512]{0:T(512)S(1)}, s32[512]{0:T(512)}, u32[]{:S(2)}) copy-start(s32[512]{0:T(512)} %param.14) | copy-start | bytes 6148
  10.5 4.4 %collective-permute-start.3 = (f32[2,2,32,1280]{3,2,1,0:T(8,128)S(1)}, f32[2,2,32,1280]{3,2,1,0:T(8,128)S(1)}, u32[]{:S(2)}, u32[]{:S(2)}) collective-permute-start(f32[2,2,32,1280]{3,2,1,0:T(8,128)S(1)} %get-tuple-element.82), channel_id=1, source_target_pairs={{0,1},{1,0},{2,3},{3,2},{4,5},{5,4},{6,7},{7,6},{8,9},{9,8},{10,11... | collective-permute-start | bytes 1966088 | tf_op jit(solution)/shard_map/ppermute | solution.py:564
  10.9 2.5 %collective-permute-start.2 = (f32[1,2560]{1,0:T(1,128)S(1)}, f32[1,2560]{1,0:T(1,128)S(1)}, u32[]{:S(2)}, u32[]{:S(2)}) collective-permute-start(f32[1,2560]{1,0:T(1,128)S(1)} %mul.3.refs_0_.own_ref.refs_6_), channel_id=1, source_target_pairs={{0,2},{1,3},{2,0},{3,1},{4,6},{5,7},{6,4},{7,5},{8,10},{9,11},{10,... | collective-permute-start | bytes 30728 | tf_op jit(solution)/shard_map/ppermute | solution.py:564
  13.5 8.0 %collective-permute-start.4 = (f32[2,32,1280]{2,1,0:T(8,128)S(1)}, f32[2,32,1280]{2,1,0:T(8,128)S(1)}, u32[]{:S(2)}, u32[]{:S(2)}) collective-permute-start(f32[2,32,1280]{2,1,0:T(8,128)S(1)} %get-tuple-element.86), channel_id=1, source_target_pairs={{0,2},{1,3},{2,0},{3,1},{4,6},{5,7},{6,4},{7,5},{8,10},{9,11},{10,... | collective-permute-start | bytes 983048 | tf_op jit(solution)/shard_map/ppermute | solution.py:564
  14.9 13.6 %collective-permute-start.5 = (f32[2,32,1280]{2,1,0:T(8,128)S(1)}, f32[2,32,1280]{2,1,0:T(8,128)S(1)}, u32[]{:S(2)}, u32[]{:S(2)}) collective-permute-start(f32[2,32,1280]{2,1,0:T(8,128)S(1)} %get-tuple-element.88), channel_id=1, source_target_pairs={{0,2},{1,3},{2,0},{3,1},{4,6},{5,7},{6,4},{7,5},{8,10},{9,11},{10,... | collective-permute-start | bytes 983048 | tf_op jit(solution)/shard_map/ppermute | solution.py:564
  21.6 7.8 %collective-permute-start.7 = (f32[32,1280]{1,0:T(8,128)S(1)}, f32[32,1280]{1,0:T(8,128)S(1)}, u32[]{:S(2)}, u32[]{:S(2)}) collective-permute-start(f32[32,1280]{1,0:T(8,128)S(1)} %get-tuple-element.92), channel_id=1, source_target_pairs={{0,4},{1,5},{2,6},{3,7},{4,0},{5,1},{6,2},{7,3},{8,12},{9,13},{10,... | collective-permute-start | bytes 491528 | tf_op jit(solution)/shard_map/ppermute | solution.py:707
  28.6 7.3 %collective-permute-start.6 = (f32[32,1280]{1,0:T(8,128)S(1)}, f32[32,1280]{1,0:T(8,128)S(1)}, u32[]{:S(2)}, u32[]{:S(2)}) collective-permute-start(f32[32,1280]{1,0:T(8,128)S(1)} %get-tuple-element.103), channel_id=1, source_target_pairs={{0,4},{1,5},{2,6},{3,7},{4,0},{5,1},{6,2},{7,3},{8,12},{9,13},{10,... | collective-permute-start | bytes 491528 | tf_op jit(solution)/shard_map/ppermute | solution.py:707
  29.4 30.5 %copy-start.2 = (f32[512,40]{0,1:T(8,128)S(1)}, f32[512,40]{0,1:T(8,128)}, u32[]{:S(2)}) copy-start(f32[512,40]{0,1:T(8,128)} %param.9) | copy-start | bytes 245764
  29.4 30.5 %copy-start.4 = (f32[40]{0:T(128)S(1)}, f32[40]{0:T(128)}, u32[]{:S(2)}) copy-start(f32[40]{0:T(128)} %param.12) | copy-start | bytes 484
  29.4 8.9 %collective-permute-start.12 = (f32[32,1280]{1,0:T(8,128)S(1)}, f32[32,1280]{1,0:T(8,128)S(1)}, u32[]{:S(2)}, u32[]{:S(2)}) collective-permute-start(f32[32,1280]{1,0:T(8,128)S(1)} %get-tuple-element.108), channel_id=1, source_target_pairs={{4,12},{5,13},{6,14},{7,15},{8,0},{9,1},{10,2},{11,3},{20,28},{21,... | collective-permute-start | bytes 491528 | tf_op jit(solution)/shard_map/ppermute | solution.py:719
  33.8 7.5 %collective-permute-start.11 = (f32[32,1280]{1,0:T(8,128)S(1)}, f32[32,1280]{1,0:T(8,128)S(1)}, u32[]{:S(2)}, u32[]{:S(2)}) collective-permute-start(f32[32,1280]{1,0:T(8,128)S(1)} %get-tuple-element.108), channel_id=1, source_target_pairs={{4,8},{5,9},{6,10},{7,11},{8,4},{9,5},{10,6},{11,7},{20,24},{21,25... | collective-permute-start | bytes 491528 | tf_op jit(solution)/shard_map/ppermute | solution.py:719
  35.8 2.6 %collective-permute-start.10 = (f32[1,2560]{1,0:T(1,128)S(1)}, f32[1,2560]{1,0:T(1,128)S(1)}, u32[]{:S(2)}, u32[]{:S(2)}) collective-permute-start(f32[1,2560]{1,0:T(1,128)S(1)} %get-tuple-element.107.refs_2_), channel_id=1, source_target_pairs={{0,4},{1,5},{2,6},{3,7},{4,0},{5,1},{6,2},{7,3},{8,12},{9,13},{10,... | collective-permute-start | bytes 30728 | tf_op jit(solution)/shard_map/ppermute | solution.py:564
  41.5 8.3 %collective-permute-start.14 = (f32[2,32,1280]{2,1,0:T(8,128)S(1)}, f32[2,32,1280]{2,1,0:T(8,128)S(1)}, u32[]{:S(2)}, u32[]{:S(2)}) collective-permute-start(f32[2,32,1280]{2,1,0:T(8,128)S(1)} %get-tuple-element.114), channel_id=1, source_target_pairs={{0,2},{1,3},{2,0},{3,1},{4,6},{5,7},{6,4},{7,5},{8,10},{9,11},{10,... | collective-permute-start | bytes 983048 | tf_op jit(solution)/shard_map/ppermute | solution.py:564
  42.3 3.5 %collective-permute-start.9 = (f32[32,1280]{1,0:T(8,128)S(1)}, f32[32,1280]{1,0:T(8,128)S(1)}, u32[]{:S(2)}, u32[]{:S(2)}) collective-permute-start(f32[32,1280]{1,0:T(8,128)S(1)} %get-tuple-element.110), channel_id=1, source_target_pairs={{4,12},{5,13},{6,14},{7,15},{8,0},{9,1},{10,2},{11,3},{20,28},{21,... | collective-permute-start | bytes 491528 | tf_op jit(solution)/shard_map/ppermute | solution.py:719
  43.6 6.1 %collective-permute-start.8 = (f32[32,1280]{1,0:T(8,128)S(1)}, f32[32,1280]{1,0:T(8,128)S(1)}, u32[]{:S(2)}, u32[]{:S(2)}) collective-permute-start(f32[32,1280]{1,0:T(8,128)S(1)} %get-tuple-element.110), channel_id=1, source_target_pairs={{4,8},{5,9},{6,10},{7,11},{8,4},{9,5},{10,6},{11,7},{20,24},{21,25... | collective-permute-start | bytes 491528 | tf_op jit(solution)/shard_map/ppermute | solution.py:719
  50.0 9.9 %collective-permute-start.15 = (f32[2,2,32,1280]{3,2,1,0:T(8,128)S(1)}, f32[2,2,32,1280]{3,2,1,0:T(8,128)S(1)}, u32[]{:S(2)}, u32[]{:S(2)}) collective-permute-start(f32[2,2,32,1280]{3,2,1,0:T(8,128)S(1)} %get-tuple-element.124), channel_id=1, source_target_pairs={{0,1},{1,0},{2,3},{3,2},{4,5},{5,4},{6,7},{7,6},{8,9},{9,8},{10,11... | collective-permute-start | bytes 1966088 | tf_op jit(solution)/shard_map/ppermute | solution.py:564
  58.2 9.3 %collective-permute-start.13 = (f32[2,32,1280]{2,1,0:T(8,128)S(1)}, f32[2,32,1280]{2,1,0:T(8,128)S(1)}, u32[]{:S(2)}, u32[]{:S(2)}) collective-permute-start(f32[2,32,1280]{2,1,0:T(8,128)S(1)} %get-tuple-element.116), channel_id=1, source_target_pairs={{0,2},{1,3},{2,0},{3,1},{4,6},{5,7},{6,4},{7,5},{8,10},{9,11},{10,... | collective-permute-start | bytes 983048 | tf_op jit(solution)/shard_map/ppermute | solution.py:564
  67.6 2.6 %collective-permute-start.16 = (f32[2,2,32,1280]{3,2,1,0:T(8,128)S(1)}, f32[2,2,32,1280]{3,2,1,0:T(8,128)S(1)}, u32[]{:S(2)}, u32[]{:S(2)}) collective-permute-start(f32[2,2,32,1280]{3,2,1,0:T(8,128)S(1)} %get-tuple-element.132), channel_id=1, source_target_pairs={{0,1},{1,0},{2,3},{3,2},{4,5},{5,4},{6,7},{7,6},{8,9},{9,8},{10,11... | collective-permute-start | bytes 1966088 | tf_op jit(solution)/shard_map/ppermute | solution.py:564

commit v4 on v3

v4 whole, which is shorter than its diff:
```python
import functools

import jax
import jax.numpy as jnp
from jax import lax
from jax.experimental import pallas as pl
from jax.experimental.pallas import tpu as pltpu
from jax.sharding import PartitionSpec as P

WIDTHS = (10, 10)
TILES = (5, 5)
SLACK = 1.0
SMALL_COST = 900_000_000
STATES_COST = 4_000_000_000
VMEM_BYTES = 28 * 1024 * 1024

F32 = jnp.float32
BF16 = jnp.bfloat16


def dot_nn(left, right):
    return lax.dot_general(left, right, (((1,), (0,)), ((), ())), preferred_element_type=F32)


def dot_nt(left, right):
    return lax.dot_general(left, right, (((1,), (1,)), ((), ())), preferred_element_type=F32)


def halves(value):
    high = value.astype(BF16)
    return high, (value - high.astype(F32)).astype(BF16)


def sum_dot(matrix, value):
    first = value.astype(BF16)
    rest = value - first.astype(F32)
    second = rest.astype(BF16)
    third = (rest - second.astype(F32)).astype(BF16)
    return dot_nn(matrix, first) + dot_nn(matrix, second) + dot_nn(matrix, third)


def head_spread(depth, offset, head_count, first_column, columns, head_size):
    row = lax.broadcasted_iota(jnp.int32, (depth, columns), 0) - offset
    held = (row >= 0) & (row < 2 * head_count)
    row = jnp.where(row >= head_count, row - head_count, row)
    column = lax.broadcasted_iota(jnp.int32, (depth, columns), 1) + first_column
    inside = column - row * head_size
    return jnp.where(held & (inside >= 0) & (inside < head_size), 1.0, 0.0).astype(BF16)


def head_collect(head_count, first_column, columns, head_size):
    row = lax.broadcasted_iota(jnp.int32, (columns, head_count), 0) + first_column
    column = lax.broadcasted_iota(jnp.int32, (columns, head_count), 1)
    offset = row - column * head_size
    return jnp.where((offset >= 0) & (offset < head_size), 1.0, 0.0).astype(BF16)


def triangle(rows, lower):
    first = lax.broadcasted_iota(jnp.int32, (rows, rows), 0)
    second = lax.broadcasted_iota(jnp.int32, (rows, rows), 1)
    return (first >= second) if lower else (first <= second)


def start_counts(starts_row):
    rows = starts_row.shape[1]
    flags = starts_row.astype(F32)
    column = jnp.sum(jnp.where(triangle(rows, True), flags, 0.0), axis=1, keepdims=True)
    spread = jnp.broadcast_to(flags, (8, rows)).astype(BF16)
    row = dot_nn(spread, triangle(rows, False).astype(F32).astype(BF16))[:1]
    return column, row


def softplus(value):
    return jnp.maximum(value, 0.0) + jnp.log1p(jnp.exp(-jnp.abs(value)))


def sum_dot_left(value, matrix):
    first = value.astype(BF16)
    rest = value - first.astype(F32)
    second = rest.astype(BF16)
    third = (rest - second.astype(F32)).astype(BF16)
    return dot_nn(first, matrix) + dot_nn(second, matrix) + dot_nn(third, matrix)


def fetch(pairs, sems):
    copies = [
        pltpu.make_async_copy(source, target, sems.at[i])
        for i, (source, target) in enumerate(pairs)
    ]
    for copy in copies:
        copy.start()
    return copies


def prep_kernel(
    head_size, raw_hbm, rate_hbm, skip_hbm, starts_hbm, query_hbm, key_hbm,
    heads_ref, maps_ref, turned_ref, rows_ref, decay_ref,
    raw_ref, rate_ref, skip_ref, starts_ref, query_ref, key_ref, sems,
):
    copies = fetch(
        [
            (raw_hbm, raw_ref), (rate_hbm, rate_ref), (skip_hbm, skip_ref),
            (starts_hbm, starts_ref), (query_hbm, query_ref), (key_hbm, key_ref),
        ],
        sems,
    )
    head_count, rows = raw_ref.shape
    upper = triangle(rows, False).astype(F32).astype(BF16)
    for copy in copies:
        copy.wait()
    step = softplus(raw_ref[...])
    rate = jnp.broadcast_to(rate_ref[...], (8, head_count)).T[:, :1]
    cumulative = sum_dot_left(-step * rate, upper)
    count, _ = start_counts(starts_ref[...])
    in_lead = count == 0.0
    in_tail = count == count[rows - 1 :, :]
    state_size = query_ref.shape[1]
    lead = jnp.where(in_lead, query_ref[...].astype(F32), 0.0)
    tail = jnp.where(in_tail, key_ref[...].astype(F32), 0.0)
    maps_ref[:, :state_size] = lead.astype(BF16)
    maps_ref[:, state_size:] = tail.astype(BF16)
    turned_ref[:state_size] = lead.T.astype(BF16)
    turned_ref[state_size:] = tail.T.astype(BF16)
    fall = jnp.exp(cumulative).T
    grow = (jnp.exp(-cumulative) * step).T
    heads_ref[...] = jnp.concatenate(
        halves(fall)
        + halves(grow)
        + (
            jnp.where(in_lead, 1.0, 0.0).astype(BF16),
            jnp.where(in_tail, 1.0, 0.0).astype(BF16),
        ),
        axis=1,
    )
    channels = rows_ref.shape[1]
    spread = head_spread(2 * head_count, 0, head_count, 0, channels, head_size)

    def wide(value):
        return dot_nn(
            jnp.concatenate(halves(jnp.broadcast_to(value, (8, head_count))), axis=1), spread
        )[:1]

    last = wide(fall[rows - 1 :, :])
    decay = jnp.where(count[rows - 1 :, :] == 0.0, last, 0.0)
    rows_ref[0:1, :] = decay
    rows_ref[1:2, :] = last
    rows_ref[2:3, :] = wide(skip_ref[...])
    decay_ref[...] = decay


def place():
    index = lax.axis_index("seq")
    return ((index & 1) == 0, (index & 2) == 0, (index & 4) == 0), index >> 3


def outward(firsts, value):
    half = value.shape[0] // 2
    low, high = value[:half], value[half:]
    other, own = jnp.where(firsts[0], high, low), jnp.where(firsts[0], low, high)
    if len(firsts) > 1:
        other, own = outward(firsts[1:], other), outward(firsts[1:], own)
    return jnp.concatenate([other, own], axis=0)


def inward(firsts, other, own):
    if len(firsts) > 1:
        half = own.shape[0] // 2
        other = inward(firsts[1:], other[:half], other[half:])
        own = inward(firsts[1:], own[:half], own[half:])
    low, high = jnp.where(firsts[0], own, other), jnp.where(firsts[0], other, own)
    return jnp.concatenate([low, high], axis=0)


def joined(first, own_decay, other_decay, own, came):
    one = jnp.ones_like(own_decay)
    forward = (
        jnp.where(first, other_decay, one) * own[0] + jnp.where(first, one, own_decay) * came[0]
    )
    backward = (
        jnp.where(first, one, other_decay) * own[1] + jnp.where(first, own_decay, one) * came[1]
    )
    return forward, backward


def split_pair(first, own_decay, other_decay, own, came, entering, leaving, put_own, put_other):
    @pl.when(first)
    def _():
        put_own(0, entering)
        put_other(0, own_decay * entering + own(0))
        put_other(1, leaving)
        put_own(1, other_decay * leaving + came(1))

    @pl.when(jnp.logical_not(first))
    def _():
        put_other(0, entering)
        put_own(0, other_decay * entering + came(0))
        put_own(1, leaving)
        put_other(1, own_decay * leaving + own(1))


def join_kernel(columns, level, kept_ref, came_ref, own_ref, other_ref, sent_ref, next_ref=None):
    firsts, unit = place()
    forward, backward = joined(
        firsts[level], own_ref[:, columns], other_ref[:, columns], kept_ref, came_ref
    )
    if level == 2:
        if next_ref is not None:
            next_ref[0] = forward
            next_ref[1] = backward
        sent_ref[...] = jnp.where((unit & 1) == 1, backward, forward)
        return
    half = forward.shape[0] // 2
    for chain, value in enumerate((forward, backward)):
        sent_ref[chain] = value[:half]
        next_ref[chain] = value[half:]


def absorb(columns, level, plane, taken_refs, others, enter_ref):
    upper = ((plane >> level) & 1) == 1
    taken = taken_refs[0][...]
    for ref in taken_refs[1:]:
        taken = taken + ref[...]
    if level == 0:
        zero = jnp.zeros_like(taken)
        return jnp.where(upper, taken, zero), jnp.where(upper, zero, taken)
    before = after = None
    for lower, ref in enumerate(others[:level]):
        other = ref[:, columns]
        above = ((plane >> lower) & 1) == 1
        one = jnp.ones_like(other)
        first = jnp.where(above, other, one)
        second = jnp.where(above, one, other)
        before = first if before is None else before * first
        after = second if after is None else after * second
    zero = jnp.zeros_like(before)
    return (
        enter_ref[0] + jnp.where(upper, before, zero) * taken,
        enter_ref[1] + jnp.where(upper, zero, after) * taken,
    )


def level_kernel(columns, level, taken_count, *refs):
    taken, refs = refs[:taken_count], refs[taken_count:]
    others, refs = refs[:level], refs[level:]
    enter_ref = None
    if level:
        enter_ref, refs = refs[0], refs[1:]
    both_ref, decay_ref, pay_ref, next_ref = refs
    _, plane = place()
    entering, leaving = absorb(columns, level, plane, taken, others, enter_ref)
    next_ref[0] = entering
    next_ref[1] = leaving
    upper = ((plane >> (level + 1)) & 1) == 1
    decay = decay_ref[:, columns]

    @pl.when(upper)
    def _():
        pay_ref[...] = decay * leaving + both_ref[1]

    @pl.when(jnp.logical_not(upper))
    def _():
        pay_ref[...] = decay * entering + both_ref[0]


def top_kernel(columns, level, taken_count, *refs):
    taken, refs = refs[:taken_count], refs[taken_count:]
    others, refs = refs[:level], refs[level:]
    enter_ref = None
    if level:
        enter_ref, refs = refs[0], refs[1:]
    kept_ref, came_ref, own_ref, other_ref, theirs_ref, mine_ref = refs
    firsts, plane = place()
    entering, leaving = absorb(columns, level, plane, taken, others, enter_ref)

    def put_own(chain, value):
        mine_ref[chain] = value

    def put_other(chain, value):
        theirs_ref[chain] = value

    split_pair(
        firsts[2], own_ref[:, columns], other_ref[:, columns], lambda i: kept_ref[i],
        lambda i: came_ref[i], entering, leaving, put_own, put_other,
    )


def return_kernel(
    columns, level, back_ref, mine_ref, kept_ref, came_ref, own_ref, other_ref, give_ref, stay_ref
):
    first = place()[0][level]
    half = back_ref.shape[1]
    for slot, source in enumerate((back_ref, mine_ref)):
        here = slice(slot * half, (slot + 1) * half)

        def put_own(chain, value, here=here):
            stay_ref[chain, here] = value

        def put_other(chain, value, here=here):
            give_ref[chain, here] = value

        split_pair(
            first, own_ref[:, columns], other_ref[:, columns],
            lambda i, here=here: kept_ref[i, here], lambda i, here=here: came_ref[i, here],
            source[0], source[1], put_own, put_other,
        )


def scale_columns(heads_ref, head_count, head_size, first, columns):
    heads = heads_ref[...]
    depth = heads.shape[1]
    args = (head_count, first, columns, head_size)
    fall = dot_nn(heads, head_spread(depth, 0, *args))
    grow = dot_nn(heads, head_spread(depth, 2 * head_count, *args))
    return fall, grow


def load_tiles(in_hbm, cot_hbm, in_ref, cot_ref, sems, first, tile):
    found = []
    for i in range(in_ref.shape[1] // tile):
        here = pl.ds(first + i * tile, tile)
        there = pl.ds(i * tile, tile)
        pair = []
        for j, (source, target) in enumerate(((in_hbm, in_ref), (cot_hbm, cot_ref))):
            copy = pltpu.make_async_copy(
                source.at[:, here], target.at[:, there], sems.at[2 * i + j]
            )
            copy.start()
            pair.append(copy)
        found.append(pair)
    return found


def states_kernel(
    head_count, head_size, first_column, tile, in_hbm, cot_hbm, heads_ref, turned_ref, rows_ref,
    send_ref, keep_ref, in_ref, cot_ref, sems,
):
    copies = load_tiles(in_hbm, cot_hbm, in_ref, cot_ref, sems, first_column, tile)
    firsts, _ = place()
    state_size = turned_ref.shape[0] // 2
    for i, pair in enumerate(copies):
        here = slice(i * tile, (i + 1) * tile)
        there = slice(first_column + i * tile, first_column + (i + 1) * tile)
        fall, grow = scale_columns(heads_ref, head_count, head_size, there.start, tile)
        for copy in pair:
            copy.wait()
        grown = (grow * in_ref[:, here].astype(F32)).astype(BF16)
        fallen = (fall * cot_ref[:, here].astype(F32)).astype(BF16)
        state = dot_nn(turned_ref[state_size:], grown) * rows_ref[1:2, there]
        direct = dot_nn(turned_ref[:state_size], fallen)
        half = state_size // 2
        for chain, value in enumerate((state, direct)):
            value = outward(firsts, value)
            send_ref[chain, :, here] = value[:half]
            keep_ref[chain, :, here] = value[half:]


def local_kernel(
    head_count, head_size, first_column, initial, final, in_hbm, cot_hbm, heads_ref, rows_ref,
    starts_ref, query_ref, key_ref, *refs,
):
    if not initial:
        score_ref, scoret_ref, total_in, refs = *refs[:3], refs[3:]
    out_ref, din_ref, grown_ref, fallen_ref, grow_ref, fall_ref, sums_ref = refs[:7]
    refs = refs[7:]
    if initial:
        (score_ref, scoret_ref), refs = refs[:2], refs[2:]
    (total_out, *key_out), (in_ref, cot_ref, sems) = refs[:-3], refs[-3:]
    rows, columns = in_ref.shape
    ((in_copy, cot_copy),) = load_tiles(
        in_hbm, cot_hbm, in_ref, cot_ref, sems, first_column, columns
    )
    if initial or final:
        column, row = start_counts(starts_ref[...])
        same = column == row
        allowed = same & triangle(rows, True)
    if initial:
        score_ref[...] = jnp.where(allowed, dot_nt(query_ref[...], key_ref[...]), 0.0).astype(BF16)
        scoret_ref[...] = jnp.where(
            same & triangle(rows, False), dot_nt(key_ref[...], query_ref[...]), 0.0
        ).astype(BF16)
    fall, grow = scale_columns(heads_ref, head_count, head_size, first_column, columns)
    fall_ref[...] = fall.astype(BF16)
    grow_ref[...] = grow.astype(BF16)
    collect = head_collect(head_count, first_column, columns, head_size)
    in_copy.wait()
    cot_copy.wait()
    in_wide = in_ref[...].astype(F32)
    cot_wide = cot_ref[...].astype(F32)
    skip = rows_ref[2:3, first_column : first_column + columns]
    grown = (grow * in_wide).astype(BF16)
    fallen = (fall * cot_wide).astype(BF16)
    grown_ref[...] = grown
    fallen_ref[...] = fallen
    total = dot_nt(fallen, grown)
    if not initial:
        total += total_in[...]
    produced = dot_nn(score_ref[...], grown)
    out_ref[...] = fall * produced + skip * in_wide
    sums_ref[0] = dot_nn((fallen.astype(F32) * produced).astype(BF16), collect)
    pulled = dot_nn(scoret_ref[...], fallen)
    din_ref[...] = grow * pulled + skip * cot_wide
    sums_ref[1] = dot_nn((grown.astype(F32) * pulled).astype(BF16), collect)
    if final:
        grads = jnp.where(allowed, total, 0.0)
        total_out[...] = dot_nn(grads.astype(BF16), key_ref[...])
        key_out[0][...] = dot_nn(grads.T.astype(BF16), query_ref[...])
    else:
        total_out[...] = total


def finish_kernel(
    head_count, head_size, first_column, tile, pieces, prior, final, *refs,
):
    blocks = [refs[7 * i : 7 * i + 7] for i in range(pieces)]
    (took_ref, own_ref, rows_ref, heads_ref, maps_ref, dquery_in, dkey_in) = refs[
        7 * pieces : 7 * pieces + 7
    ]
    refs = refs[7 * pieces + 7 :]
    if final:
        (raw_ref, rate_ref), refs = refs[:2], refs[2:]
    if prior:
        (sums_in, edge_in), refs = refs[:2], refs[4:]
    out_hbm, din_hbm, dquery_ref, dkey_ref, *results, out_ref, din_ref, sems = refs
    rows, state_size = dquery_in.shape
    firsts, _ = place()
    rise = sink = edge = dlead = dtail = None
    if prior:
        rise, sink, edge = sums_in[0], sums_in[1], edge_in[...]
    copies = []
    for i, block in enumerate(blocks):
        local_out_ref, local_din_ref, grown_ref, fallen_ref, grow_ref, fall_ref, sums_ref = block
        here = slice(i * tile, (i + 1) * tile)
        there = slice(first_column + i * tile, first_column + (i + 1) * tile)
        entering = inward(firsts, took_ref[0, :, here], own_ref[0, :, here])
        leaving = inward(firsts, took_ref[1, :, here], own_ref[1, :, here])
        grown = grown_ref[...]
        fallen = fallen_ref[...]
        entering_bf = entering.astype(BF16)
        leaving_bf = (leaving * rows_ref[1:2, there]).astype(BF16)
        reached = dot_nn(maps_ref[:, :state_size], entering_bf)
        behind = dot_nn(maps_ref[:, state_size:], leaving_bf)
        out_ref[:, here] = (local_out_ref[...] + fall_ref[...].astype(F32) * reached).astype(BF16)
        din_ref[:, here] = (local_din_ref[...] + grow_ref[...].astype(F32) * behind).astype(BF16)
        for j, (source, target) in enumerate(((out_ref, out_hbm), (din_ref, din_hbm))):
            copy = pltpu.make_async_copy(
                source.at[:, pl.ds(here.start, tile)], target.at[:, pl.ds(there.start, tile)],
                sems.at[2 * i + j],
            )
            copy.start()
            copies.append(copy)
        collect = head_collect(head_count, there.start, tile, head_size)
        rise_now = dot_nn((fallen.astype(F32) * reached).astype(BF16), collect) + sums_ref[0]
        pulled = grown.astype(F32) * behind
        sink_now = dot_nn(pulled.astype(BF16), collect) + sums_ref[1]
        edge_row = jnp.sum(pulled, axis=0, keepdims=True) + rows_ref[0:1, there] * jnp.sum(
            entering * leaving, axis=0, keepdims=True
        )
        high, rest = halves(jnp.broadcast_to(edge_row, (8, tile)))
        edge_now = dot_nn(high, collect) + dot_nn(rest, collect)
        dlead_now = dot_nt(fallen, entering_bf)
        dtail_now = dot_nt(grown, leaving_bf)
        rise = rise_now if rise is None else rise + rise_now
        sink = sink_now if sink is None else sink + sink_now
        edge = edge_now if edge is None else edge + edge_now
        dlead = dlead_now if dlead is None else dlead + dlead_now
        dtail = dtail_now if dtail is None else dtail + dtail_now
    in_lead = heads_ref[:, 4 * head_count : 4 * head_count + 1].astype(F32) > 0.5
    in_tail = heads_ref[:, 4 * head_count + 1 : 4 * head_count + 2].astype(F32) > 0.5
    dquery_ref[...] = (dquery_in[...] + jnp.where(in_lead, dlead, 0.0)).astype(dquery_ref.dtype)
    dkey_ref[...] = (dkey_in[...] + jnp.where(in_tail, dtail, 0.0)).astype(dkey_ref.dtype)
    if final:
        lower = triangle(rows, True).astype(F32).astype(BF16)
        sink_turned = sink.T
        later = sum_dot_left(rise.T - sink_turned, lower) + edge.T[:, :1]
        raw = raw_ref[...]
        rate = jnp.broadcast_to(rate_ref[...], (8, head_count)).T[:, :1]
        results[0][...] = (sink_turned / softplus(raw) - rate * later) / (1.0 + jnp.exp(-raw))
    else:
        results[0][0] = rise
        results[0][1] = sink
        results[1][...] = edge
    for copy in copies:
        copy.wait()


def schedule(widths, tiles, levels):
    total = sum(widths)
    chunks = len(widths)
    pieces = [tile for width, tile in zip(widths, tiles) for _ in range(width // tile)]
    middle = ["climb"] * (levels - 1)
    stages = ["chip", "plane", "pair"] + middle + ["top", "side", "device", "end"]
    moves = [15.6, 7.8] + [5.8] * levels + [7.8, 15.6, 3.0, 0.0]
    links = ["side", "low"] + ["high"] * levels + ["low", "side", "core", None]
    at = [0] * chunks
    ready = [3.0 + 0.3 * k for k in range(chunks)]
    free = {}
    now, blocks, order, ended = 3.0, 0, [], 0
    while ended < chunks:
        chain = [k for k in range(chunks) if at[k] < len(stages) - 1]
        soon = min(chain, key=lambda k: (ready[k], -at[k]), default=None)
        work = 11.0 * widths[ended] / total
        left = blocks < len(pieces)
        block = 11.5 * pieces[blocks] / total if left else 0.0
        can_end = at[ended] == len(stages) - 1 and not left
        fits = soon is not None and now + block <= ready[soon] + SLACK
        if left and min(at) > 0 and (fits or soon is None):
            order.append(("parts", blocks))
            now += block
            blocks += 1
            continue
        if soon is None:
            pick = ended
        elif can_end and max(now, ready[ended]) + work <= ready[soon] + 3.0:
            pick = ended
        else:
            pick = soon
        now = max(now, ready[pick])
        stage = stages[at[pick]]
        order.append((stage, pick))
        if stage == "end":
            now += work
            ended += 1
            at[pick] += 1
            continue
        now += 1.6
        link = links[at[pick]]
        begin = max(now, free.get(link, 0.0))
        free[link] = begin + moves[at[pick]] * widths[pick] / total
        ready[pick] = free[link] + 0.5
        at[pick] += 1
    return order


def params():
    return pltpu.CompilerParams(vmem_limit_bytes=VMEM_BYTES)


def cost(flops, count):
    return pl.CostEstimate(flops=flops, bytes_accessed=count, transcendentals=0)


def after(kernel, count, extra):
    def run(*refs):
        kernel(*refs[:count], *refs[count + extra :])

    return run


ANY = pl.BlockSpec(memory_space=pl.ANY)
HBM = pl.BlockSpec(memory_space=pltpu.HBM)
NEAR = pl.BlockSpec(memory_space=pltpu.VMEM)


def local(inputs, raw_steps, input_map, output_map, decay_rates, skip_gain, starts, cotangent):
    rows, channels = inputs.shape
    head_count = decay_rates.shape[0]
    head_size = channels // head_count
    state_size = input_map.shape[1]
    eighth = state_size // 8
    unit = channels // sum(WIDTHS)
    widths = [count * unit for count in WIDTHS]
    tile_of = [count * unit for count in TILES]
    chunks = len(widths)
    firsts = [sum(widths[:k]) for k in range(chunks)]

    size = lax.axis_size("seq")
    planes = size // 8
    levels = planes.bit_length() - 1
    starts_row = starts.reshape(1, rows)
    rate_row = decay_rates.reshape(1, head_count)
    skip_heads = skip_gain.reshape(1, head_count)
    raw_turned = raw_steps.T

    def far(value):
        return pltpu.with_memory_space_constraint(value, pltpu.HBM)

    def shape(dims, kind=F32):
        return jax.ShapeDtypeStruct(dims, kind)

    heads, maps, turned, wide_rows, decay = pl.pallas_call(
        functools.partial(prep_kernel, head_size),
        out_shape=(
            shape((rows, 4 * head_count + 2), BF16),
            shape((rows, 2 * state_size), BF16),
            shape((2 * state_size, rows), BF16),
            shape((8, channels)),
            shape((1, channels)),
        ),
        in_specs=[HBM] * 6,
        scratch_shapes=[
            pltpu.VMEM((head_count, rows), F32), pltpu.VMEM((1, head_count), F32),
            pltpu.VMEM((1, head_count), F32), pltpu.VMEM((1, rows), jnp.int32),
            pltpu.VMEM((rows, state_size), BF16), pltpu.VMEM((rows, state_size), BF16),
            pltpu.SemaphoreType.DMA((6,)),
        ],
        compiler_params=params(),
        name="prep",
    )(*(far(v) for v in (raw_turned, rate_row, skip_heads, starts_row, output_map, input_map)))

    row_shape = shape((1, channels))

    def flat_shape(chunk):
        return shape((eighth, widths[chunk]))

    def pair_shape(chunk, scale=1):
        return shape((2, scale * eighth, widths[chunk]))

    def tile_scratch(chunk):
        block = (rows, widths[chunk])
        return [
            pltpu.VMEM(block, BF16), pltpu.VMEM(block, BF16),
            pltpu.SemaphoreType.DMA((2 * widths[chunk] // tile_of[chunk],)),
        ]

    def device_states(chunk, last):
        kernel = functools.partial(
            states_kernel, head_count, head_size, firsts[chunk], tile_of[chunk]
        )
        return pl.pallas_call(
            after(kernel, 5, len(last)),
            out_shape=(pair_shape(chunk, 4), pair_shape(chunk, 4)),
            in_specs=[HBM, HBM, NEAR, NEAR, NEAR] + [ANY] * len(last),
            scratch_shapes=tile_scratch(chunk),
            compiler_params=params(),
            cost_estimate=cost(STATES_COST, 1000),
            name="states",
        )(far(inputs), far(cotangent), heads, turned, wide_rows, *last)

    def swap(value, bit):
        return lax.ppermute(value, "seq", [(i, i ^ bit) for i in range(size)])

    def level_perms(level):
        span = 1 << level
        perms = []
        for shift in range(span):
            pairs = []
            for base in range(0, planes, 2 * span):
                pairs.append((base + span - 1, base + span + shift))
                pairs.append((base + span, base + span - 1 - shift))
            perms.append([(8 * a + r, 8 * b + r) for a, b in pairs for r in range(8)])
        return perms

    held = {"last": ()}

    def small(kernel, out_shape, name, *operands):
        last = held["last"]
        return pl.pallas_call(
            after(kernel, len(operands), len(last)),
            out_shape=out_shape,
            in_specs=[NEAR] * len(operands) + [ANY] * len(last),
            compiler_params=params(),
            cost_estimate=cost(SMALL_COST, 1000),
            name=name,
        )(*operands, *last)

    tiles = [
        (k, firsts[k] + i * tile_of[k], tile_of[k])
        for k in range(chunks)
        for i in range(widths[k] // tile_of[k])
    ]

    def block_parts(piece, sofar):
        last = held["last"]
        initial = piece == 0
        final = piece == len(tiles) - 1
        _, first, tile = tiles[piece]
        square = (rows, rows)
        block = (rows, tile)
        outs = [shape(block)] * 2 + [shape(block, BF16)] * 4 + [shape((2, rows, head_count))]
        if initial:
            outs += [shape(square, BF16), shape(square, BF16)]
        outs += [shape((rows, state_size))] * 2 if final else [shape(square)]
        operands = [
            far(inputs), far(cotangent), heads, wide_rows, starts_row, output_map, input_map,
        ] + list(sofar)
        kernel = functools.partial(local_kernel, head_count, head_size, first, initial, final)
        made = pl.pallas_call(
            after(kernel, len(operands), len(last)),
            out_shape=tuple(outs),
            in_specs=[HBM, HBM] + [NEAR] * (len(operands) - 2) + [ANY] * len(last),
            scratch_shapes=[
                pltpu.VMEM(block, BF16), pltpu.VMEM(block, BF16), pltpu.SemaphoreType.DMA((2,)),
            ],
            compiler_params=params(),
            cost_estimate=cost(1000, 1000),
            name="block",
        )(*operands, *last)
        if final:
            return made[:7], tuple(made[-2:])
        if initial:
            return made[:7], tuple(made[7:])
        return made[:7], (sofar[0], sofar[1], made[7])

    def finish(chunk, blocks, took, own, grads, prior):
        flat = (rows, state_size)
        tile = tile_of[chunk]
        last = held["last"]
        final = chunk == chunks - 1
        operands = [value for block in blocks for value in block]
        operands += [took, own, wide_rows, heads, maps, *grads]
        if final:
            operands += [raw_turned, rate_row]
        in_specs = [NEAR] * len(operands)
        aliases = {}
        if prior:
            aliases = {len(operands) + 2: 0, len(operands) + 3: 1}
            operands += list(prior)
            in_specs += [NEAR, NEAR, ANY, ANY]
        kind = BF16 if final else F32
        ends = [shape((head_count, rows))]
        if not final:
            ends = [shape((2, rows, head_count)), shape((8, head_count))]
        kernel = functools.partial(
            finish_kernel, head_count, head_size, firsts[chunk], tile, len(blocks), bool(prior),
            final,
        )
        result = shape((rows, widths[chunk]), BF16)
        return pl.pallas_call(
            after(kernel, len(operands), len(last)),
            out_shape=(
                shape((rows, channels), BF16), shape((rows, channels), BF16),
                shape(flat, kind), shape(flat, kind), *ends,
            ),
            in_specs=in_specs + [ANY] * len(last),
            out_specs=(ANY, ANY, NEAR, NEAR) + (NEAR,) * len(ends),
            scratch_shapes=[
                pltpu.VMEM(result.shape, BF16), pltpu.VMEM(result.shape, BF16),
                pltpu.SemaphoreType.DMA((2 * widths[chunk] // tile,)),
            ],
            input_output_aliases=aliases,
            compiler_params=params(),
            cost_estimate=cost(1000, 1000),
            name="finish",
        )(*operands, *last)

    every = range(chunks)
    span = [slice(firsts[k], firsts[k] + widths[k]) for k in every]

    def join(k, level):
        kept, came = held["kept", k, level]
        own_decay, other_decay = held["decay", level]
        sent = flat_shape(k) if level == 2 else pair_shape(k, 2 - level)
        made = (sent, pair_shape(k, max(1, 2 - level)))
        if level == 2 and levels == 1:
            made = made[:1]
        sent, *kept = small(
            functools.partial(join_kernel, span[k], level), made, "join",
            kept, came, own_decay, other_decay,
        )
        kept = kept[0] if kept else None
        held["last"] = (sent,)
        if level == 2:
            held["level", k] = (sent, kept, None, 0)
            send(k)
        else:
            held["kept", k, level + 1] = (kept, swap(sent, 2 << level))

    def parts(k):
        held["block", k], held["sofar"] = block_parts(k, held.get("sofar", ()))
        held["last"] = (held["block", k][6],)

    def taken(k, level):
        pay = held["level", k][0]
        return [lax.ppermute(pay, "seq", perm) for perm in level_perms(level)]

    def send(k):
        held["taken", k] = taken(k, held["level", k][3])

    def climb(k):
        _, both, enter, level = held["level", k]
        came = held["taken", k]
        operands = came + held["others"][:level] + ([enter] if level else [])
        pay, enter = small(
            functools.partial(level_kernel, span[k], level, len(came)),
            (flat_shape(k), pair_shape(k)), "level", *operands, both, held["unit"],
        )
        held["level", k] = (pay, both, enter, level + 1)
        held["last"] = (pay,)
        send(k)

    def top(k):
        kept, came = held["kept", k, 2]
        _, _, enter, level = held["level", k]
        got = held["taken", k]
        operands = got + held["others"][:level] + ([enter] if level else [])
        theirs, mine = small(
            functools.partial(top_kernel, span[k], level, len(got)),
            (pair_shape(k), pair_shape(k)), "top", *operands, kept, came,
            *held["decay", 2],
        )
        held["back", k, 2] = (mine, swap(theirs, 4))
        held["last"] = (theirs,)

    def give_back(k, level):
        mine, back = held["back", k, level + 1]
        kept, came = held["kept", k, level]
        made = pair_shape(k, 4 >> level)
        give, own = small(
            functools.partial(return_kernel, span[k], level), (made, made), "return",
            back, mine, kept, came, *held["decay", level],
        )
        held["back", k, level] = (own, swap(give, 1 << level))
        held["last"] = (give,)

    def end(k):
        own, took = held["back", k, 0]
        blocks = [held["block", i] for i, (owner, _, _) in enumerate(tiles) if owner == k]
        out, din, dquery, dkey, *sums = finish(
            k, blocks, took, own, held["sofar"], held.get("prior", ())
        )
        held["sofar"] = (dquery, dkey)
        held["prior"] = (*sums, out, din)
        held["last"] = (sums[0],)

    decay_other = swap(decay, 1)
    across = swap(decay, 2)
    corner = swap(decay, 3)
    held["decay", 0] = (decay, decay_other)
    chip_decay = decay * decay_other
    chip_other = across * corner
    held["decay", 1] = (chip_decay, chip_other)
    plane_decay = chip_decay * chip_other
    last = ()
    for k in every:
        sent, kept = device_states(k, last)
        held["kept", k, 0] = (kept, swap(sent, 1))
        last = (plane_decay, sent)
    held["last"] = (sent,)
    plane_other = swap(plane_decay, 4)
    held["decay", 2] = (plane_decay, plane_other)
    group = held["unit"] = plane_decay * plane_other
    others = held["others"] = []
    for level in range(levels - 1):
        other = swap(group, 8 << level)
        others.append(other)
        group = group * other

    for name, k in schedule(WIDTHS, TILES, levels):
        if name == "chip":
            join(k, 0)
        elif name == "parts":
            held["last"] += (plane_other,)
            parts(k)
        elif name == "plane":
            join(k, 1)
        elif name == "pair":
            join(k, 2)
        elif name == "climb":
            climb(k)
        elif name == "top":
            top(k)
        elif name == "side":
            give_back(k, 1)
        elif name == "device":
            give_back(k, 0)
        else:
            end(k)
    draw, out, din = held["prior"]
    dquery, dkey = held["sofar"]
    return out, din, draw.T, dkey, dquery


def solution(mesh):
    sequence = P(("groups", "seq"), None)
    return jax.shard_map(
        local,
        mesh=mesh,
        in_specs=(
            sequence, sequence, sequence, sequence, P(), P(), P(("groups", "seq")), sequence,
        ),
        out_specs=(sequence,) * 5,
        check_vma=False,
    )
```

time: 77.3 us -> 69.8 us (0.903)
  the two profiles are of different devices: /device:TPU:9 before, /device:TPU:0 now
where the time goes in v4:
time: 69.8 us; the launch traced here: 69.5 us
  Pallas kernels  32.2 us (46%)
  starting transfers between devices  18.6 us (27%)
  waiting for transfers between devices  17.6 us (25%)
  between operations  1.03 us (1%)
    ppermute x16, waiting for transfers between devices, swap(): return lax.ppermute(value, 'seq', [(i, i ^ bit) for i in range(size)])  15.8 us
    ppermute x16, starting transfers between devices, swap(): return lax.ppermute(value, 'seq', [(i, i ^ bit) for i in range(size)])  15.7 us
    pallas_call x4, Pallas kernels, block_parts(): pl.pallas_call(after(kernel, len(operands), len(last)), out_shape=tuple(o...  15.1 us
    pallas_call x2, Pallas kernels, finish(): pl.pallas_call(after(kernel, len(operands), len(last)), out_shape=(shape(...  8.6 us
    pallas_call x2, Pallas kernels, device_states(): pl.pallas_call(after(kernel, 5, len(last)), out_shape=(pair_shape(chunk,...  5.28 us
    ppermute x2, starting transfers between devices, taken(): return [lax.ppermute(pay, 'seq', perm) for perm in level_perms(level)]  2.94 us
    pallas_call x1, Pallas kernels, local(): pl.pallas_call(functools.partial(prep_kernel, head_size), out_shape=(shap...  2.08 us
    ppermute x2, waiting for transfers between devices, taken(): return [lax.ppermute(pay, 'seq', perm) for perm in level_perms(level)]  1.76 us
  transfers between devices with their start and end apart: 18, of which 9 were waited for; matrix products, arithmetic and copies ran while one was open for 0% of the time, Pallas kernels for 36%

profile of v4, /device:TPU:0, one launch (start us, length us, event | category | flops | bytes accessed | tf_op | source)
XLA Modules:
  0.0 69.5 jit_solution(7680894824960211187)
XLA Ops:
  0.6 2.1 %prep.1 = (bf16[512,162]{1,0:T(8,128)(2,1)S(1)}, bf16[512,256]{1,0:T(8,128)(2,1)S(1)}, bf16[256,512]{1,0:T(8,128)(2,1)S(1)}, f32[8,2560]{1,0:T(8,128)S(1)}, f32[1,2560]{1,0:T(1,128)S(1)}) custom-call(f32[40,512]{1,0:T(8,128)} %bitcast.5, f32[1,40]{1,0:T(1,128)} %bitcast.12, f32[1,40]{1,0:T(1,128)} %bitcast.14, s32[1,512]{1,0:T(1,128)} %bitcast.7, ...), custom_call_target="tpu_custom_call" | custom-call | tf_op jit(solution)/shard_map/prep/pallas_call | solution.py:580
  2.7 2.5 %collective-permute-start.2 = (f32[1,2560]{1,0:T(1,128)S(1)}, f32[1,2560]{1,0:T(1,128)S(1)}, u32[]{:S(2)}, u32[]{:S(2)}) collective-permute-start(f32[1,2560]{1,0:T(1,128)S(1)} %get-tuple-element.83.refs_2_.refs_4_), channel_id=1, source_target_pairs={{0,3},{1,2},{2,1},{3,0},{4,7},{5,6},{6,5},{7,4},{8,11},{9,10},{10,... | collective-permute-start | bytes 30728 | tf_op jit(solution)/shard_map/ppermute | solution.py:630
  5.2 0.6 collective-permute-start.1
  5.9 2.6 %states.2 = (f32[2,64,1280]{2,1,0:T(8,128)S(1)}, f32[2,64,1280]{2,1,0:T(8,128)S(1)}) custom-call(bf16[512,2560]{1,0:T(8,128)(2,1)} %refs_0_.11, bf16[512,2560]{1,0:T(8,128)(2,1)} %refs_1_.11, bf16[512,162]{1,0:T(8,128)(2,1)S(1)} %get-tuple-element.80.refs_2_.refs_17_, bf16[256,512]{1,0:T(8,128)(2,1)S(1)} %get-tuple-element.82.refs_3_, ...), custom_call_target="tpu_custom_call" | custom-call | flops 4000000000 | bytes 1000 | tf_op jit(solution)/shard_map/states/pallas_call | solution.py:619
  8.5 0.6 collective-permute-start.4
  9.1 2.7 %states.3 = (f32[2,64,1280]{2,1,0:T(8,128)S(1)}, f32[2,64,1280]{2,1,0:T(8,128)S(1)}) custom-call(bf16[512,2560]{1,0:T(8,128)(2,1)} %refs_0_.11, bf16[512,2560]{1,0:T(8,128)(2,1)} %refs_1_.11, bf16[512,162]{1,0:T(8,128)(2,1)S(1)} %get-tuple-element.80.refs_2_.refs_17_, bf16[256,512]{1,0:T(8,128)(2,1)S(1)} %get-tuple-element.82.refs_3_, ...), custom_call_target="tpu_custom_call" | custom-call | flops 4000000000 | bytes 1000 | tf_op jit(solution)/shard_map/states/pallas_call | solution.py:619
  12.0 1.8 %collective-permute-start.6 = (f32[2,32,1280]{2,1,0:T(8,128)S(1)}, f32[2,32,1280]{2,1,0:T(8,128)S(1)}, u32[]{:S(2)}, u32[]{:S(2)}) collective-permute-start(f32[2,32,1280]{2,1,0:T(8,128)S(1)} %get-tuple-element.88.refs_4_), channel_id=1, source_target_pairs={{0,2},{1,3},{2,0},{3,1},{4,6},{5,7},{6,4},{7,5},{8,10},{9,11},{10,... | collective-permute-start | bytes 983048 | tf_op jit(solution)/shard_map/ppermute | solution.py:630
  13.8 1.6 %collective-permute-start.5 = (f32[1,2560]{1,0:T(1,128)S(1)}, f32[1,2560]{1,0:T(1,128)S(1)}, u32[]{:S(2)}, u32[]{:S(2)}) collective-permute-start(f32[1,2560]{1,0:T(1,128)S(1)} %get-tuple-element.155.refs_5_.refs_2_.refs_3_), channel_id=1, source_target_pairs={{0,4},{1,5},{2,6},{3,7},{4,0},{5,1},{6,2},{7,3},{8,12},{9,13},{10,... | collective-permute-start | bytes 30728 | tf_op jit(solution)/shard_map/ppermute | solution.py:630
  15.5 0.6 collective-permute-start.7
  16.1 1.4 %collective-permute-done.5.refs_8_.refs_11_.refs_3_.refs_4_ = f32[1,2560]{1,0:T(1,128)S(1)} collective-permute-done((f32[1,2560]{1,0:T(1,128)S(1)}, f32[1,2560]{1,0:T(1,128)S(1)}, u32[]{:S(2)}, u32[]{:S(2)}) %collective-permute-start.5) | collective-permute-done | bytes 10272 | tf_op jit(solution)/shard_map/ppermute | solution.py:630
  17.5 3.3 %block.4 = (f32[512,640]{1,0:T(8,128)S(1)}, f32[512,640]{1,0:T(8,128)S(1)}, bf16[512,640]{1,0:T(8,128)(2,1)S(1)}, bf16[512,640]{1,0:T(8,128)(2,1)S(1)}, bf16[512...) custom-call(bf16[512,2560]{1,0:T(8,128)(2,1)} %refs_0_.11, ...), custom_call_target="tpu_custom_call" | custom-call | flops 1000 | bytes 1000 | tf_op jit(solution)/shard_map/block/pallas_call | solution.py:677
  20.8 3.8 %block.5 = (f32[512,640]{1,0:T(8,128)S(1)}, f32[512,640]{1,0:T(8,128)S(1)}, bf16[512,640]{1,0:T(8,128)(2,1)S(1)}, bf16[512,640]{1,0:T(8,128)(2,1)S(1)}, bf16[512...) custom-call(bf16[512,2560]{1,0:T(8,128)(2,1)} %refs_0_.11, ...), custom_call_target="tpu_custom_call" | custom-call | flops 1000 | bytes 1000 | tf_op jit(solution)/shard_map/block/pallas_call | solution.py:677
  24.6 1.6 %collective-permute-start.8 = (f32[2,16,1280]{2,1,0:T(8,128)S(1)}, f32[2,16,1280]{2,1,0:T(8,128)S(1)}, u32[]{:S(2)}, u32[]{:S(2)}) collective-permute-start(f32[2,16,1280]{2,1,0:T(8,128)S(1)} %get-tuple-element.97.refs_10_), channel_id=1, source_target_pairs={{0,4},{1,5},{2,6},{3,7},{4,0},{5,1},{6,2},{7,3},{8,12},{9,13},{10,... | collective-permute-start | bytes 491528 | tf_op jit(solution)/shard_map/ppermute | solution.py:630
  26.3 4.0 %block.6 = (f32[512,640]{1,0:T(8,128)S(1)}, f32[512,640]{1,0:T(8,128)S(1)}, bf16[512,640]{1,0:T(8,128)(2,1)S(1)}, bf16[512,640]{1,0:T(8,128)(2,1)S(1)}, bf16[512...) custom-call(bf16[512,2560]{1,0:T(8,128)(2,1)} %refs_0_.11, ...), custom_call_target="tpu_custom_call" | custom-call | flops 1000 | bytes 1000 | tf_op jit(solution)/shard_map/block/pallas_call | solution.py:677
  30.3 2.7 %collective-permute-start.10 = (f32[16,1280]{1,0:T(8,128)S(1)}, f32[16,1280]{1,0:T(8,128)S(1)}, u32[]{:S(2)}, u32[]{:S(2)}) collective-permute-start(f32[16,1280]{1,0:T(8,128)S(1)} %join.9.refs_4_), channel_id=1, source_target_pairs={{0,8},{1,9},{2,10},{3,11},{4,12},{5,13},{6,14},{7,15},{8,0},{9,1},... | collective-permute-start | bytes 245768 | tf_op jit(solution)/shard_map/ppermute | solution.py:764
  33.0 1.4 %collective-permute-start.9 = (f32[2,16,1280]{2,1,0:T(8,128)S(1)}, f32[2,16,1280]{2,1,0:T(8,128)S(1)}, u32[]{:S(2)}, u32[]{:S(2)}) collective-permute-start(f32[2,16,1280]{2,1,0:T(8,128)S(1)} %get-tuple-element.109.refs_5_), channel_id=1, source_target_pairs={{0,4},{1,5},{2,6},{3,7},{4,0},{5,1},{6,2},{7,3},{8,12},{9,13},{10,... | collective-permute-start | bytes 491528 | tf_op jit(solution)/shard_map/ppermute | solution.py:630
  34.4 1.4 %collective-permute-done.10.refs_0_ = f32[16,1280]{1,0:T(8,128)S(1)} collective-permute-done((f32[16,1280]{1,0:T(8,128)S(1)}, f32[16,1280]{1,0:T(8,128)S(1)}, u32[]{:S(2)}, u32[]{:S(2)}) %collective-permute-start.10) | collective-permute-done | bytes 81952 | tf_op jit(solution)/shard_map/ppermute | solution.py:764
  35.9 1.4 %collective-permute-start.12 = (f32[2,16,1280]{2,1,0:T(8,128)S(1)}, f32[2,16,1280]{2,1,0:T(8,128)S(1)}, u32[]{:S(2)}, u32[]{:S(2)}) collective-permute-start(f32[2,16,1280]{2,1,0:T(8,128)S(1)} %get-tuple-element.110.refs_4_), channel_id=1, source_target_pairs={{0,4},{1,5},{2,6},{3,7},{4,0},{5,1},{6,2},{7,3},{8,12},{9,13},{10,... | collective-permute-start | bytes 491528 | tf_op jit(solution)/shard_map/ppermute | solution.py:630
  37.2 3.0 %collective-permute-done.9.refs_1_.refs_2_ = f32[2,16,1280]{2,1,0:T(8,128)S(1)} collective-permute-done((f32[2,16,1280]{2,1,0:T(8,128)S(1)}, f32[2,16,1280]{2,1,0:T(8,128)S(1)}, u32[]{:S(2)}, u32[]{:S(2)}) %collective-permute-start.9) | collective-permute-done | bytes 163872 | tf_op jit(solution)/shard_map/ppermute | solution.py:630
  40.5 4.1 %block.7 = (f32[512,640]{1,0:T(8,128)S(1)}, f32[512,640]{1,0:T(8,128)S(1)}, bf16[512,640]{1,0:T(8,128)(2,1)S(1)}, bf16[512,640]{1,0:T(8,128)(2,1)S(1)}, bf16[512...) custom-call(bf16[512,2560]{1,0:T(8,128)(2,1)} %refs_0_.11, ...), custom_call_target="tpu_custom_call" | custom-call | flops 1000 | bytes 1000 | tf_op jit(solution)/shard_map/block/pallas_call | solution.py:677
  44.7 0.7 %collective-permute-start.15 = (f32[2,32,1280]{2,1,0:T(8,128)S(1)}, f32[2,32,1280]{2,1,0:T(8,128)S(1)}, u32[]{:S(2)}, u32[]{:S(2)}) collective-permute-start(f32[2,32,1280]{2,1,0:T(8,128)S(1)} %get-tuple-element.119.refs_5_), channel_id=1, source_target_pairs={{0,2},{1,3},{2,0},{3,1},{4,6},{5,7},{6,4},{7,5},{8,10},{9,11},{10,... | collective-permute-start | bytes 983048 | tf_op jit(solution)/shard_map/ppermute | solution.py:630
  45.4 0.3 collective-permute-done.11.refs_0_
  45.8 1.9 %collective-permute-start.13 = (f32[2,16,1280]{2,1,0:T(8,128)S(1)}, f32[2,16,1280]{2,1,0:T(8,128)S(1)}, u32[]{:S(2)}, u32[]{:S(2)}) collective-permute-start(f32[2,16,1280]{2,1,0:T(8,128)S(1)} %get-tuple-element.120.refs_6_), channel_id=1, source_target_pairs={{0,4},{1,5},{2,6},{3,7},{4,0},{5,1},{6,2},{7,3},{8,12},{9,13},{10,... | collective-permute-start | bytes 491528 | tf_op jit(solution)/shard_map/ppermute | solution.py:630
  47.7 3.5 %collective-permute-done.13.refs_0_ = f32[2,16,1280]{2,1,0:T(8,128)S(1)} collective-permute-done((f32[2,16,1280]{2,1,0:T(8,128)S(1)}, f32[2,16,1280]{2,1,0:T(8,128)S(1)}, u32[]{:S(2)}, u32[]{:S(2)}) %collective-permute-start.13) | collective-permute-done | bytes 163872 | tf_op jit(solution)/shard_map/ppermute | solution.py:630
  51.3 0.6 collective-permute-done.15.refs_0_
  52.1 0.7 %collective-permute-start.14 = (f32[2,32,1280]{2,1,0:T(8,128)S(1)}, f32[2,32,1280]{2,1,0:T(8,128)S(1)}, u32[]{:S(2)}, u32[]{:S(2)}) collective-permute-start(f32[2,32,1280]{2,1,0:T(8,128)S(1)} %get-tuple-element.122.refs_6_), channel_id=1, source_target_pairs={{0,2},{1,3},{2,0},{3,1},{4,6},{5,7},{6,4},{7,5},{8,10},{9,11},{10,... | collective-permute-start | bytes 983048 | tf_op jit(solution)/shard_map/ppermute | solution.py:630
  52.8 1.4 %collective-permute-done.16.refs_14_ = f32[2,64,1280]{2,1,0:T(8,128)S(1)} collective-permute-done((f32[2,64,1280]{2,1,0:T(8,128)S(1)}, f32[2,64,1280]{2,1,0:T(8,128)S(1)}, u32[]{:S(2)}, u32[]{:S(2)}) %collective-permute-start.16) | collective-permute-done | bytes 655392 | tf_op jit(solution)/shard_map/ppermute | solution.py:630
  54.2 4.1 %finish.2 = (bf16[512,2560]{1,0:T(8,128)(2,1)}, bf16[512,2560]{1,0:T(8,128)(2,1)}, f32[512,128]{1,0:T(8,128)S(1)}, f32[512,128]{1,0:T(8,128)S(1)}, f32[2,512,40]{2,1,0:T(8,128)S(1)}, /*index=5*/f32[8,40]{1,0:T(8,128)S(1)}) custom-call(f32[512,640]{1,0:T(8,128)S(1)} %get-tuple-element.124.refs_0_, f32[512,640]{1,0:T(8,128)S(1)} %get-tuple-element.125.refs_1_, ...), custom_call_target="tpu_custom_call" | custom-call | flops 1000 | bytes 1000 | tf_op jit(solution)/shard_map/finish/pallas_call | solution.py:718
  58.3 3.9 %collective-permute-done.14.refs_0_ = f32[2,32,1280]{2,1,0:T(8,128)S(1)} collective-permute-done((f32[2,32,1280]{2,1,0:T(8,128)S(1)}, f32[2,32,1280]{2,1,0:T(8,128)S(1)}, u32[]{:S(2)}, u32[]{:S(2)}) %collective-permute-start.14) | collective-permute-done | bytes 327712 | tf_op jit(solution)/shard_map/ppermute | solution.py:630
  62.2 0.4 return.7
  62.7 2.1 %collective-permute-done.17.refs_14_ = f32[2,64,1280]{2,1,0:T(8,128)S(1)} collective-permute-done((f32[2,64,1280]{2,1,0:T(8,128)S(1)}, f32[2,64,1280]{2,1,0:T(8,128)S(1)}, u32[]{:S(2)}, u32[]{:S(2)}) %collective-permute-start.17) | collective-permute-done | bytes 655392 | tf_op jit(solution)/shard_map/ppermute | solution.py:630
  64.8 4.5 %finish.3 = (bf16[512,2560]{1,0:T(8,128)(2,1)}, bf16[512,2560]{1,0:T(8,128)(2,1)}, bf16[512,128]{1,0:T(8,128)(2,1)}, bf16[512,128]{1,0:T(8,128)(2,1)}, f32[40,512]{1,0:T(8,128)}) custom-call(f32[512,640]{1,0:T(8,128)S(1)} %get-tuple-element.98.refs_0_, f32[512,640]{1,0:T(8,128)S(1)} %get-tuple-element.99.refs_1_, ...), custom_call_target="tpu_custom_call", output_to_operand_aliasing={{0}: (25, {}), {1}: (26, {})} | custom-call | flops 1000 | bytes 1000 | tf_op jit(solution)/shard_map/finish/pallas_call | solution.py:718
  (36 shorter events, 1.4 us)
Async XLA Ops:
  2.7 6.3 %collective-permute-start.2 = (f32[1,2560]{1,0:T(1,128)S(1)}, f32[1,2560]{1,0:T(1,128)S(1)}, u32[]{:S(2)}, u32[]{:S(2)}) collective-permute-start(f32[1,2560]{1,0:T(1,128)S(1)} %get-tuple-element.83.refs_2_.refs_4_), channel_id=1, source_target_pairs={{0,3},{1,2},{2,1},{3,0},{4,7},{5,6},{6,5},{7,4},{8,11},{9,10},{10,... | collective-permute-start | bytes 30728 | tf_op jit(solution)/shard_map/ppermute | solution.py:630
  5.2 3.9 %collective-permute-start.1 = (f32[1,2560]{1,0:T(1,128)S(1)}, f32[1,2560]{1,0:T(1,128)S(1)}, u32[]{:S(2)}, u32[]{:S(2)}) collective-permute-start(f32[1,2560]{1,0:T(1,128)S(1)} %get-tuple-element.83.refs_2_.refs_4_), channel_id=1, source_target_pairs={{0,2},{1,3},{2,0},{3,1},{4,6},{5,7},{6,4},{7,5},{8,10},{9,11},{10,... | collective-permute-start | bytes 30728 | tf_op jit(solution)/shard_map/ppermute | solution.py:630
  5.8 3.2 %collective-permute-start = (f32[1,2560]{1,0:T(1,128)S(1)}, f32[1,2560]{1,0:T(1,128)S(1)}, u32[]{:S(2)}, u32[]{:S(2)}) collective-permute-start(f32[1,2560]{1,0:T(1,128)S(1)} %get-tuple-element.83.refs_2_.refs_4_), channel_id=1, source_target_pairs={{0,1},{1,0},{2,3},{3,2},{4,5},{5,4},{6,7},{7,6},{8,9},{9,8},{10,11... | collective-permute-start | bytes 30728 | tf_op jit(solution)/shard_map/ppermute | solution.py:630
  8.5 3.4 %collective-permute-start.4 = (f32[2,64,1280]{2,1,0:T(8,128)S(1)}, f32[2,64,1280]{2,1,0:T(8,128)S(1)}, u32[]{:S(2)}, u32[]{:S(2)}) collective-permute-start(f32[2,64,1280]{2,1,0:T(8,128)S(1)} %get-tuple-element.84.refs_6_), channel_id=1, source_target_pairs={{0,1},{1,0},{2,3},{3,2},{4,5},{5,4},{6,7},{7,6},{8,9},{9,8},{10,11... | collective-permute-start | bytes 1966088 | tf_op jit(solution)/shard_map/ppermute | solution.py:630
  11.8 3.6 %collective-permute-start.3 = (f32[2,64,1280]{2,1,0:T(8,128)S(1)}, f32[2,64,1280]{2,1,0:T(8,128)S(1)}, u32[]{:S(2)}, u32[]{:S(2)}) collective-permute-start(f32[2,64,1280]{2,1,0:T(8,128)S(1)} %get-tuple-element.86.refs_4_), channel_id=1, source_target_pairs={{0,1},{1,0},{2,3},{3,2},{4,5},{5,4},{6,7},{7,6},{8,9},{9,8},{10,11... | collective-permute-start | bytes 1966088 | tf_op jit(solution)/shard_map/ppermute | solution.py:630
  12.0 12.6 %collective-permute-start.6 = (f32[2,32,1280]{2,1,0:T(8,128)S(1)}, f32[2,32,1280]{2,1,0:T(8,128)S(1)}, u32[]{:S(2)}, u32[]{:S(2)}) collective-permute-start(f32[2,32,1280]{2,1,0:T(8,128)S(1)} %get-tuple-element.88.refs_4_), channel_id=1, source_target_pairs={{0,2},{1,3},{2,0},{3,1},{4,6},{5,7},{6,4},{7,5},{8,10},{9,11},{10,... | collective-permute-start | bytes 983048 | tf_op jit(solution)/shard_map/ppermute | solution.py:630
  13.8 3.7 %collective-permute-start.5 = (f32[1,2560]{1,0:T(1,128)S(1)}, f32[1,2560]{1,0:T(1,128)S(1)}, u32[]{:S(2)}, u32[]{:S(2)}) collective-permute-start(f32[1,2560]{1,0:T(1,128)S(1)} %get-tuple-element.155.refs_5_.refs_2_.refs_3_), channel_id=1, source_target_pairs={{0,4},{1,5},{2,6},{3,7},{4,0},{5,1},{6,2},{7,3},{8,12},{9,13},{10,... | collective-permute-start | bytes 30728 | tf_op jit(solution)/shard_map/ppermute | solution.py:630
  15.4 2.1 %copy-start = (bf16[512,128]{1,0:T(8,128)(2,1)S(1)}, bf16[512,128]{1,0:T(8,128)(2,1)}, u32[]{:S(2)}) copy-start(bf16[512,128]{1,0:T(8,128)(2,1)} %refs_5_.7) | copy-start | bytes 393220
  15.4 2.1 %copy-start.1 = (bf16[512,128]{1,0:T(8,128)(2,1)S(1)}, bf16[512,128]{1,0:T(8,128)(2,1)}, u32[]{:S(2)}) copy-start(bf16[512,128]{1,0:T(8,128)(2,1)} %refs_6_.7) | copy-start | bytes 393220
  15.4 2.1 %copy-start.3 = (s32[512]{0:T(512)S(1)}, s32[512]{0:T(512)}, u32[]{:S(2)}) copy-start(s32[512]{0:T(512)} %param.14) | copy-start | bytes 6148
  15.5 17.5 %collective-permute-start.7 = (f32[2,32,1280]{2,1,0:T(8,128)S(1)}, f32[2,32,1280]{2,1,0:T(8,128)S(1)}, u32[]{:S(2)}, u32[]{:S(2)}) collective-permute-start(f32[2,32,1280]{2,1,0:T(8,128)S(1)} %get-tuple-element.89.refs_7_), channel_id=1, source_target_pairs={{0,2},{1,3},{2,0},{3,1},{4,6},{5,7},{6,4},{7,5},{8,10},{9,11},{10,... | collective-permute-start | bytes 983048 | tf_op jit(solution)/shard_map/ppermute | solution.py:630
  24.6 5.6 %collective-permute-start.8 = (f32[2,16,1280]{2,1,0:T(8,128)S(1)}, f32[2,16,1280]{2,1,0:T(8,128)S(1)}, u32[]{:S(2)}, u32[]{:S(2)}) collective-permute-start(f32[2,16,1280]{2,1,0:T(8,128)S(1)} %get-tuple-element.97.refs_10_), channel_id=1, source_target_pairs={{0,4},{1,5},{2,6},{3,7},{4,0},{5,1},{6,2},{7,3},{8,12},{9,13},{10,... | collective-permute-start | bytes 491528 | tf_op jit(solution)/shard_map/ppermute | solution.py:630
  30.3 5.6 %collective-permute-start.10 = (f32[16,1280]{1,0:T(8,128)S(1)}, f32[16,1280]{1,0:T(8,128)S(1)}, u32[]{:S(2)}, u32[]{:S(2)}) collective-permute-start(f32[16,1280]{1,0:T(8,128)S(1)} %join.9.refs_4_), channel_id=1, source_target_pairs={{0,8},{1,9},{2,10},{3,11},{4,12},{5,13},{6,14},{7,15},{8,0},{9,1},... | collective-permute-start | bytes 245768 | tf_op jit(solution)/shard_map/ppermute | solution.py:764
  33.0 7.2 %collective-permute-start.9 = (f32[2,16,1280]{2,1,0:T(8,128)S(1)}, f32[2,16,1280]{2,1,0:T(8,128)S(1)}, u32[]{:S(2)}, u32[]{:S(2)}) collective-permute-start(f32[2,16,1280]{2,1,0:T(8,128)S(1)} %get-tuple-element.109.refs_5_), channel_id=1, source_target_pairs={{0,4},{1,5},{2,6},{3,7},{4,0},{5,1},{6,2},{7,3},{8,12},{9,13},{10,... | collective-permute-start | bytes 491528 | tf_op jit(solution)/shard_map/ppermute | solution.py:630
  35.9 8.7 %collective-permute-start.12 = (f32[2,16,1280]{2,1,0:T(8,128)S(1)}, f32[2,16,1280]{2,1,0:T(8,128)S(1)}, u32[]{:S(2)}, u32[]{:S(2)}) collective-permute-start(f32[2,16,1280]{2,1,0:T(8,128)S(1)} %get-tuple-element.110.refs_4_), channel_id=1, source_target_pairs={{0,4},{1,5},{2,6},{3,7},{4,0},{5,1},{6,2},{7,3},{8,12},{9,13},{10,... | collective-permute-start | bytes 491528 | tf_op jit(solution)/shard_map/ppermute | solution.py:630
  40.3 5.5 %collective-permute-start.11 = (f32[16,1280]{1,0:T(8,128)S(1)}, f32[16,1280]{1,0:T(8,128)S(1)}, u32[]{:S(2)}, u32[]{:S(2)}) collective-permute-start(f32[16,1280]{1,0:T(8,128)S(1)} %join.11.refs_10_), channel_id=1, source_target_pairs={{0,8},{1,9},{2,10},{3,11},{4,12},{5,13},{6,14},{7,15},{8,0},{9,1},... | collective-permute-start | bytes 245768 | tf_op jit(solution)/shard_map/ppermute | solution.py:764
  44.7 7.1 %collective-permute-start.15 = (f32[2,32,1280]{2,1,0:T(8,128)S(1)}, f32[2,32,1280]{2,1,0:T(8,128)S(1)}, u32[]{:S(2)}, u32[]{:S(2)}) collective-permute-start(f32[2,32,1280]{2,1,0:T(8,128)S(1)} %get-tuple-element.119.refs_5_), channel_id=1, source_target_pairs={{0,2},{1,3},{2,0},{3,1},{4,6},{5,7},{6,4},{7,5},{8,10},{9,11},{10,... | collective-permute-start | bytes 983048 | tf_op jit(solution)/shard_map/ppermute | solution.py:630
  45.8 5.4 %collective-permute-start.13 = (f32[2,16,1280]{2,1,0:T(8,128)S(1)}, f32[2,16,1280]{2,1,0:T(8,128)S(1)}, u32[]{:S(2)}, u32[]{:S(2)}) collective-permute-start(f32[2,16,1280]{2,1,0:T(8,128)S(1)} %get-tuple-element.120.refs_6_), channel_id=1, source_target_pairs={{0,4},{1,5},{2,6},{3,7},{4,0},{5,1},{6,2},{7,3},{8,12},{9,13},{10,... | collective-permute-start | bytes 491528 | tf_op jit(solution)/shard_map/ppermute | solution.py:630
  52.0 2.2 %collective-permute-start.16 = (f32[2,64,1280]{2,1,0:T(8,128)S(1)}, f32[2,64,1280]{2,1,0:T(8,128)S(1)}, u32[]{:S(2)}, u32[]{:S(2)}) collective-permute-start(f32[2,64,1280]{2,1,0:T(8,128)S(1)} %get-tuple-element.137.refs_21_), channel_id=1, source_target_pairs={{0,1},{1,0},{2,3},{3,2},{4,5},{5,4},{6,7},{7,6},{8,9},{9,8},{10,11... | collective-permute-start | bytes 1966088 | tf_op jit(solution)/shard_map/ppermute | solution.py:630
  52.1 10.1 %collective-permute-start.14 = (f32[2,32,1280]{2,1,0:T(8,128)S(1)}, f32[2,32,1280]{2,1,0:T(8,128)S(1)}, u32[]{:S(2)}, u32[]{:S(2)}) collective-permute-start(f32[2,32,1280]{2,1,0:T(8,128)S(1)} %get-tuple-element.122.refs_6_), channel_id=1, source_target_pairs={{0,2},{1,3},{2,0},{3,1},{4,6},{5,7},{6,4},{7,5},{8,10},{9,11},{10,... | collective-permute-start | bytes 983048 | tf_op jit(solution)/shard_map/ppermute | solution.py:630
  62.2 2.5 %copy-start.2 = (f32[512,40]{0,1:T(8,128)S(1)}, f32[512,40]{0,1:T(8,128)}, u32[]{:S(2)}) copy-start(f32[512,40]{0,1:T(8,128)} %param.9) | copy-start | bytes 245764
  62.2 2.5 %copy-start.4 = (f32[40]{0:T(128)S(1)}, f32[40]{0:T(128)}, u32[]{:S(2)}) copy-start(f32[40]{0:T(128)} %param.12) | copy-start | bytes 484
  62.6 2.2 %collective-permute-start.17 = (f32[2,64,1280]{2,1,0:T(8,128)S(1)}, f32[2,64,1280]{2,1,0:T(8,128)S(1)}, u32[]{:S(2)}, u32[]{:S(2)}) collective-permute-start(f32[2,64,1280]{2,1,0:T(8,128)S(1)} %get-tuple-element.143.refs_27_), channel_id=1, source_target_pairs={{0,1},{1,0},{2,3},{3,2},{4,5},{5,4},{6,7},{7,6},{8,9},{9,8},{10,11... | collective-permute-start | bytes 1966088 | tf_op jit(solution)/shard_map/ppermute | solution.py:630

commit v5 on v4

--- a/solution.py
+++ b/solution.py
@@ -9,8 +9,7 @@
 
 WIDTHS = (10, 10)
 TILES = (5, 5)
-SLACK = 1.0
-SMALL_COST = 900_000_000
+SMALL_COST = 1000
 STATES_COST = 4_000_000_000
 VMEM_BYTES = 28 * 1024 * 1024
 
@@ -198,21 +197,66 @@
         put_other(1, own_decay * leaving + own(1))
 
 
-def join_kernel(columns, level, kept_ref, came_ref, own_ref, other_ref, sent_ref, next_ref=None):
+def join_kernel(columns, kept_ref, came_ref, own_ref, other_ref, *results):
+    firsts, _ = place()
+    forward, backward = joined(
+        firsts[0], own_ref[:, columns], other_ref[:, columns], kept_ref, came_ref
+    )
+    quarter = forward.shape[0] // 4
+    for slot, ref in enumerate(results):
+        here = slice(slot * quarter, (slot + 1) * quarter)
+        ref[:quarter] = forward[here]
+        ref[quarter : 2 * quarter] = backward[here]
+        if ref.shape[0] > 2 * quarter:
+            width = ref.shape[1]
+            for chunk in range(own_ref.shape[1] // width):
+                there = slice(chunk * width, (chunk + 1) * width)
+                row = 2 * quarter + chunk
+                ref[row : row + 1, :] = own_ref[:, there] * other_ref[:, there]
+
+
+def four_chips(firsts, row, values, decays):
+    half = decays[0].shape[0] - 8
+    quarter = half // 2
+    return (
+        in_order(firsts, *(ref[half + row : half + row + 1, :] for ref in decays)),
+        in_order(firsts, *(ref[:quarter] for ref in values)),
+        in_order(firsts, *(ref[quarter:half] for ref in values)),
+    )
+
+
+def in_order(firsts, own, side, depth, corner):
+    _, near, low = firsts
+    first, second = jnp.where(near, own, side), jnp.where(near, side, own)
+    third, fourth = jnp.where(near, depth, corner), jnp.where(near, corner, depth)
+    return (
+        jnp.where(low, first, third), jnp.where(low, second, fourth),
+        jnp.where(low, third, first), jnp.where(low, fourth, second),
+    )
+
+
+def for_chips(firsts, values):
+    _, near, low = firsts
+    first, second = jnp.where(low, values[0], values[2]), jnp.where(low, values[1], values[3])
+    third, fourth = jnp.where(low, values[2], values[0]), jnp.where(low, values[3], values[1])
+    return (
+        jnp.where(near, first, second), jnp.where(near, second, first),
+        jnp.where(near, third, fourth), jnp.where(near, fourth, third),
+    )
+
+
+def quad_kernel(row, *refs):
+    values, decays, results = refs[:4], refs[4:8], refs[8:]
     firsts, unit = place()
-    forward, backward = joined(
-        firsts[level], own_ref[:, columns], other_ref[:, columns], kept_ref, came_ref
-    )
-    if level == 2:
-        if next_ref is not None:
-            next_ref[0] = forward
-            next_ref[1] = backward
-        sent_ref[...] = jnp.where((unit & 1) == 1, backward, forward)
-        return
-    half = forward.shape[0] // 2
-    for chain, value in enumerate((forward, backward)):
-        sent_ref[chain] = value[:half]
-        next_ref[chain] = value[half:]
+    decay, states, directs = four_chips(firsts, row, values, decays)
+    forward, backward = states[0], directs[3]
+    for i in (1, 2, 3):
+        forward = decay[i] * forward + states[i]
+        backward = directs[3 - i] + decay[3 - i] * backward
+    results[0][...] = jnp.where((unit & 1) == 1, backward, forward)
+    if len(results) > 1:
+        results[1][0] = forward
+        results[1][1] = backward
 
 
 def absorb(columns, level, plane, taken_refs, others, enter_ref):
@@ -262,35 +306,32 @@
         pay_ref[...] = decay * entering + both_ref[0]
 
 
-def top_kernel(columns, level, taken_count, *refs):
+def top_kernel(columns, row, level, taken_count, *refs):
     taken, refs = refs[:taken_count], refs[taken_count:]
     others, refs = refs[:level], refs[level:]
     enter_ref = None
     if level:
         enter_ref, refs = refs[0], refs[1:]
-    kept_ref, came_ref, own_ref, other_ref, theirs_ref, mine_ref = refs
-    firsts, plane = place()
-    entering, leaving = absorb(columns, level, plane, taken, others, enter_ref)
-
-    def put_own(chain, value):
-        mine_ref[chain] = value
-
-    def put_other(chain, value):
-        theirs_ref[chain] = value
-
-    split_pair(
-        firsts[2], own_ref[:, columns], other_ref[:, columns], lambda i: kept_ref[i],
-        lambda i: came_ref[i], entering, leaving, put_own, put_other,
-    )
-
-
-def return_kernel(
-    columns, level, back_ref, mine_ref, kept_ref, came_ref, own_ref, other_ref, give_ref, stay_ref
-):
-    first = place()[0][level]
-    half = back_ref.shape[1]
-    for slot, source in enumerate((back_ref, mine_ref)):
-        here = slice(slot * half, (slot + 1) * half)
+    values, decays, results = refs[:4], refs[4:8], refs[8:]
+    firsts, unit = place()
+    entering, leaving = absorb(columns, level, unit, taken, others, enter_ref)
+    decay, states, directs = four_chips(firsts, row, values, decays)
+    enters, leaves = [entering], [leaving]
+    for i in (0, 1, 2):
+        enters.append(decay[i] * enters[-1] + states[i])
+        leaves.append(decay[3 - i] * leaves[-1] + directs[3 - i])
+    for chain, value in enumerate((enters, leaves[::-1])):
+        for ref, part in zip(results, for_chips(firsts, value)):
+            ref[chain] = part
+
+
+def return_kernel(columns, *refs):
+    sources = refs[:4]
+    kept_ref, came_ref, own_ref, other_ref, give_ref, stay_ref = refs[4:]
+    first = place()[0][0]
+    quarter = sources[0].shape[1]
+    for slot, source in enumerate(sources):
+        here = slice(slot * quarter, (slot + 1) * quarter)
 
         def put_own(chain, value, here=here):
             stay_ref[chain, here] = value
@@ -412,20 +453,20 @@
     head_count, head_size, first_column, tile, pieces, prior, final, *refs,
 ):
     blocks = [refs[7 * i : 7 * i + 7] for i in range(pieces)]
-    (took_ref, own_ref, rows_ref, heads_ref, maps_ref, dquery_in, dkey_in) = refs[
-        7 * pieces : 7 * pieces + 7
-    ]
-    refs = refs[7 * pieces + 7 :]
+    (took_ref, own_ref, rows_ref, heads_ref, maps_ref) = refs[7 * pieces : 7 * pieces + 5]
+    refs = refs[7 * pieces + 5 :]
     if final:
-        (raw_ref, rate_ref), refs = refs[:2], refs[2:]
+        (dquery_in, dkey_in, raw_ref, rate_ref), refs = refs[:4], refs[4:]
     if prior:
-        (sums_in, edge_in), refs = refs[:2], refs[4:]
+        (sums_in, edge_in, dlead_in, dtail_in), refs = refs[:4], refs[6:]
     out_hbm, din_hbm, dquery_ref, dkey_ref, *results, out_ref, din_ref, sems = refs
-    rows, state_size = dquery_in.shape
+    state_size = maps_ref.shape[1] // 2
+    rows = heads_ref.shape[0]
     firsts, _ = place()
     rise = sink = edge = dlead = dtail = None
     if prior:
         rise, sink, edge = sums_in[0], sums_in[1], edge_in[...]
+        dlead, dtail = dlead_in[...], dtail_in[...]
     copies = []
     for i, block in enumerate(blocks):
         local_out_ref, local_din_ref, grown_ref, fallen_ref, grow_ref, fall_ref, sums_ref = block
@@ -464,11 +505,11 @@
         edge = edge_now if edge is None else edge + edge_now
         dlead = dlead_now if dlead is None else dlead + dlead_now
         dtail = dtail_now if dtail is None else dtail + dtail_now
-    in_lead = heads_ref[:, 4 * head_count : 4 * head_count + 1].astype(F32) > 0.5
-    in_tail = heads_ref[:, 4 * head_count + 1 : 4 * head_count + 2].astype(F32) > 0.5
-    dquery_ref[...] = (dquery_in[...] + jnp.where(in_lead, dlead, 0.0)).astype(dquery_ref.dtype)
-    dkey_ref[...] = (dkey_in[...] + jnp.where(in_tail, dtail, 0.0)).astype(dkey_ref.dtype)
     if final:
+        in_lead = heads_ref[:, 4 * head_count : 4 * head_count + 1].astype(F32) > 0.5
+        in_tail = heads_ref[:, 4 * head_count + 1 : 4 * head_count + 2].astype(F32) > 0.5
+        dquery_ref[...] = (dquery_in[...] + jnp.where(in_lead, dlead, 0.0)).astype(BF16)
+        dkey_ref[...] = (dkey_in[...] + jnp.where(in_tail, dtail, 0.0)).astype(BF16)
         lower = triangle(rows, True).astype(F32).astype(BF16)
         sink_turned = sink.T
         later = sum_dot_left(rise.T - sink_turned, lower) + edge.T[:, :1]
@@ -476,6 +517,8 @@
         rate = jnp.broadcast_to(rate_ref[...], (8, head_count)).T[:, :1]
         results[0][...] = (sink_turned / softplus(raw) - rate * later) / (1.0 + jnp.exp(-raw))
     else:
+        dquery_ref[...] = dlead
+        dkey_ref[...] = dtail
         results[0][0] = rise
         results[0][1] = sink
         results[1][...] = edge
@@ -483,52 +526,15 @@
         copy.wait()
 
 
-def schedule(widths, tiles, levels):
-    total = sum(widths)
-    chunks = len(widths)
-    pieces = [tile for width, tile in zip(widths, tiles) for _ in range(width // tile)]
-    middle = ["climb"] * (levels - 1)
-    stages = ["chip", "plane", "pair"] + middle + ["top", "side", "device", "end"]
-    moves = [15.6, 7.8] + [5.8] * levels + [7.8, 15.6, 3.0, 0.0]
-    links = ["side", "low"] + ["high"] * levels + ["low", "side", "core", None]
-    at = [0] * chunks
-    ready = [3.0 + 0.3 * k for k in range(chunks)]
-    free = {}
-    now, blocks, order, ended = 3.0, 0, [], 0
-    while ended < chunks:
-        chain = [k for k in range(chunks) if at[k] < len(stages) - 1]
-        soon = min(chain, key=lambda k: (ready[k], -at[k]), default=None)
-        work = 11.0 * widths[ended] / total
-        left = blocks < len(pieces)
-        block = 11.5 * pieces[blocks] / total if left else 0.0
-        can_end = at[ended] == len(stages) - 1 and not left
-        fits = soon is not None and now + block <= ready[soon] + SLACK
-        if left and min(at) > 0 and (fits or soon is None):
-            order.append(("parts", blocks))
-            now += block
-            blocks += 1
-            continue
-        if soon is None:
-            pick = ended
-        elif can_end and max(now, ready[ended]) + work <= ready[soon] + 3.0:
-            pick = ended
-        else:
-            pick = soon
-        now = max(now, ready[pick])
-        stage = stages[at[pick]]
-        order.append((stage, pick))
-        if stage == "end":
-            now += work
-            ended += 1
-            at[pick] += 1
-            continue
-        now += 1.6
-        link = links[at[pick]]
-        begin = max(now, free.get(link, 0.0))
-        free[link] = begin + moves[at[pick]] * widths[pick] / total
-        ready[pick] = free[link] + 0.5
-        at[pick] += 1
-    return order
+def schedule(levels):
+    climbs = [("climb", k) for _ in range(levels - 1) for k in (0, 1)]
+    middle = [("top", 0), ("quad", 1)]
+    if climbs:
+        middle = [("quad", 1), *climbs, ("top", 0)]
+    return [
+        ("join", 0), ("parts", 0), ("join", 1), ("quad", 0), ("parts", 1), *middle, ("parts", 2),
+        ("top", 1), ("device", 0), ("end", 0), ("parts", 3), ("device", 1), ("end", 1),
+    ]
 
 
 def params():
@@ -697,15 +703,15 @@
         last = held["last"]
         final = chunk == chunks - 1
         operands = [value for block in blocks for value in block]
-        operands += [took, own, wide_rows, heads, maps, *grads]
+        operands += [took, own, wide_rows, heads, maps]
         if final:
-            operands += [raw_turned, rate_row]
+            operands += [*grads, raw_turned, rate_row]
         in_specs = [NEAR] * len(operands)
         aliases = {}
         if prior:
-            aliases = {len(operands) + 2: 0, len(operands) + 3: 1}
+            aliases = {len(operands) + 4: 0, len(operands) + 5: 1}
             operands += list(prior)
-            in_specs += [NEAR, NEAR, ANY, ANY]
+            in_specs += [NEAR] * 4 + [ANY, ANY]
         kind = BF16 if final else F32
         ends = [shape((head_count, rows))]
         if not final:
@@ -736,24 +742,33 @@
     every = range(chunks)
     span = [slice(firsts[k], firsts[k] + widths[k]) for k in every]
 
-    def join(k, level):
-        kept, came = held["kept", k, level]
-        own_decay, other_decay = held["decay", level]
-        sent = flat_shape(k) if level == 2 else pair_shape(k, 2 - level)
-        made = (sent, pair_shape(k, max(1, 2 - level)))
-        if level == 2 and levels == 1:
-            made = made[:1]
-        sent, *kept = small(
-            functools.partial(join_kernel, span[k], level), made, "join",
-            kept, came, own_decay, other_decay,
-        )
-        kept = kept[0] if kept else None
-        held["last"] = (sent,)
-        if level == 2:
-            held["level", k] = (sent, kept, None, 0)
-            send(k)
-        else:
-            held["kept", k, level + 1] = (kept, swap(sent, 2 << level))
+    def join(k):
+        kept, came = held["kept", k]
+        part = shape((2 * eighth + (8 if k == 0 else 0), widths[k]))
+        corner, side, depth, stay = small(
+            functools.partial(join_kernel, span[k]), (part,) * 4, "join",
+            kept, came, decay, decay_other,
+        )
+        held["last"] = (side,)
+        held["four", k] = (stay, swap(side, 2), swap(depth, 4), swap(corner, 6))
+
+    def quad(k):
+        made = (flat_shape(k),) + ((pair_shape(k),) if levels > 1 else ())
+        pay, *both = small(
+            functools.partial(quad_kernel, k), made, "quad", *held["four", k], *held["four", 0],
+        )
+        held["last"] = (pay,)
+        held["level", k] = (pay, both[0] if both else None, None, 0)
+        if k == 0 and levels > 1:
+            rows_of = [value[2 * eighth : 2 * eighth + chunks] for value in held["four", 0]]
+            group = functools.reduce(jnp.multiply, rows_of).reshape(1, channels)
+            held["unit"] = group
+            others = held["others"] = []
+            for level in range(levels - 1):
+                other = swap(group, 8 << level)
+                others.append(other)
+                group = group * other
+        send(k)
 
     def parts(k):
         held["block", k], held["sofar"] = block_parts(k, held.get("sofar", ()))
@@ -779,84 +794,49 @@
         send(k)
 
     def top(k):
-        kept, came = held["kept", k, 2]
         _, _, enter, level = held["level", k]
         got = held["taken", k]
         operands = got + held["others"][:level] + ([enter] if level else [])
-        theirs, mine = small(
-            functools.partial(top_kernel, span[k], level, len(got)),
-            (pair_shape(k), pair_shape(k)), "top", *operands, kept, came,
-            *held["decay", 2],
-        )
-        held["back", k, 2] = (mine, swap(theirs, 4))
-        held["last"] = (theirs,)
-
-    def give_back(k, level):
-        mine, back = held["back", k, level + 1]
-        kept, came = held["kept", k, level]
-        made = pair_shape(k, 4 >> level)
+        mine, side, depth, corner = small(
+            functools.partial(top_kernel, span[k], k, level, len(got)), (pair_shape(k),) * 4, "top",
+            *operands, *held["four", k], *held["four", 0],
+        )
+        held["back", k] = (swap(corner, 6), swap(side, 2), swap(depth, 4), mine)
+        held["last"] = (mine,)
+
+    def device(k):
+        kept, came = held["kept", k]
+        made = pair_shape(k, 4)
         give, own = small(
-            functools.partial(return_kernel, span[k], level), (made, made), "return",
-            back, mine, kept, came, *held["decay", level],
-        )
-        held["back", k, level] = (own, swap(give, 1 << level))
+            functools.partial(return_kernel, span[k]), (made, made), "return",
+            *held["back", k], kept, came, decay, decay_other,
+        )
+        held["final", k] = (own, swap(give, 1))
         held["last"] = (give,)
 
     def end(k):
-        own, took = held["back", k, 0]
+        own, took = held["final", k]
         blocks = [held["block", i] for i, (owner, _, _) in enumerate(tiles) if owner == k]
         out, din, dquery, dkey, *sums = finish(
             k, blocks, took, own, held["sofar"], held.get("prior", ())
         )
-        held["sofar"] = (dquery, dkey)
-        held["prior"] = (*sums, out, din)
+        held["prior"] = (*sums, dquery, dkey, out, din)
         held["last"] = (sums[0],)
 
     decay_other = swap(decay, 1)
-    across = swap(decay, 2)
-    corner = swap(decay, 3)
-    held["decay", 0] = (decay, decay_other)
-    chip_decay = decay * decay_other
-    chip_other = across * corner
-    held["decay", 1] = (chip_decay, chip_other)
-    plane_decay = chip_decay * chip_other
-    last = ()
     for k in every:
-        sent, kept = device_states(k, last)
-        held["kept", k, 0] = (kept, swap(sent, 1))
-        last = (plane_decay, sent)
-    held["last"] = (sent,)
-    plane_other = swap(plane_decay, 4)
-    held["decay", 2] = (plane_decay, plane_other)
-    group = held["unit"] = plane_decay * plane_other
-    others = held["others"] = []
-    for level in range(levels - 1):
-        other = swap(group, 8 << level)
-        others.append(other)
-        group = group * other
-
-    for name, k in schedule(WIDTHS, TILES, levels):
-        if name == "chip":
-            join(k, 0)
-        elif name == "parts":
-            held["last"] += (plane_other,)
-            parts(k)
-        elif name == "plane":
-            join(k, 1)
-        elif name == "pair":
-            join(k, 2)
-        elif name == "climb":
-            climb(k)
-        elif name == "top":
-            top(k)
-        elif name == "side":
-            give_back(k, 1)
-        elif name == "device":
-            give_back(k, 0)
-        else:
-            end(k)
-    draw, out, din = held["prior"]
-    dquery, dkey = held["sofar"]
+        sent, kept = device_states(k, (decay_other, held["last"][0]) if k else ())
+        held["kept", k] = (kept, swap(sent, 1))
+        held["last"] = (sent,)
+    held["others"] = []
+
+    steps = {
+        "join": join, "parts": parts, "quad": quad, "climb": climb, "top": top,
+        "device": device, "end": end,
+    }
+    for name, k in schedule(levels):
+        steps[name](k)
+    draw, dquery, dkey, out, din = held["prior"]
     return out, din, draw.T, dkey, dquery
 
 

time: 69.8 us -> 64.2 us (0.920)
  waiting for transfers between devices: 17.6 us -> 8.77 us
  starting transfers between devices: 18.6 us -> 21.1 us
  Pallas kernels: 32.2 us -> 33 us
    ppermute x16 -> x17, waiting for transfers between devices: 15.8 us -> 7.3 us  [swap(): return lax.ppermute(value, 'seq', [(i, i ^ bit) for i in range(size)])]
    ppermute x2, starting transfers between devices: 2.94 us -> 4.55 us  [taken(): return [lax.ppermute(pay, 'seq', perm) for perm in level_perms(level)]]
    ppermute x16 -> x17, starting transfers between devices: 15.7 us -> 16.5 us  [swap(): return lax.ppermute(value, 'seq', [(i, i ^ bit) for i in range(size)])]
  transfers between devices with their start and end apart: 18 -> 19, of which waited for: 9 -> 4; matrix products, arithmetic and copies ran while one was open for 0% -> 0% of each run, Pallas kernels for 36% -> 40%
where the time goes in v5:
time: 64.2 us; the launch traced here: 63.9 us
  Pallas kernels  33 us (51%)
  starting transfers between devices  21.1 us (33%)
  waiting for transfers between devices  8.77 us (14%)
  between operations  1.05 us (2%)
    ppermute x17, starting transfers between devices, swap(): return lax.ppermute(value, 'seq', [(i, i ^ bit) for i in range(size)])  16.5 us
    pallas_call x4, Pallas kernels, block_parts(): pl.pallas_call(after(kernel, len(operands), len(last)), out_shape=tuple(o...  15.3 us
    pallas_call x2, Pallas kernels, finish(): pl.pallas_call(after(kernel, len(operands), len(last)), out_shape=(shape(...  9.13 us
    ppermute x17, waiting for transfers between devices, swap(): return lax.ppermute(value, 'seq', [(i, i ^ bit) for i in range(size)])  7.3 us
    pallas_call x2, Pallas kernels, device_states(): pl.pallas_call(after(kernel, 5, len(last)), out_shape=(pair_shape(chunk,...  5.31 us
    ppermute x2, starting transfers between devices, taken(): return [lax.ppermute(pay, 'seq', perm) for perm in level_perms(level)]  4.55 us
    pallas_call x1, Pallas kernels, local(): pl.pallas_call(functools.partial(prep_kernel, head_size), out_shape=(shap...  2.08 us
    ppermute x2, waiting for transfers between devices, taken(): return [lax.ppermute(pay, 'seq', perm) for perm in level_perms(level)]  1.47 us
  transfers between devices with their start and end apart: 19, of which 4 were waited for; matrix products, arithmetic and copies ran while one was open for 0% of the time, Pallas kernels for 40%

profile of v5, /device:TPU:0, one launch (start us, length us, event | category | flops | bytes accessed | tf_op | source)
XLA Modules:
  0.0 63.9 jit_solution(616022283676914006)
XLA Ops:
  0.6 2.1 %prep.1 = (bf16[512,162]{1,0:T(8,128)(2,1)S(1)}, bf16[512,256]{1,0:T(8,128)(2,1)S(1)}, bf16[256,512]{1,0:T(8,128)(2,1)S(1)}, f32[8,2560]{1,0:T(8,128)S(1)}, f32[1,2560]{1,0:T(1,128)S(1)}) custom-call(f32[40,512]{1,0:T(8,128)} %bitcast.5, f32[1,40]{1,0:T(1,128)} %bitcast.12, f32[1,40]{1,0:T(1,128)} %bitcast.14, s32[1,512]{1,0:T(1,128)} %bitcast.7, ...), custom_call_target="tpu_custom_call" | custom-call | tf_op jit(solution)/shard_map/prep/pallas_call | solution.py:586
  2.7 0.5 collective-permute-start.1
  3.2 2.6 %states.2 = (f32[2,64,1280]{2,1,0:T(8,128)S(1)}, f32[2,64,1280]{2,1,0:T(8,128)S(1)}) custom-call(bf16[512,2560]{1,0:T(8,128)(2,1)} %refs_0_.11, bf16[512,2560]{1,0:T(8,128)(2,1)} %refs_1_.11, bf16[512,162]{1,0:T(8,128)(2,1)S(1)} %get-tuple-element.80.refs_2_.refs_17_, bf16[256,512]{1,0:T(8,128)(2,1)S(1)} %get-tuple-element.82.refs_3_, ...), custom_call_target="tpu_custom_call" | custom-call | flops 4000000000 | bytes 1000 | tf_op jit(solution)/shard_map/states/pallas_call | solution.py:625
  6.0 2.7 %states.3 = (f32[2,64,1280]{2,1,0:T(8,128)S(1)}, f32[2,64,1280]{2,1,0:T(8,128)S(1)}) custom-call(bf16[512,2560]{1,0:T(8,128)(2,1)} %refs_0_.11, bf16[512,2560]{1,0:T(8,128)(2,1)} %refs_1_.11, bf16[512,162]{1,0:T(8,128)(2,1)S(1)} %get-tuple-element.80.refs_2_.refs_17_, bf16[256,512]{1,0:T(8,128)(2,1)S(1)} %get-tuple-element.82.refs_3_, ...), custom_call_target="tpu_custom_call" | custom-call | flops 4000000000 | bytes 1000 | tf_op jit(solution)/shard_map/states/pallas_call | solution.py:625
  8.7 0.5 collective-permute-start.5
  9.3 2.7 %collective-permute-start.3 = (f32[40,1280]{1,0:T(8,128)S(1)}, f32[40,1280]{1,0:T(8,128)S(1)}, u32[]{:S(2)}, u32[]{:S(2)}) collective-permute-start(f32[40,1280]{1,0:T(8,128)S(1)} %get-tuple-element.92), channel_id=1, source_target_pairs={{0,4},{1,5},{2,6},{3,7},{4,0},{5,1},{6,2},{7,3},{8,12},{9,13},{10,... | collective-permute-start | bytes 614408 | tf_op jit(solution)/shard_map/ppermute | solution.py:636
  12.0 1.4 %collective-permute-start.4 = (f32[40,1280]{1,0:T(8,128)S(1)}, f32[40,1280]{1,0:T(8,128)S(1)}, u32[]{:S(2)}, u32[]{:S(2)}) collective-permute-start(f32[40,1280]{1,0:T(8,128)S(1)} %get-tuple-element.93), channel_id=1, source_target_pairs={{0,6},{1,7},{2,4},{3,5},{4,2},{5,3},{6,0},{7,1},{8,14},{9,15},{10,... | collective-permute-start | bytes 614408 | tf_op jit(solution)/shard_map/ppermute | solution.py:636
  13.4 0.1 collective-permute-start.2
  13.6 3.3 %block.4 = (f32[512,640]{1,0:T(8,128)S(1)}, f32[512,640]{1,0:T(8,128)S(1)}, bf16[512,640]{1,0:T(8,128)(2,1)S(1)}, bf16[512,640]{1,0:T(8,128)(2,1)S(1)}, bf16[512...) custom-call(bf16[512,2560]{1,0:T(8,128)(2,1)} %refs_0_.11, ...), custom_call_target="tpu_custom_call" | custom-call | flops 1000 | bytes 1000 | tf_op jit(solution)/shard_map/block/pallas_call | solution.py:683
  17.0 2.0 %collective-permute-start.7 = (f32[32,1280]{1,0:T(8,128)S(1)}, f32[32,1280]{1,0:T(8,128)S(1)}, u32[]{:S(2)}, u32[]{:S(2)}) collective-permute-start(f32[32,1280]{1,0:T(8,128)S(1)} %get-tuple-element.99), channel_id=1, source_target_pairs={{0,4},{1,5},{2,6},{3,7},{4,0},{5,1},{6,2},{7,3},{8,12},{9,13},{10,... | collective-permute-start | bytes 491528 | tf_op jit(solution)/shard_map/ppermute | solution.py:636
  19.0 1.4 %collective-permute-start.8 = (f32[32,1280]{1,0:T(8,128)S(1)}, f32[32,1280]{1,0:T(8,128)S(1)}, u32[]{:S(2)}, u32[]{:S(2)}) collective-permute-start(f32[32,1280]{1,0:T(8,128)S(1)} %get-tuple-element.100), channel_id=1, source_target_pairs={{0,6},{1,7},{2,4},{3,5},{4,2},{5,3},{6,0},{7,1},{8,14},{9,15},{10,... | collective-permute-start | bytes 491528 | tf_op jit(solution)/shard_map/ppermute | solution.py:636
  20.4 0.1 collective-permute-start.6
  20.6 3.1 %collective-permute-done.4.refs_3_.refs_7_.refs_4_.refs_8_ = f32[40,1280]{1,0:T(8,128)S(1)} collective-permute-done((f32[40,1280]{1,0:T(8,128)S(1)}, f32[40,1280]{1,0:T(8,128)S(1)}, u32[]{:S(2)}, u32[]{:S(2)}) %collective-permute-start.4) | collective-permute-done | bytes 204832 | tf_op jit(solution)/shard_map/ppermute | solution.py:636
  23.7 2.1 %collective-permute-done.2.refs_1_.refs_5_.refs_2_.refs_6_ = f32[40,1280]{1,0:T(8,128)S(1)} collective-permute-done((f32[40,1280]{1,0:T(8,128)S(1)}, f32[40,1280]{1,0:T(8,128)S(1)}, u32[]{:S(2)}, u32[]{:S(2)}) %collective-permute-start.2) | collective-permute-done | bytes 204832 | tf_op jit(solution)/shard_map/ppermute | solution.py:636
  25.9 2.7 %collective-permute-start.9 = (f32[16,1280]{1,0:T(8,128)S(1)}, f32[16,1280]{1,0:T(8,128)S(1)}, u32[]{:S(2)}, u32[]{:S(2)}) collective-permute-start(f32[16,1280]{1,0:T(8,128)S(1)} %quad.2.refs_10_), channel_id=1, source_target_pairs={{0,8},{1,9},{2,10},{3,11},{4,12},{5,13},{6,14},{7,15},{8,0},{9,1},... | collective-permute-start | bytes 245768 | tf_op jit(solution)/shard_map/ppermute | solution.py:779
  28.5 3.8 %block.5 = (f32[512,640]{1,0:T(8,128)S(1)}, f32[512,640]{1,0:T(8,128)S(1)}, bf16[512,640]{1,0:T(8,128)(2,1)S(1)}, bf16[512,640]{1,0:T(8,128)(2,1)S(1)}, bf16[512...) custom-call(bf16[512,2560]{1,0:T(8,128)(2,1)} %refs_0_.11, ...), custom_call_target="tpu_custom_call" | custom-call | flops 1000 | bytes 1000 | tf_op jit(solution)/shard_map/block/pallas_call | solution.py:683
  32.4 0.2 top.2
  32.5 2.4 %collective-permute-start.10 = (f32[2,16,1280]{2,1,0:T(8,128)S(1)}, f32[2,16,1280]{2,1,0:T(8,128)S(1)}, u32[]{:S(2)}, u32[]{:S(2)}) collective-permute-start(f32[2,16,1280]{2,1,0:T(8,128)S(1)} %get-tuple-element.123), channel_id=1, source_target_pairs={{0,6},{1,7},{2,4},{3,5},{4,2},{5,3},{6,0},{7,1},{8,14},{9,15},{10,... | collective-permute-start | bytes 491528 | tf_op jit(solution)/shard_map/ppermute | solution.py:636
  34.9 0.7 %collective-permute-start.11 = (f32[2,16,1280]{2,1,0:T(8,128)S(1)}, f32[2,16,1280]{2,1,0:T(8,128)S(1)}, u32[]{:S(2)}, u32[]{:S(2)}) collective-permute-start(f32[2,16,1280]{2,1,0:T(8,128)S(1)} %get-tuple-element.124), channel_id=1, source_target_pairs={{0,2},{1,3},{2,0},{3,1},{4,6},{5,7},{6,4},{7,5},{8,10},{9,11},{10,... | collective-permute-start | bytes 491528 | tf_op jit(solution)/shard_map/ppermute | solution.py:636
  35.6 0.4 collective-permute-start.12
  36.2 1.9 %collective-permute-start.13 = (f32[16,1280]{1,0:T(8,128)S(1)}, f32[16,1280]{1,0:T(8,128)S(1)}, u32[]{:S(2)}, u32[]{:S(2)}) collective-permute-start(f32[16,1280]{1,0:T(8,128)S(1)} %quad.3.refs_10_), channel_id=1, source_target_pairs={{0,8},{1,9},{2,10},{3,11},{4,12},{5,13},{6,14},{7,15},{8,0},{9,1},... | collective-permute-start | bytes 245768 | tf_op jit(solution)/shard_map/ppermute | solution.py:779
  38.1 4.0 %block.6 = (f32[512,640]{1,0:T(8,128)S(1)}, f32[512,640]{1,0:T(8,128)S(1)}, bf16[512,640]{1,0:T(8,128)(2,1)S(1)}, bf16[512,640]{1,0:T(8,128)(2,1)S(1)}, bf16[512...) custom-call(bf16[512,2560]{1,0:T(8,128)(2,1)} %refs_0_.11, ...), custom_call_target="tpu_custom_call" | custom-call | flops 1000 | bytes 1000 | tf_op jit(solution)/shard_map/block/pallas_call | solution.py:683
  42.1 1.5 %collective-permute-done.13.refs_0_ = f32[16,1280]{1,0:T(8,128)S(1)} collective-permute-done((f32[16,1280]{1,0:T(8,128)S(1)}, f32[16,1280]{1,0:T(8,128)S(1)}, u32[]{:S(2)}, u32[]{:S(2)}) %collective-permute-start.13) | collective-permute-done | bytes 81952 | tf_op jit(solution)/shard_map/ppermute | solution.py:779
  43.6 0.2 top.3
  43.7 0.1 return.2
  44.0 1.9 %collective-permute-start.15 = (f32[2,16,1280]{2,1,0:T(8,128)S(1)}, f32[2,16,1280]{2,1,0:T(8,128)S(1)}, u32[]{:S(2)}, u32[]{:S(2)}) collective-permute-start(f32[2,16,1280]{2,1,0:T(8,128)S(1)} %get-tuple-element.138), channel_id=1, source_target_pairs={{0,6},{1,7},{2,4},{3,5},{4,2},{5,3},{6,0},{7,1},{8,14},{9,15},{10,... | collective-permute-start | bytes 491528 | tf_op jit(solution)/shard_map/ppermute | solution.py:636
  45.9 2.0 %collective-permute-start.16 = (f32[2,16,1280]{2,1,0:T(8,128)S(1)}, f32[2,16,1280]{2,1,0:T(8,128)S(1)}, u32[]{:S(2)}, u32[]{:S(2)}) collective-permute-start(f32[2,16,1280]{2,1,0:T(8,128)S(1)} %get-tuple-element.139), channel_id=1, source_target_pairs={{0,2},{1,3},{2,0},{3,1},{4,6},{5,7},{6,4},{7,5},{8,10},{9,11},{10,... | collective-permute-start | bytes 491528 | tf_op jit(solution)/shard_map/ppermute | solution.py:636
  47.9 4.5 %finish.2 = (bf16[512,2560]{1,0:T(8,128)(2,1)}, bf16[512,2560]{1,0:T(8,128)(2,1)}, f32[512,128]{1,0:T(8,128)S(1)}, f32[512,128]{1,0:T(8,128)S(1)}, f32[2,512,40]{2,1,0:T(8,128)S(1)}, /*index=5*/f32[8,40]{1,0:T(8,128)S(1)}) custom-call(f32[512,640]{1,0:T(8,128)S(1)} %get-tuple-element.111.refs_0_, f32[512,640]{1,0:T(8,128)S(1)} %get-tuple-element.112.refs_1_, ...), custom_call_target="tpu_custom_call" | custom-call | flops 1000 | bytes 1000 | tf_op jit(solution)/shard_map/finish/pallas_call | solution.py:724
  52.4 4.1 %block.7 = (f32[512,640]{1,0:T(8,128)S(1)}, f32[512,640]{1,0:T(8,128)S(1)}, bf16[512,640]{1,0:T(8,128)(2,1)S(1)}, bf16[512,640]{1,0:T(8,128)(2,1)S(1)}, bf16[512...) custom-call(bf16[512,2560]{1,0:T(8,128)(2,1)} %refs_0_.11, ...), custom_call_target="tpu_custom_call" | custom-call | flops 1000 | bytes 1000 | tf_op jit(solution)/shard_map/block/pallas_call | solution.py:683
  56.6 0.4 return.3
  57.0 2.1 %collective-permute-done.18.refs_14_ = f32[2,64,1280]{2,1,0:T(8,128)S(1)} collective-permute-done((f32[2,64,1280]{2,1,0:T(8,128)S(1)}, f32[2,64,1280]{2,1,0:T(8,128)S(1)}, u32[]{:S(2)}, u32[]{:S(2)}) %collective-permute-start.18) | collective-permute-done | bytes 655392 | tf_op jit(solution)/shard_map/ppermute | solution.py:636
  59.1 4.6 %finish.3 = (bf16[512,2560]{1,0:T(8,128)(2,1)}, bf16[512,2560]{1,0:T(8,128)(2,1)}, bf16[512,128]{1,0:T(8,128)(2,1)}, bf16[512,128]{1,0:T(8,128)(2,1)}, f32[40,512]{1,0:T(8,128)}) custom-call(f32[512,640]{1,0:T(8,128)S(1)} %get-tuple-element.103.refs_0_, f32[512,640]{1,0:T(8,128)S(1)} %get-tuple-element.104.refs_1_, ...), custom_call_target="tpu_custom_call", output_to_operand_aliasing={{0}: (27, {}), {1}: (28, {})} | custom-call | flops 1000 | bytes 1000 | tf_op jit(solution)/shard_map/finish/pallas_call | solution.py:724
  (33 shorter events, 0.7 us)
Async XLA Ops:
  2.7 3.3 %collective-permute-start.1 = (f32[1,2560]{1,0:T(1,128)S(1)}, f32[1,2560]{1,0:T(1,128)S(1)}, u32[]{:S(2)}, u32[]{:S(2)}) collective-permute-start(f32[1,2560]{1,0:T(1,128)S(1)} %get-tuple-element.85.refs_2_.refs_6_), channel_id=1, source_target_pairs={{0,1},{1,0},{2,3},{3,2},{4,5},{5,4},{6,7},{7,6},{8,9},{9,8},{10,11... | collective-permute-start | bytes 30728 | tf_op jit(solution)/shard_map/ppermute | solution.py:636
  5.9 3.4 %collective-permute-start = (f32[2,64,1280]{2,1,0:T(8,128)S(1)}, f32[2,64,1280]{2,1,0:T(8,128)S(1)}, u32[]{:S(2)}, u32[]{:S(2)}) collective-permute-start(f32[2,64,1280]{2,1,0:T(8,128)S(1)} %get-tuple-element.84.refs_6_), channel_id=1, source_target_pairs={{0,1},{1,0},{2,3},{3,2},{4,5},{5,4},{6,7},{7,6},{8,9},{9,8},{10,11... | collective-permute-start | bytes 1966088 | tf_op jit(solution)/shard_map/ppermute | solution.py:636
  8.7 4.9 %copy-start = (bf16[512,128]{1,0:T(8,128)(2,1)S(1)}, bf16[512,128]{1,0:T(8,128)(2,1)}, u32[]{:S(2)}) copy-start(bf16[512,128]{1,0:T(8,128)(2,1)} %refs_5_.7) | copy-start | bytes 393220
  8.7 4.9 %copy-start.1 = (bf16[512,128]{1,0:T(8,128)(2,1)S(1)}, bf16[512,128]{1,0:T(8,128)(2,1)}, u32[]{:S(2)}) copy-start(bf16[512,128]{1,0:T(8,128)(2,1)} %refs_6_.7) | copy-start | bytes 393220
  8.7 4.8 %copy-start.3 = (s32[512]{0:T(512)S(1)}, s32[512]{0:T(512)}, u32[]{:S(2)}) copy-start(s32[512]{0:T(512)} %param.14) | copy-start | bytes 6148
  8.7 8.2 %collective-permute-start.5 = (f32[2,64,1280]{2,1,0:T(8,128)S(1)}, f32[2,64,1280]{2,1,0:T(8,128)S(1)}, u32[]{:S(2)}, u32[]{:S(2)}) collective-permute-start(f32[2,64,1280]{2,1,0:T(8,128)S(1)} %get-tuple-element.86.refs_4_), channel_id=1, source_target_pairs={{0,1},{1,0},{2,3},{3,2},{4,5},{5,4},{6,7},{7,6},{8,9},{9,8},{10,11... | collective-permute-start | bytes 1966088 | tf_op jit(solution)/shard_map/ppermute | solution.py:636
  9.3 11.1 %collective-permute-start.3 = (f32[40,1280]{1,0:T(8,128)S(1)}, f32[40,1280]{1,0:T(8,128)S(1)}, u32[]{:S(2)}, u32[]{:S(2)}) collective-permute-start(f32[40,1280]{1,0:T(8,128)S(1)} %get-tuple-element.92), channel_id=1, source_target_pairs={{0,4},{1,5},{2,6},{3,7},{4,0},{5,1},{6,2},{7,3},{8,12},{9,13},{10,... | collective-permute-start | bytes 614408 | tf_op jit(solution)/shard_map/ppermute | solution.py:636
  12.0 11.7 %collective-permute-start.4 = (f32[40,1280]{1,0:T(8,128)S(1)}, f32[40,1280]{1,0:T(8,128)S(1)}, u32[]{:S(2)}, u32[]{:S(2)}) collective-permute-start(f32[40,1280]{1,0:T(8,128)S(1)} %get-tuple-element.93), channel_id=1, source_target_pairs={{0,6},{1,7},{2,4},{3,5},{4,2},{5,3},{6,0},{7,1},{8,14},{9,15},{10,... | collective-permute-start | bytes 614408 | tf_op jit(solution)/shard_map/ppermute | solution.py:636
  13.4 12.3 %collective-permute-start.2 = (f32[40,1280]{1,0:T(8,128)S(1)}, f32[40,1280]{1,0:T(8,128)S(1)}, u32[]{:S(2)}, u32[]{:S(2)}) collective-permute-start(f32[40,1280]{1,0:T(8,128)S(1)} %get-tuple-element.87.refs_7_), channel_id=1, source_target_pairs={{0,2},{1,3},{2,0},{3,1},{4,6},{5,7},{6,4},{7,5},{8,10},{9,11},{10,... | collective-permute-start | bytes 614408 | tf_op jit(solution)/shard_map/ppermute | solution.py:636
  17.0 18.6 %collective-permute-start.7 = (f32[32,1280]{1,0:T(8,128)S(1)}, f32[32,1280]{1,0:T(8,128)S(1)}, u32[]{:S(2)}, u32[]{:S(2)}) collective-permute-start(f32[32,1280]{1,0:T(8,128)S(1)} %get-tuple-element.99), channel_id=1, source_target_pairs={{0,4},{1,5},{2,6},{3,7},{4,0},{5,1},{6,2},{7,3},{8,12},{9,13},{10,... | collective-permute-start | bytes 491528 | tf_op jit(solution)/shard_map/ppermute | solution.py:636
  19.0 17.1 %collective-permute-start.8 = (f32[32,1280]{1,0:T(8,128)S(1)}, f32[32,1280]{1,0:T(8,128)S(1)}, u32[]{:S(2)}, u32[]{:S(2)}) collective-permute-start(f32[32,1280]{1,0:T(8,128)S(1)} %get-tuple-element.100), channel_id=1, source_target_pairs={{0,6},{1,7},{2,4},{3,5},{4,2},{5,3},{6,0},{7,1},{8,14},{9,15},{10,... | collective-permute-start | bytes 491528 | tf_op jit(solution)/shard_map/ppermute | solution.py:636
  20.4 15.6 %collective-permute-start.6 = (f32[32,1280]{1,0:T(8,128)S(1)}, f32[32,1280]{1,0:T(8,128)S(1)}, u32[]{:S(2)}, u32[]{:S(2)}) collective-permute-start(f32[32,1280]{1,0:T(8,128)S(1)} %get-tuple-element.96.refs_8_), channel_id=1, source_target_pairs={{0,2},{1,3},{2,0},{3,1},{4,6},{5,7},{6,4},{7,5},{8,10},{9,11},{10,... | collective-permute-start | bytes 491528 | tf_op jit(solution)/shard_map/ppermute | solution.py:636
  25.9 6.5 %collective-permute-start.9 = (f32[16,1280]{1,0:T(8,128)S(1)}, f32[16,1280]{1,0:T(8,128)S(1)}, u32[]{:S(2)}, u32[]{:S(2)}) collective-permute-start(f32[16,1280]{1,0:T(8,128)S(1)} %quad.2.refs_10_), channel_id=1, source_target_pairs={{0,8},{1,9},{2,10},{3,11},{4,12},{5,13},{6,14},{7,15},{8,0},{9,1},... | collective-permute-start | bytes 245768 | tf_op jit(solution)/shard_map/ppermute | solution.py:779
  32.5 11.2 %collective-permute-start.10 = (f32[2,16,1280]{2,1,0:T(8,128)S(1)}, f32[2,16,1280]{2,1,0:T(8,128)S(1)}, u32[]{:S(2)}, u32[]{:S(2)}) collective-permute-start(f32[2,16,1280]{2,1,0:T(8,128)S(1)} %get-tuple-element.123), channel_id=1, source_target_pairs={{0,6},{1,7},{2,4},{3,5},{4,2},{5,3},{6,0},{7,1},{8,14},{9,15},{10,... | collective-permute-start | bytes 491528 | tf_op jit(solution)/shard_map/ppermute | solution.py:636
  34.9 8.8 %collective-permute-start.11 = (f32[2,16,1280]{2,1,0:T(8,128)S(1)}, f32[2,16,1280]{2,1,0:T(8,128)S(1)}, u32[]{:S(2)}, u32[]{:S(2)}) collective-permute-start(f32[2,16,1280]{2,1,0:T(8,128)S(1)} %get-tuple-element.124), channel_id=1, source_target_pairs={{0,2},{1,3},{2,0},{3,1},{4,6},{5,7},{6,4},{7,5},{8,10},{9,11},{10,... | collective-permute-start | bytes 491528 | tf_op jit(solution)/shard_map/ppermute | solution.py:636
  35.6 8.1 %collective-permute-start.12 = (f32[2,16,1280]{2,1,0:T(8,128)S(1)}, f32[2,16,1280]{2,1,0:T(8,128)S(1)}, u32[]{:S(2)}, u32[]{:S(2)}) collective-permute-start(f32[2,16,1280]{2,1,0:T(8,128)S(1)} %get-tuple-element.125), channel_id=1, source_target_pairs={{0,4},{1,5},{2,6},{3,7},{4,0},{5,1},{6,2},{7,3},{8,12},{9,13},{10,... | collective-permute-start | bytes 491528 | tf_op jit(solution)/shard_map/ppermute | solution.py:636
  36.2 7.4 %collective-permute-start.13 = (f32[16,1280]{1,0:T(8,128)S(1)}, f32[16,1280]{1,0:T(8,128)S(1)}, u32[]{:S(2)}, u32[]{:S(2)}) collective-permute-start(f32[16,1280]{1,0:T(8,128)S(1)} %quad.3.refs_10_), channel_id=1, source_target_pairs={{0,8},{1,9},{2,10},{3,11},{4,12},{5,13},{6,14},{7,15},{8,0},{9,1},... | collective-permute-start | bytes 245768 | tf_op jit(solution)/shard_map/ppermute | solution.py:779
  43.9 4.0 %collective-permute-start.14 = (f32[2,64,1280]{2,1,0:T(8,128)S(1)}, f32[2,64,1280]{2,1,0:T(8,128)S(1)}, u32[]{:S(2)}, u32[]{:S(2)}) collective-permute-start(f32[2,64,1280]{2,1,0:T(8,128)S(1)} %get-tuple-element.127.refs_19_), channel_id=1, source_target_pairs={{0,1},{1,0},{2,3},{3,2},{4,5},{5,4},{6,7},{7,6},{8,9},{9,8},{10,11... | collective-permute-start | bytes 1966088 | tf_op jit(solution)/shard_map/ppermute | solution.py:636
  44.0 12.6 %collective-permute-start.15 = (f32[2,16,1280]{2,1,0:T(8,128)S(1)}, f32[2,16,1280]{2,1,0:T(8,128)S(1)}, u32[]{:S(2)}, u32[]{:S(2)}) collective-permute-start(f32[2,16,1280]{2,1,0:T(8,128)S(1)} %get-tuple-element.138), channel_id=1, source_target_pairs={{0,6},{1,7},{2,4},{3,5},{4,2},{5,3},{6,0},{7,1},{8,14},{9,15},{10,... | collective-permute-start | bytes 491528 | tf_op jit(solution)/shard_map/ppermute | solution.py:636
  45.9 10.7 %collective-permute-start.16 = (f32[2,16,1280]{2,1,0:T(8,128)S(1)}, f32[2,16,1280]{2,1,0:T(8,128)S(1)}, u32[]{:S(2)}, u32[]{:S(2)}) collective-permute-start(f32[2,16,1280]{2,1,0:T(8,128)S(1)} %get-tuple-element.139), channel_id=1, source_target_pairs={{0,2},{1,3},{2,0},{3,1},{4,6},{5,7},{6,4},{7,5},{8,10},{9,11},{10,... | collective-permute-start | bytes 491528 | tf_op jit(solution)/shard_map/ppermute | solution.py:636
  47.9 8.7 %collective-permute-start.17 = (f32[2,16,1280]{2,1,0:T(8,128)S(1)}, f32[2,16,1280]{2,1,0:T(8,128)S(1)}, u32[]{:S(2)}, u32[]{:S(2)}) collective-permute-start(f32[2,16,1280]{2,1,0:T(8,128)S(1)} %get-tuple-element.140), channel_id=1, source_target_pairs={{0,4},{1,5},{2,6},{3,7},{4,0},{5,1},{6,2},{7,3},{8,12},{9,13},{10,... | collective-permute-start | bytes 491528 | tf_op jit(solution)/shard_map/ppermute | solution.py:636
  56.5 2.6 %copy-start.2 = (f32[512,40]{0,1:T(8,128)S(1)}, f32[512,40]{0,1:T(8,128)}, u32[]{:S(2)}) copy-start(f32[512,40]{0,1:T(8,128)} %param.9) | copy-start | bytes 245764
  56.5 2.6 %copy-start.4 = (f32[40]{0:T(128)S(1)}, f32[40]{0:T(128)}, u32[]{:S(2)}) copy-start(f32[40]{0:T(128)} %param.12) | copy-start | bytes 484
  57.0 2.2 %collective-permute-start.18 = (f32[2,64,1280]{2,1,0:T(8,128)S(1)}, f32[2,64,1280]{2,1,0:T(8,128)S(1)}, u32[]{:S(2)}, u32[]{:S(2)}) collective-permute-start(f32[2,64,1280]{2,1,0:T(8,128)S(1)} %get-tuple-element.141.refs_29_), channel_id=1, source_target_pairs={{0,1},{1,0},{2,3},{3,2},{4,5},{5,4},{6,7},{7,6},{8,9},{9,8},{10,11... | collective-permute-start | bytes 1966088 | tf_op jit(solution)/shard_map/ppermute | solution.py:636

commit v6 on v5

--- a/solution.py
+++ b/solution.py
@@ -197,7 +197,7 @@
         put_other(1, own_decay * leaving + own(1))
 
 
-def join_kernel(columns, kept_ref, came_ref, own_ref, other_ref, *results):
+def join_kernel(columns, spans, kept_ref, came_ref, own_ref, other_ref, *results):
     firsts, _ = place()
     forward, backward = joined(
         firsts[0], own_ref[:, columns], other_ref[:, columns], kept_ref, came_ref
@@ -208,18 +208,19 @@
         ref[:quarter] = forward[here]
         ref[quarter : 2 * quarter] = backward[here]
         if ref.shape[0] > 2 * quarter:
-            width = ref.shape[1]
-            for chunk in range(own_ref.shape[1] // width):
-                there = slice(chunk * width, (chunk + 1) * width)
+            for chunk, there in enumerate(spans):
                 row = 2 * quarter + chunk
-                ref[row : row + 1, :] = own_ref[:, there] * other_ref[:, there]
+                ref[row : row + 1, : there.stop - there.start] = (
+                    own_ref[:, there] * other_ref[:, there]
+                )
 
 
 def four_chips(firsts, row, values, decays):
     half = decays[0].shape[0] - 8
     quarter = half // 2
+    width = values[0].shape[1]
     return (
-        in_order(firsts, *(ref[half + row : half + row + 1, :] for ref in decays)),
+        in_order(firsts, *(ref[half + row : half + row + 1, :width] for ref in decays)),
         in_order(firsts, *(ref[:quarter] for ref in values)),
         in_order(firsts, *(ref[quarter:half] for ref in values)),
     )
@@ -532,8 +533,8 @@
     if climbs:
         middle = [("quad", 1), *climbs, ("top", 0)]
     return [
-        ("join", 0), ("parts", 0), ("join", 1), ("quad", 0), ("parts", 1), *middle, ("parts", 2),
-        ("top", 1), ("device", 0), ("end", 0), ("parts", 3), ("device", 1), ("end", 1),
+        ("join", 0), ("parts", 0), ("join", 1), ("parts", 1), ("quad", 0), ("parts", 2), *middle,
+        ("parts", 3), ("top", 1), ("device", 0), ("end", 0), ("device", 1), ("end", 1),
     ]
 
 
@@ -746,7 +747,7 @@
         kept, came = held["kept", k]
         part = shape((2 * eighth + (8 if k == 0 else 0), widths[k]))
         corner, side, depth, stay = small(
-            functools.partial(join_kernel, span[k]), (part,) * 4, "join",
+            functools.partial(join_kernel, span[k], span), (part,) * 4, "join",
             kept, came, decay, decay_other,
         )
         held["last"] = (side,)
@@ -760,8 +761,10 @@
         held["last"] = (pay,)
         held["level", k] = (pay, both[0] if both else None, None, 0)
         if k == 0 and levels > 1:
-            rows_of = [value[2 * eighth : 2 * eighth + chunks] for value in held["four", 0]]
-            group = functools.reduce(jnp.multiply, rows_of).reshape(1, channels)
+            product = functools.reduce(jnp.multiply, held["four", 0])[2 * eighth :]
+            group = jnp.concatenate(
+                [product[i : i + 1, : widths[i]] for i in every], axis=1
+            )
             held["unit"] = group
             others = held["others"] = []
             for level in range(levels - 1):

time: 64.2 us -> 61.9 us (0.964)
  waiting for transfers between devices: 8.77 us -> 6.43 us
    ppermute x17, waiting for transfers between devices: 7.3 us -> 6.02 us  [swap(): return lax.ppermute(value, 'seq', [(i, i ^ bit) for i in range(size)])]
    ppermute x2, waiting for transfers between devices: 1.47 us -> 0.41 us  [taken(): return [lax.ppermute(pay, 'seq', perm) for perm in level_perms(level)]]
  transfers between devices with their start and end apart: 19 -> 19, of which waited for: 4 -> 5; matrix products, arithmetic and copies ran while one was open for 0% -> 0% of each run, Pallas kernels for 40% -> 42%
where the time goes in v6:
time: 61.9 us; the launch traced here: 61.6 us
  Pallas kernels  33.2 us (54%)
  starting transfers between devices  20.9 us (34%)
  waiting for transfers between devices  6.43 us (10%)
  between operations  1.03 us (2%)
    ppermute x17, starting transfers between devices, swap(): return lax.ppermute(value, 'seq', [(i, i ^ bit) for i in range(size)])  16.6 us
    pallas_call x4, Pallas kernels, block_parts(): pl.pallas_call(after(kernel, len(operands), len(last)), out_shape=tuple(o...  15.5 us
    pallas_call x2, Pallas kernels, finish(): pl.pallas_call(after(kernel, len(operands), len(last)), out_shape=(shape(...  9.11 us
    ppermute x17, waiting for transfers between devices, swap(): return lax.ppermute(value, 'seq', [(i, i ^ bit) for i in range(size)])  6.02 us
    pallas_call x2, Pallas kernels, device_states(): pl.pallas_call(after(kernel, 5, len(last)), out_shape=(pair_shape(chunk,...  5.31 us
    ppermute x2, starting transfers between devices, taken(): return [lax.ppermute(pay, 'seq', perm) for perm in level_perms(level)]  4.29 us
    pallas_call x1, Pallas kernels, local(): pl.pallas_call(functools.partial(prep_kernel, head_size), out_shape=(shap...  2.08 us
  transfers between devices with their start and end apart: 19, of which 5 were waited for; matrix products, arithmetic and copies ran while one was open for 0% of the time, Pallas kernels for 42%

profile of v6, /device:TPU:0, one launch (start us, length us, event | category | flops | bytes accessed | tf_op | source)
XLA Modules:
  0.0 61.6 jit_solution(76875316093585317)
XLA Ops:
  0.6 2.1 %prep.1 = (bf16[512,162]{1,0:T(8,128)(2,1)S(1)}, bf16[512,256]{1,0:T(8,128)(2,1)S(1)}, bf16[256,512]{1,0:T(8,128)(2,1)S(1)}, f32[8,2560]{1,0:T(8,128)S(1)}, f32[1,2560]{1,0:T(1,128)S(1)}) custom-call(f32[40,512]{1,0:T(8,128)} %bitcast.5, f32[1,40]{1,0:T(1,128)} %bitcast.12, f32[1,40]{1,0:T(1,128)} %bitcast.14, s32[1,512]{1,0:T(1,128)} %bitcast.7, ...), custom_call_target="tpu_custom_call" | custom-call | tf_op jit(solution)/shard_map/prep/pallas_call | solution.py:587
  2.7 0.5 collective-permute-start.1
  3.2 2.6 %states.2 = (f32[2,64,1280]{2,1,0:T(8,128)S(1)}, f32[2,64,1280]{2,1,0:T(8,128)S(1)}) custom-call(bf16[512,2560]{1,0:T(8,128)(2,1)} %refs_0_.11, bf16[512,2560]{1,0:T(8,128)(2,1)} %refs_1_.11, bf16[512,162]{1,0:T(8,128)(2,1)S(1)} %get-tuple-element.80.refs_2_.refs_17_, bf16[256,512]{1,0:T(8,128)(2,1)S(1)} %get-tuple-element.82.refs_3_, ...), custom_call_target="tpu_custom_call" | custom-call | flops 4000000000 | bytes 1000 | tf_op jit(solution)/shard_map/states/pallas_call | solution.py:626
  6.0 2.7 %states.3 = (f32[2,64,1280]{2,1,0:T(8,128)S(1)}, f32[2,64,1280]{2,1,0:T(8,128)S(1)}) custom-call(bf16[512,2560]{1,0:T(8,128)(2,1)} %refs_0_.11, bf16[512,2560]{1,0:T(8,128)(2,1)} %refs_1_.11, bf16[512,162]{1,0:T(8,128)(2,1)S(1)} %get-tuple-element.80.refs_2_.refs_17_, bf16[256,512]{1,0:T(8,128)(2,1)S(1)} %get-tuple-element.82.refs_3_, ...), custom_call_target="tpu_custom_call" | custom-call | flops 4000000000 | bytes 1000 | tf_op jit(solution)/shard_map/states/pallas_call | solution.py:626
  8.7 0.5 collective-permute-start.2
  9.3 2.7 %collective-permute-start.4 = (f32[40,1280]{1,0:T(8,128)S(1)}, f32[40,1280]{1,0:T(8,128)S(1)}, u32[]{:S(2)}, u32[]{:S(2)}) collective-permute-start(f32[40,1280]{1,0:T(8,128)S(1)} %get-tuple-element.96), channel_id=1, source_target_pairs={{0,4},{1,5},{2,6},{3,7},{4,0},{5,1},{6,2},{7,3},{8,12},{9,13},{10,... | collective-permute-start | bytes 614408 | tf_op jit(solution)/shard_map/ppermute | solution.py:637
  12.0 1.4 %collective-permute-start.5 = (f32[40,1280]{1,0:T(8,128)S(1)}, f32[40,1280]{1,0:T(8,128)S(1)}, u32[]{:S(2)}, u32[]{:S(2)}) collective-permute-start(f32[40,1280]{1,0:T(8,128)S(1)} %get-tuple-element.97), channel_id=1, source_target_pairs={{0,6},{1,7},{2,4},{3,5},{4,2},{5,3},{6,0},{7,1},{8,14},{9,15},{10,... | collective-permute-start | bytes 614408 | tf_op jit(solution)/shard_map/ppermute | solution.py:637
  13.4 0.1 collective-permute-start.3
  13.6 3.4 %block.4 = (f32[512,640]{1,0:T(8,128)S(1)}, f32[512,640]{1,0:T(8,128)S(1)}, bf16[512,640]{1,0:T(8,128)(2,1)S(1)}, bf16[512,640]{1,0:T(8,128)(2,1)S(1)}, bf16[512...) custom-call(bf16[512,2560]{1,0:T(8,128)(2,1)} %refs_0_.11, ...), custom_call_target="tpu_custom_call" | custom-call | flops 1000 | bytes 1000 | tf_op jit(solution)/shard_map/block/pallas_call | solution.py:684
  17.1 2.0 %collective-permute-start.7 = (f32[32,1280]{1,0:T(8,128)S(1)}, f32[32,1280]{1,0:T(8,128)S(1)}, u32[]{:S(2)}, u32[]{:S(2)}) collective-permute-start(f32[32,1280]{1,0:T(8,128)S(1)} %get-tuple-element.108), channel_id=1, source_target_pairs={{0,4},{1,5},{2,6},{3,7},{4,0},{5,1},{6,2},{7,3},{8,12},{9,13},{10,... | collective-permute-start | bytes 491528 | tf_op jit(solution)/shard_map/ppermute | solution.py:637
  19.1 1.5 %collective-permute-start.6 = (f32[32,1280]{1,0:T(8,128)S(1)}, f32[32,1280]{1,0:T(8,128)S(1)}, u32[]{:S(2)}, u32[]{:S(2)}) collective-permute-start(f32[32,1280]{1,0:T(8,128)S(1)} %get-tuple-element.93.refs_10_), channel_id=1, source_target_pairs={{0,2},{1,3},{2,0},{3,1},{4,6},{5,7},{6,4},{7,5},{8,10},{9,11},{10,... | collective-permute-start | bytes 491528 | tf_op jit(solution)/shard_map/ppermute | solution.py:637
  20.6 3.9 %block.5 = (f32[512,640]{1,0:T(8,128)S(1)}, f32[512,640]{1,0:T(8,128)S(1)}, bf16[512,640]{1,0:T(8,128)(2,1)S(1)}, bf16[512,640]{1,0:T(8,128)(2,1)S(1)}, bf16[512...) custom-call(bf16[512,2560]{1,0:T(8,128)(2,1)} %refs_0_.11, ...), custom_call_target="tpu_custom_call" | custom-call | flops 1000 | bytes 1000 | tf_op jit(solution)/shard_map/block/pallas_call | solution.py:684
  24.6 1.2 %collective-permute-done.3.refs_1_.refs_5_.refs_2_.refs_6_ = f32[40,1280]{1,0:T(8,128)S(1)} collective-permute-done((f32[40,1280]{1,0:T(8,128)S(1)}, f32[40,1280]{1,0:T(8,128)S(1)}, u32[]{:S(2)}, u32[]{:S(2)}) %collective-permute-start.3) | collective-permute-done | bytes 204832 | tf_op jit(solution)/shard_map/ppermute | solution.py:637
  25.9 2.7 %collective-permute-start.9 = (f32[16,1280]{1,0:T(8,128)S(1)}, f32[16,1280]{1,0:T(8,128)S(1)}, u32[]{:S(2)}, u32[]{:S(2)}) collective-permute-start(f32[16,1280]{1,0:T(8,128)S(1)} %quad.2.refs_10_), channel_id=1, source_target_pairs={{0,8},{1,9},{2,10},{3,11},{4,12},{5,13},{6,14},{7,15},{8,0},{9,1},... | collective-permute-start | bytes 245768 | tf_op jit(solution)/shard_map/ppermute | solution.py:782
  28.5 4.1 %block.6 = (f32[512,640]{1,0:T(8,128)S(1)}, f32[512,640]{1,0:T(8,128)S(1)}, bf16[512,640]{1,0:T(8,128)(2,1)S(1)}, bf16[512,640]{1,0:T(8,128)(2,1)S(1)}, bf16[512...) custom-call(bf16[512,2560]{1,0:T(8,128)(2,1)} %refs_0_.11, ...), custom_call_target="tpu_custom_call" | custom-call | flops 1000 | bytes 1000 | tf_op jit(solution)/shard_map/block/pallas_call | solution.py:684
  32.6 0.2 top.2
  32.8 2.5 %collective-permute-start.14 = (f32[2,16,1280]{2,1,0:T(8,128)S(1)}, f32[2,16,1280]{2,1,0:T(8,128)S(1)}, u32[]{:S(2)}, u32[]{:S(2)}) collective-permute-start(f32[2,16,1280]{2,1,0:T(8,128)S(1)} %get-tuple-element.134), channel_id=1, source_target_pairs={{0,6},{1,7},{2,4},{3,5},{4,2},{5,3},{6,0},{7,1},{8,14},{9,15},{10,... | collective-permute-start | bytes 491528 | tf_op jit(solution)/shard_map/ppermute | solution.py:637
  35.3 0.6 %collective-permute-start.15 = (f32[2,16,1280]{2,1,0:T(8,128)S(1)}, f32[2,16,1280]{2,1,0:T(8,128)S(1)}, u32[]{:S(2)}, u32[]{:S(2)}) collective-permute-start(f32[2,16,1280]{2,1,0:T(8,128)S(1)} %get-tuple-element.135), channel_id=1, source_target_pairs={{0,2},{1,3},{2,0},{3,1},{4,6},{5,7},{6,4},{7,5},{8,10},{9,11},{10,... | collective-permute-start | bytes 491528 | tf_op jit(solution)/shard_map/ppermute | solution.py:637
  35.9 0.4 collective-permute-start.16
  36.5 1.6 %collective-permute-start.10 = (f32[16,1280]{1,0:T(8,128)S(1)}, f32[16,1280]{1,0:T(8,128)S(1)}, u32[]{:S(2)}, u32[]{:S(2)}) collective-permute-start(f32[16,1280]{1,0:T(8,128)S(1)} %quad.3.refs_10_), channel_id=1, source_target_pairs={{0,8},{1,9},{2,10},{3,11},{4,12},{5,13},{6,14},{7,15},{8,0},{9,1},... | collective-permute-start | bytes 245768 | tf_op jit(solution)/shard_map/ppermute | solution.py:782
  38.1 4.2 %block.7 = (f32[512,640]{1,0:T(8,128)S(1)}, f32[512,640]{1,0:T(8,128)S(1)}, bf16[512,640]{1,0:T(8,128)(2,1)S(1)}, bf16[512,640]{1,0:T(8,128)(2,1)S(1)}, bf16[512...) custom-call(bf16[512,2560]{1,0:T(8,128)(2,1)} %refs_0_.11, ...), custom_call_target="tpu_custom_call" | custom-call | flops 1000 | bytes 1000 | tf_op jit(solution)/shard_map/block/pallas_call | solution.py:684
  42.3 0.4 collective-permute-done.10.refs_0_
  42.7 0.2 top.3
  42.9 0.1 collective-permute-done.16.refs_2_
  43.0 0.1 return.2
  43.2 2.6 %collective-permute-start.11 = (f32[2,16,1280]{2,1,0:T(8,128)S(1)}, f32[2,16,1280]{2,1,0:T(8,128)S(1)}, u32[]{:S(2)}, u32[]{:S(2)}) collective-permute-start(f32[2,16,1280]{2,1,0:T(8,128)S(1)} %get-tuple-element.118), channel_id=1, source_target_pairs={{0,6},{1,7},{2,4},{3,5},{4,2},{5,3},{6,0},{7,1},{8,14},{9,15},{10,... | collective-permute-start | bytes 491528 | tf_op jit(solution)/shard_map/ppermute | solution.py:637
  45.9 1.2 %collective-permute-start.12 = (f32[2,16,1280]{2,1,0:T(8,128)S(1)}, f32[2,16,1280]{2,1,0:T(8,128)S(1)}, u32[]{:S(2)}, u32[]{:S(2)}) collective-permute-start(f32[2,16,1280]{2,1,0:T(8,128)S(1)} %get-tuple-element.119), channel_id=1, source_target_pairs={{0,2},{1,3},{2,0},{3,1},{4,6},{5,7},{6,4},{7,5},{8,10},{9,11},{10,... | collective-permute-start | bytes 491528 | tf_op jit(solution)/shard_map/ppermute | solution.py:637
  47.1 4.5 %finish.2 = (bf16[512,2560]{1,0:T(8,128)(2,1)}, bf16[512,2560]{1,0:T(8,128)(2,1)}, f32[512,128]{1,0:T(8,128)S(1)}, f32[512,128]{1,0:T(8,128)S(1)}, f32[2,512,40]{2,1,0:T(8,128)S(1)}, /*index=5*/f32[8,40]{1,0:T(8,128)S(1)}) custom-call(f32[512,640]{1,0:T(8,128)S(1)} %get-tuple-element.122.refs_0_, f32[512,640]{1,0:T(8,128)S(1)} %get-tuple-element.123.refs_1_, ...), custom_call_target="tpu_custom_call" | custom-call | flops 1000 | bytes 1000 | tf_op jit(solution)/shard_map/finish/pallas_call | solution.py:725
  51.7 2.6 %collective-permute-done.12.refs_1_ = f32[2,16,1280]{2,1,0:T(8,128)S(1)} collective-permute-done((f32[2,16,1280]{2,1,0:T(8,128)S(1)}, f32[2,16,1280]{2,1,0:T(8,128)S(1)}, u32[]{:S(2)}, u32[]{:S(2)}) %collective-permute-start.12) | collective-permute-done | bytes 163872 | tf_op jit(solution)/shard_map/ppermute | solution.py:637
  54.3 0.4 return.3
  54.7 2.1 %collective-permute-done.18.refs_14_ = f32[2,64,1280]{2,1,0:T(8,128)S(1)} collective-permute-done((f32[2,64,1280]{2,1,0:T(8,128)S(1)}, f32[2,64,1280]{2,1,0:T(8,128)S(1)}, u32[]{:S(2)}, u32[]{:S(2)}) %collective-permute-start.18) | collective-permute-done | bytes 655392 | tf_op jit(solution)/shard_map/ppermute | solution.py:637
  56.8 4.6 %finish.3 = (bf16[512,2560]{1,0:T(8,128)(2,1)}, bf16[512,2560]{1,0:T(8,128)(2,1)}, bf16[512,128]{1,0:T(8,128)(2,1)}, bf16[512,128]{1,0:T(8,128)(2,1)}, f32[40,512]{1,0:T(8,128)}) custom-call(f32[512,640]{1,0:T(8,128)S(1)} %get-tuple-element.99.refs_0_, f32[512,640]{1,0:T(8,128)S(1)} %get-tuple-element.100.refs_1_, ...), custom_call_target="tpu_custom_call", output_to_operand_aliasing={{0}: (27, {}), {1}: (28, {})} | custom-call | flops 1000 | bytes 1000 | tf_op jit(solution)/shard_map/finish/pallas_call | solution.py:725
  (33 shorter events, 0.8 us)
Async XLA Ops:
  2.7 3.3 %collective-permute-start.1 = (f32[1,2560]{1,0:T(1,128)S(1)}, f32[1,2560]{1,0:T(1,128)S(1)}, u32[]{:S(2)}, u32[]{:S(2)}) collective-permute-start(f32[1,2560]{1,0:T(1,128)S(1)} %get-tuple-element.85.refs_2_.refs_6_), channel_id=1, source_target_pairs={{0,1},{1,0},{2,3},{3,2},{4,5},{5,4},{6,7},{7,6},{8,9},{9,8},{10,11... | collective-permute-start | bytes 30728 | tf_op jit(solution)/shard_map/ppermute | solution.py:637
  5.9 3.4 %collective-permute-start = (f32[2,64,1280]{2,1,0:T(8,128)S(1)}, f32[2,64,1280]{2,1,0:T(8,128)S(1)}, u32[]{:S(2)}, u32[]{:S(2)}) collective-permute-start(f32[2,64,1280]{2,1,0:T(8,128)S(1)} %get-tuple-element.84.refs_6_), channel_id=1, source_target_pairs={{0,1},{1,0},{2,3},{3,2},{4,5},{5,4},{6,7},{7,6},{8,9},{9,8},{10,11... | collective-permute-start | bytes 1966088 | tf_op jit(solution)/shard_map/ppermute | solution.py:637
  8.7 4.9 %copy-start = (bf16[512,128]{1,0:T(8,128)(2,1)S(1)}, bf16[512,128]{1,0:T(8,128)(2,1)}, u32[]{:S(2)}) copy-start(bf16[512,128]{1,0:T(8,128)(2,1)} %refs_5_.7) | copy-start | bytes 393220
  8.7 4.9 %copy-start.1 = (bf16[512,128]{1,0:T(8,128)(2,1)S(1)}, bf16[512,128]{1,0:T(8,128)(2,1)}, u32[]{:S(2)}) copy-start(bf16[512,128]{1,0:T(8,128)(2,1)} %refs_6_.7) | copy-start | bytes 393220
  8.7 4.8 %copy-start.3 = (s32[512]{0:T(512)S(1)}, s32[512]{0:T(512)}, u32[]{:S(2)}) copy-start(s32[512]{0:T(512)} %param.14) | copy-start | bytes 6148
  8.7 8.2 %collective-permute-start.2 = (f32[2,64,1280]{2,1,0:T(8,128)S(1)}, f32[2,64,1280]{2,1,0:T(8,128)S(1)}, u32[]{:S(2)}, u32[]{:S(2)}) collective-permute-start(f32[2,64,1280]{2,1,0:T(8,128)S(1)} %get-tuple-element.86.refs_4_), channel_id=1, source_target_pairs={{0,1},{1,0},{2,3},{3,2},{4,5},{5,4},{6,7},{7,6},{8,9},{9,8},{10,11... | collective-permute-start | bytes 1966088 | tf_op jit(solution)/shard_map/ppermute | solution.py:637
  9.3 15.1 %collective-permute-start.4 = (f32[40,1280]{1,0:T(8,128)S(1)}, f32[40,1280]{1,0:T(8,128)S(1)}, u32[]{:S(2)}, u32[]{:S(2)}) collective-permute-start(f32[40,1280]{1,0:T(8,128)S(1)} %get-tuple-element.96), channel_id=1, source_target_pairs={{0,4},{1,5},{2,6},{3,7},{4,0},{5,1},{6,2},{7,3},{8,12},{9,13},{10,... | collective-permute-start | bytes 614408 | tf_op jit(solution)/shard_map/ppermute | solution.py:637
  12.0 12.6 %collective-permute-start.5 = (f32[40,1280]{1,0:T(8,128)S(1)}, f32[40,1280]{1,0:T(8,128)S(1)}, u32[]{:S(2)}, u32[]{:S(2)}) collective-permute-start(f32[40,1280]{1,0:T(8,128)S(1)} %get-tuple-element.97), channel_id=1, source_target_pairs={{0,6},{1,7},{2,4},{3,5},{4,2},{5,3},{6,0},{7,1},{8,14},{9,15},{10,... | collective-permute-start | bytes 614408 | tf_op jit(solution)/shard_map/ppermute | solution.py:637
  13.4 12.3 %collective-permute-start.3 = (f32[40,1280]{1,0:T(8,128)S(1)}, f32[40,1280]{1,0:T(8,128)S(1)}, u32[]{:S(2)}, u32[]{:S(2)}) collective-permute-start(f32[40,1280]{1,0:T(8,128)S(1)} %get-tuple-element.87.refs_7_), channel_id=1, source_target_pairs={{0,2},{1,3},{2,0},{3,1},{4,6},{5,7},{6,4},{7,5},{8,10},{9,11},{10,... | collective-permute-start | bytes 614408 | tf_op jit(solution)/shard_map/ppermute | solution.py:637
  17.1 18.8 %collective-permute-start.7 = (f32[32,1280]{1,0:T(8,128)S(1)}, f32[32,1280]{1,0:T(8,128)S(1)}, u32[]{:S(2)}, u32[]{:S(2)}) collective-permute-start(f32[32,1280]{1,0:T(8,128)S(1)} %get-tuple-element.108), channel_id=1, source_target_pairs={{0,4},{1,5},{2,6},{3,7},{4,0},{5,1},{6,2},{7,3},{8,12},{9,13},{10,... | collective-permute-start | bytes 491528 | tf_op jit(solution)/shard_map/ppermute | solution.py:637
  19.1 17.3 %collective-permute-start.6 = (f32[32,1280]{1,0:T(8,128)S(1)}, f32[32,1280]{1,0:T(8,128)S(1)}, u32[]{:S(2)}, u32[]{:S(2)}) collective-permute-start(f32[32,1280]{1,0:T(8,128)S(1)} %get-tuple-element.93.refs_10_), channel_id=1, source_target_pairs={{0,2},{1,3},{2,0},{3,1},{4,6},{5,7},{6,4},{7,5},{8,10},{9,11},{10,... | collective-permute-start | bytes 491528 | tf_op jit(solution)/shard_map/ppermute | solution.py:637
  24.5 11.8 %collective-permute-start.8 = (f32[32,1280]{1,0:T(8,128)S(1)}, f32[32,1280]{1,0:T(8,128)S(1)}, u32[]{:S(2)}, u32[]{:S(2)}) collective-permute-start(f32[32,1280]{1,0:T(8,128)S(1)} %get-tuple-element.109), channel_id=1, source_target_pairs={{0,6},{1,7},{2,4},{3,5},{4,2},{5,3},{6,0},{7,1},{8,14},{9,15},{10,... | collective-permute-start | bytes 491528 | tf_op jit(solution)/shard_map/ppermute | solution.py:637
  25.9 6.7 %collective-permute-start.9 = (f32[16,1280]{1,0:T(8,128)S(1)}, f32[16,1280]{1,0:T(8,128)S(1)}, u32[]{:S(2)}, u32[]{:S(2)}) collective-permute-start(f32[16,1280]{1,0:T(8,128)S(1)} %quad.2.refs_10_), channel_id=1, source_target_pairs={{0,8},{1,9},{2,10},{3,11},{4,12},{5,13},{6,14},{7,15},{8,0},{9,1},... | collective-permute-start | bytes 245768 | tf_op jit(solution)/shard_map/ppermute | solution.py:782
  32.8 10.1 %collective-permute-start.14 = (f32[2,16,1280]{2,1,0:T(8,128)S(1)}, f32[2,16,1280]{2,1,0:T(8,128)S(1)}, u32[]{:S(2)}, u32[]{:S(2)}) collective-permute-start(f32[2,16,1280]{2,1,0:T(8,128)S(1)} %get-tuple-element.134), channel_id=1, source_target_pairs={{0,6},{1,7},{2,4},{3,5},{4,2},{5,3},{6,0},{7,1},{8,14},{9,15},{10,... | collective-permute-start | bytes 491528 | tf_op jit(solution)/shard_map/ppermute | solution.py:637
  35.3 7.6 %collective-permute-start.15 = (f32[2,16,1280]{2,1,0:T(8,128)S(1)}, f32[2,16,1280]{2,1,0:T(8,128)S(1)}, u32[]{:S(2)}, u32[]{:S(2)}) collective-permute-start(f32[2,16,1280]{2,1,0:T(8,128)S(1)} %get-tuple-element.135), channel_id=1, source_target_pairs={{0,2},{1,3},{2,0},{3,1},{4,6},{5,7},{6,4},{7,5},{8,10},{9,11},{10,... | collective-permute-start | bytes 491528 | tf_op jit(solution)/shard_map/ppermute | solution.py:637
  35.9 7.1 %collective-permute-start.16 = (f32[2,16,1280]{2,1,0:T(8,128)S(1)}, f32[2,16,1280]{2,1,0:T(8,128)S(1)}, u32[]{:S(2)}, u32[]{:S(2)}) collective-permute-start(f32[2,16,1280]{2,1,0:T(8,128)S(1)} %get-tuple-element.136), channel_id=1, source_target_pairs={{0,4},{1,5},{2,6},{3,7},{4,0},{5,1},{6,2},{7,3},{8,12},{9,13},{10,... | collective-permute-start | bytes 491528 | tf_op jit(solution)/shard_map/ppermute | solution.py:637
  36.5 6.2 %collective-permute-start.10 = (f32[16,1280]{1,0:T(8,128)S(1)}, f32[16,1280]{1,0:T(8,128)S(1)}, u32[]{:S(2)}, u32[]{:S(2)}) collective-permute-start(f32[16,1280]{1,0:T(8,128)S(1)} %quad.3.refs_10_), channel_id=1, source_target_pairs={{0,8},{1,9},{2,10},{3,11},{4,12},{5,13},{6,14},{7,15},{8,0},{9,1},... | collective-permute-start | bytes 245768 | tf_op jit(solution)/shard_map/ppermute | solution.py:782
  43.2 4.0 %collective-permute-start.17 = (f32[2,64,1280]{2,1,0:T(8,128)S(1)}, f32[2,64,1280]{2,1,0:T(8,128)S(1)}, u32[]{:S(2)}, u32[]{:S(2)}) collective-permute-start(f32[2,64,1280]{2,1,0:T(8,128)S(1)} %get-tuple-element.137.refs_19_), channel_id=1, source_target_pairs={{0,1},{1,0},{2,3},{3,2},{4,5},{5,4},{6,7},{7,6},{8,9},{9,8},{10,11... | collective-permute-start | bytes 1966088 | tf_op jit(solution)/shard_map/ppermute | solution.py:637
  43.2 8.4 %collective-permute-start.11 = (f32[2,16,1280]{2,1,0:T(8,128)S(1)}, f32[2,16,1280]{2,1,0:T(8,128)S(1)}, u32[]{:S(2)}, u32[]{:S(2)}) collective-permute-start(f32[2,16,1280]{2,1,0:T(8,128)S(1)} %get-tuple-element.118), channel_id=1, source_target_pairs={{0,6},{1,7},{2,4},{3,5},{4,2},{5,3},{6,0},{7,1},{8,14},{9,15},{10,... | collective-permute-start | bytes 491528 | tf_op jit(solution)/shard_map/ppermute | solution.py:637
  45.9 8.4 %collective-permute-start.12 = (f32[2,16,1280]{2,1,0:T(8,128)S(1)}, f32[2,16,1280]{2,1,0:T(8,128)S(1)}, u32[]{:S(2)}, u32[]{:S(2)}) collective-permute-start(f32[2,16,1280]{2,1,0:T(8,128)S(1)} %get-tuple-element.119), channel_id=1, source_target_pairs={{0,2},{1,3},{2,0},{3,1},{4,6},{5,7},{6,4},{7,5},{8,10},{9,11},{10,... | collective-permute-start | bytes 491528 | tf_op jit(solution)/shard_map/ppermute | solution.py:637
  47.1 7.2 %collective-permute-start.13 = (f32[2,16,1280]{2,1,0:T(8,128)S(1)}, f32[2,16,1280]{2,1,0:T(8,128)S(1)}, u32[]{:S(2)}, u32[]{:S(2)}) collective-permute-start(f32[2,16,1280]{2,1,0:T(8,128)S(1)} %get-tuple-element.120), channel_id=1, source_target_pairs={{0,4},{1,5},{2,6},{3,7},{4,0},{5,1},{6,2},{7,3},{8,12},{9,13},{10,... | collective-permute-start | bytes 491528 | tf_op jit(solution)/shard_map/ppermute | solution.py:637
  51.6 5.2 %copy-start.2 = (f32[512,40]{0,1:T(8,128)S(1)}, f32[512,40]{0,1:T(8,128)}, u32[]{:S(2)}) copy-start(f32[512,40]{0,1:T(8,128)} %param.9) | copy-start | bytes 245764
  51.6 5.2 %copy-start.4 = (f32[40]{0:T(128)S(1)}, f32[40]{0:T(128)}, u32[]{:S(2)}) copy-start(f32[40]{0:T(128)} %param.12) | copy-start | bytes 484
  54.6 2.2 %collective-permute-start.18 = (f32[2,64,1280]{2,1,0:T(8,128)S(1)}, f32[2,64,1280]{2,1,0:T(8,128)S(1)}, u32[]{:S(2)}, u32[]{:S(2)}) collective-permute-start(f32[2,64,1280]{2,1,0:T(8,128)S(1)} %get-tuple-element.141.refs_29_), channel_id=1, source_target_pairs={{0,1},{1,0},{2,3},{3,2},{4,5},{5,4},{6,7},{7,6},{8,9},{9,8},{10,11... | collective-permute-start | bytes 1966088 | tf_op jit(solution)/shard_map/ppermute | solution.py:637
